TPU v7x, 32 devices: a whole 2x2x4 slice. The times are simulated.
32 devices in a mesh: seq: 4 (over x, core), dp: 8 (over z, y).
Axes of the slice: x: 2, y: 2, z: 4, core: 2. Of those that a mesh axis runs over, the one named last changes fastest.
Arguments:
- queries: bfloat16 [8, 512, 4096], P('dp', 'seq'), may hold values from -6 to 6
- keys: bfloat16 [8, 512, 512], P('dp', 'seq'), may hold values from -6 to 6
- values: bfloat16 [8, 512, 512], P('dp', 'seq'), may hold values from -6 to 6
- grad_out: bfloat16 [8, 512, 4096], P('dp', 'seq'), may hold values from -6 to 6
- features: bfloat16 [8, 512, 4096], P('dp', 'seq'), may hold values from -100 to 100
- doc_lengths: int32 [8, 8], P('dp'), may hold values from 1 to 128, 512 in all within a row
Outputs:
- key_grad: bfloat16 [8, 512, 512], P('dp', 'seq')
- clipped_grad: float32 [4096, 512], P(('seq', 'dp'))
Inputs may be any that keep to these rules, and one draw needn't show every extreme that they name: `doc_lengths`: each row sums to 512; the longest document of every data group has exactly 128 tokens.
All inputs are finite; a program needn't handle non-finite values.
Results may differ from a plain program's by a relative error of at most 0.0058.
Values may be sent and summed in bfloat16 or wider, within the bound.
No kernel may reach another device: no remote copies, remote signals or barrier semaphores. Data moves between devices by JAX's collectives and lax.ppermute only.
A program may use at most 64 MiB of HBM per device.

v0:
```python
import math

import jax
import jax.numpy as jnp
from jax import lax
from jax.sharding import PartitionSpec as P

HD = 128
HQ = 32
KVH = 4
DW = 4096
DOC_MAX = 128
QBLK = 512


NEG_FILL = -1e30


def doc_index(lengths, positions):
    doc_ends = jnp.cumsum(lengths, dtype=jnp.int32)
    located = jnp.sum((doc_ends[None, :] <= positions[:, None]).astype(jnp.int32), axis=1)
    return jnp.where(positions < 0, -1, located)


def shards(queries, keys, values, grad_out, features, doc_lengths):
    seq_count = lax.axis_size("seq")
    tok_rows = queries.shape[1]
    slab_len = tok_rows * seq_count
    local_heads = HQ // seq_count
    sharers = seq_count // KVH
    block_rows = DW // seq_count
    score_scale = 1.0 / math.sqrt(HD)
    block_width = QBLK + DOC_MAX
    query_send = queries[0].reshape(tok_rows, seq_count, local_heads * HD)
    grad_send = grad_out[0].reshape(tok_rows, seq_count, local_heads * HD)
    query_heads, grad_heads = (
        lax.all_to_all(query_send, "seq", split_axis=1, concat_axis=0, tiled=True),
        lax.all_to_all(grad_send, "seq", split_axis=1, concat_axis=0, tiled=True),
    )
    query_heads = query_heads.reshape(slab_len, local_heads, HD)
    grad_heads = grad_heads.reshape(slab_len, local_heads, HD)
    key_three = keys[0].reshape(tok_rows, KVH, HD)
    value_three = values[0].reshape(tok_rows, KVH, HD)
    pair_send = jnp.repeat(jnp.concatenate([key_three, value_three], axis=2), sharers, axis=1)
    feature_send = features[0].reshape(tok_rows, seq_count, block_rows)
    pair_heads, feature_cols = (
        lax.all_to_all(pair_send, "seq", split_axis=1, concat_axis=0, tiled=True),
        lax.all_to_all(feature_send, "seq", split_axis=1, concat_axis=0, tiled=True),
    )
    feature_block = feature_cols.reshape(slab_len, block_rows)
    pair_heads = pair_heads.reshape(slab_len, 2 * HD)
    key_pad = jnp.concatenate([jnp.zeros((DOC_MAX, 2 * HD), jnp.bfloat16), pair_heads], axis=0)
    lengths = doc_lengths[0]

    def one_block(block_index, key_total):
        row_start = (block_index * QBLK).astype(jnp.int32)
        query_rows = lax.dynamic_slice_in_dim(query_heads, row_start, QBLK, 0)
        grad_rows = lax.dynamic_slice_in_dim(grad_heads, row_start, QBLK, 0)
        window = lax.dynamic_slice_in_dim(key_pad, row_start, block_width, 0)
        key_window = window[:, :HD]
        value_window = window[:, HD:]
        query_pos = row_start + jnp.arange(QBLK, dtype=jnp.int32)
        key_pos = row_start - DOC_MAX + jnp.arange(block_width, dtype=jnp.int32)
        query_doc = doc_index(lengths, query_pos)
        key_doc = doc_index(lengths, key_pos)
        visible = (query_doc[:, None] == key_doc[None, :]) & (
            key_pos[None, :] <= query_pos[:, None]
        )
        scores = (
            jnp.einsum("qhd,kd->hqk", query_rows, key_window, preferred_element_type=jnp.float32)
            * score_scale
        )
        scores = jnp.where(visible[None], scores, NEG_FILL)
        row_peak = jnp.max(scores, axis=2, keepdims=True)
        exponent = jnp.exp(scores - row_peak)
        attention = exponent / jnp.sum(exponent, axis=2, keepdims=True)
        grad_weights = jnp.einsum(
            "qhd,kd->hqk", grad_rows, value_window, preferred_element_type=jnp.float32
        )
        row_delta = jnp.sum(attention * grad_weights, axis=2, keepdims=True)
        grad_scores = (attention * (grad_weights - row_delta) * score_scale).astype(jnp.bfloat16)
        contribution = jnp.einsum(
            "hqk,qhd->kd", grad_scores, query_rows, preferred_element_type=jnp.float32
        )
        current = lax.dynamic_slice_in_dim(key_total, row_start, block_width, 0)
        return lax.dynamic_update_slice_in_dim(key_total, current + contribution, row_start, 0)

    key_total = lax.fori_loop(
        0, slab_len // QBLK, one_block, jnp.zeros((DOC_MAX + slab_len, HD), jnp.float32)
    )
    key_part = key_total[DOC_MAX:].astype(jnp.bfloat16)
    key_back = lax.all_to_all(key_part, "seq", split_axis=0, concat_axis=1, tiled=True)
    key_sum = jnp.sum(key_back.reshape(tok_rows, KVH, sharers, HD).astype(jnp.float32), axis=2)
    key_grad = key_sum.reshape(tok_rows, KVH * HD).astype(jnp.bfloat16)
    weight_part = lax.dot_general(
        feature_block,
        lax.all_gather(key_grad, "seq", axis=0, tiled=True),
        (((0,), (0,)), ((), ())),
        preferred_element_type=jnp.float32,
    )
    entry_count = DW * KVH * HD
    own_rows = lax.psum_scatter(weight_part, "dp", scatter_dimension=0, tiled=True)
    squares = lax.psum(jnp.sum(own_rows * own_rows), ("seq", "dp"))
    root_mean = jnp.sqrt(squares / entry_count + 1e-06)
    clipped_grad = own_rows * jnp.minimum(1.0, 1.0 / root_mean)
    return (key_grad[None], clipped_grad)


def solution(mesh):
    in_specs = (
        P("dp", "seq", None),
        P("dp", "seq", None),
        P("dp", "seq", None),
        P("dp", "seq", None),
        P("dp", "seq", None),
        P("dp", None),
    )
    out_specs = (P("dp", "seq", None), P(("seq", "dp"), None))
    return jax.shard_map(shards, mesh=mesh, in_specs=in_specs, out_specs=out_specs, check_vma=False)
```

profile of v0, /device:TPU:0, one launch (start us, length us, event | category | flops | bytes accessed | tf_op | source)
XLA Modules:
  0.0 228.8 jit_solution(11860006835194357804)
XLA Ops:
  7.2 0.0 copy-start
  7.2 0.0 copy-start.1
  7.2 1.0 reshape_squeeze.15
  8.2 0.9 reshape_squeeze.16
  9.2 0.7 pad_maximum_fusion
  9.9 4.2 %all-to-all-start = ((bf16[128,4,256]{2,0,1:T(8,128)(2,1)}), bf16[128,4,256]{2,0,1:T(8,128)(2,1)S(1)}, u32[]{:S(2)}, u32[]{:S(2)}) async-start(bf16[128,4,256]{2,0,1:T(8,128)(2,1)} %pad_maximum_fusion), calls=%async_computation | async-start | bytes 524288 | tf_op jit(solution)/shard_map/all_to_all | solution.py:47
  14.2 1.8 reshape_squeeze.17
  16.0 1.3 copy.36
  17.4 2.8 %all-to-all-done = bf16[128,4,256]{2,0,1:T(8,128)(2,1)S(1)} async-done(((bf16[128,4,256]{2,0,1:T(8,128)(2,1)}), bf16[128,4,256]{2,0,1:T(8,128)(2,1)S(1)}, u32[]{:S(2)}, u32[]{:S(2)}) %all-to-all-start) | async-done | bytes 262176 | tf_op jit(solution)/shard_map/all_to_all | solution.py:47
  20.2 3.5 %all-to-all-start.1 = ((bf16[128,4,1024]{2,0,1:T(8,128)(2,1)}), bf16[128,4,1024]{2,0,1:T(8,128)(2,1)S(1)}, u32[]{:S(2)}, u32[]{:S(2)}) async-start(bf16[128,4,1024]{2,0,1:T(8,128)(2,1)} %copy.36), calls=%async_computation.1 | async-start | bytes 2097152 | tf_op jit(solution)/shard_map/all_to_all | solution.py:37
  23.7 1.9 reshape_squeeze.18
  25.6 1.3 copy.38
  26.9 0.0 copy-done
  26.9 1.3 copy.42
  28.2 0.0 copy-done.1
  28.2 0.2 reduce-window.8
  28.4 9.8 %all-to-all-done.1 = bf16[128,4,1024]{2,0,1:T(8,128)(2,1)S(1)} async-done(((bf16[128,4,1024]{2,0,1:T(8,128)(2,1)}), bf16[128,4,1024]{2,0,1:T(8,128)(2,1)S(1)}, u32[]{:S(2)}, u32[]{:S(2)}) %all-to-all-start.1) | async-done | bytes 1048608 | tf_op jit(solution)/shard_map/all_to_all | solution.py:37
  38.1 3.5 %all-to-all-start.2 = ((bf16[128,4,1024]{2,0,1:T(8,128)(2,1)}), bf16[128,4,1024]{2,0,1:T(8,128)(2,1)S(1)}, u32[]{:S(2)}, u32[]{:S(2)}) async-start(bf16[128,4,1024]{2,0,1:T(8,128)(2,1)} %copy.38), calls=%async_computation.2 | async-start | bytes 2097152 | tf_op jit(solution)/shard_map/all_to_all | solution.py:38
  41.7 0.1 convert_reduce_fusion.1
  41.8 0.1 convert_reduce_fusion
  41.9 1.1 fusion.14
  42.9 0.3 copy.46
  43.2 12.9 %all-to-all-done.2 = bf16[128,4,1024]{2,0,1:T(8,128)(2,1)S(1)} async-done(((bf16[128,4,1024]{2,0,1:T(8,128)(2,1)}), bf16[128,4,1024]{2,0,1:T(8,128)(2,1)S(1)}, u32[]{:S(2)}, u32[]{:S(2)}) %all-to-all-start.2) | async-done | bytes 1048608 | tf_op jit(solution)/shard_map/all_to_all | solution.py:38
  56.1 3.5 %all-to-all-start.4 = ((bf16[128,4,1024]{0,2,1:T(8,128)(2,1)}), bf16[128,4,1024]{0,2,1:T(8,128)(2,1)S(1)}, u32[]{:S(2)}, u32[]{:S(2)}) async-start(bf16[128,4,1024]{0,2,1:T(8,128)(2,1)} %bitcast.18), calls=%async_computation.4 | async-start | bytes 2097152 | tf_op jit(solution)/shard_map/all_to_all | solution.py:48
  59.6 10.2 %fusion.12 = f32[8,512,640]{1,2,0:T(8,128)} fusion(pred[512,640]{0,1:T(8,128)(4,1)} %fusion.14, bf16[512,8,128]{2,1,0:T(8,128)(2,1)S(1)} %bitcast.93, bf16[512,256]{1,0:T(8,128)(2,1)S(1)} %bitcast.91), kind=kOutput, calls=%fused_computation.15 | convolution fusion | flops 681583872 | bytes 12124160 | tf_op jit(solution)/shard_map/while/body/eval_jaxpr/div | solution.py:76
  69.8 0.3 copy.47
  70.1 5.4 %fusion.20 = f32[640,512,8]{1,0,2:T(8,128)} fusion(bf16[512,8,128]{2,1,0:T(8,128)(2,1)S(1)} %bitcast.85, bf16[512,256]{1,0:T(8,128)(2,1)S(1)} %bitcast.92), kind=kOutput, calls=%fused_computation.22 | convolution fusion | flops 671088640 | bytes 11796480 | tf_op jit(solution)/shard_map/while/body/eval_jaxpr/qhd,kd->hqk/dot_general | solution.py:77
  75.4 14.6 %fusion.15 = bf16[640,128]{1,0:T(8,128)(2,1)S(1)} fusion(f32[8,512,640]{1,2,0:T(8,128)} %fusion.12, f32[640,512,8]{1,0,2:T(8,128)} %fusion.20, bf16[512,8,128]{2,1,0:T(8,128)(2,1)S(1)} %bitcast.94), kind=kOutput, calls=%fused_computation.20 | convolution fusion | flops 684200576 | bytes 22183936 | tf_op jit(solution)/shard_map/while/body/eval_jaxpr/hqk,qhd->kd/dot_general | solution.py:82
  90.0 0.8 copy.41
  90.8 0.0 all-to-all-done.4
  90.8 3.3 %all-to-all-start.3 = ((bf16[4,128,128]{1,2,0:T(8,128)(2,1)}), bf16[4,128,128]{1,2,0:T(8,128)(2,1)S(1)}, u32[]{:S(2)}, u32[]{:S(2)}) async-start(bf16[4,128,128]{1,2,0:T(8,128)(2,1)} %copy.41), calls=%async_computation.3 | async-start | bytes 262144 | tf_op jit(solution)/shard_map/all_to_all | solution.py:92
  94.1 0.0 reduce-scatter.2.cloned.1.call-start
  94.2 0.5 copy.43
  94.7 4.0 %all-to-all-done.3 = bf16[4,128,128]{1,2,0:T(8,128)(2,1)S(1)} async-done(((bf16[4,128,128]{1,2,0:T(8,128)(2,1)}), bf16[4,128,128]{1,2,0:T(8,128)(2,1)S(1)}, u32[]{:S(2)}, u32[]{:S(2)}) %all-to-all-start.3) | async-done | bytes 131104 | tf_op jit(solution)/shard_map/all_to_all | solution.py:92
  98.7 6.5 %all_gather.3 = bf16[512,512]{0,1:T(8,128)(2,1)S(1)} all-gather(bf16[128,512]{0,1:T(8,128)(2,1)S(1)} %bitcast.89), channel_id=1, replica_groups=mesh['seq'=4,'dp'=8] {'seq'}, dimensions={0}, use_global_device_ids=true | all-gather | bytes 655360 | tf_op jit(solution)/shard_map/all_gather | solution.py:97
  105.3 2.1 convolution_bitcast_fusion
  107.3 0.0 reduce-scatter.2.cloned.1.call-update
  107.4 69.9 %reduce-scatter.2.cloned.1.call-done = f32[128,512]{0,1:T(8,128)} async-done(((f32[1024,512]{0,1:T(8,128)}), f32[128,512]{0,1:T(8,128)}) %reduce-scatter.2.cloned.1.call-update) | async-done | bytes 262160 | tf_op jit(solution)/shard_map/reduce_scatter | solution.py:102
  177.3 1.6 multiply_reduce_fusion
  178.9 0.8 copy.44
  179.7 39.8 %psum.7 = f32[]{:T(128)} all-reduce(f32[]{:T(128)} %multiply_reduce_fusion), channel_id=1, replica_groups=mesh['seq'=4,'dp'=8] {'seq','dp'}, use_global_device_ids=true, to_apply=%region_8.9 | all-reduce | flops 1 | bytes 8 | tf_op jit(solution)/shard_map/psum | solution.py:103
  220.1 1.0 broadcast_multiply_fusion
  221.1 0.8 copy.45
  (5 shorter events, 0.1 us)
Async XLA Ops:
  7.2 19.7 %copy-start = (bf16[1,128,4096]{2,1,0:T(8,128)(2,1)S(1)}, bf16[1,128,4096]{2,1,0:T(8,128)(2,1)}, u32[]{:S(2)}) copy-start(bf16[1,128,4096]{2,1,0:T(8,128)(2,1)} %param.10) | copy-start | bytes 3145732
  7.2 21.0 %copy-start.1 = (s32[1,8]{1,0:T(1,128)S(1)}, s32[1,8]{1,0:T(1,128)}, u32[]{:S(2)}) copy-start(s32[1,8]{1,0:T(1,128)} %param.11) | copy-start | bytes 100
  9.9 10.2 %all-to-all-start = ((bf16[128,4,256]{2,0,1:T(8,128)(2,1)}), bf16[128,4,256]{2,0,1:T(8,128)(2,1)S(1)}, u32[]{:S(2)}, u32[]{:S(2)}) async-start(bf16[128,4,256]{2,0,1:T(8,128)(2,1)} %pad_maximum_fusion), calls=%async_computation | async-start | bytes 524288 | tf_op jit(solution)/shard_map/all_to_all | solution.py:47
  20.2 18.0 %all-to-all-start.1 = ((bf16[128,4,1024]{2,0,1:T(8,128)(2,1)}), bf16[128,4,1024]{2,0,1:T(8,128)(2,1)S(1)}, u32[]{:S(2)}, u32[]{:S(2)}) async-start(bf16[128,4,1024]{2,0,1:T(8,128)(2,1)} %copy.36), calls=%async_computation.1 | async-start | bytes 2097152 | tf_op jit(solution)/shard_map/all_to_all | solution.py:37
  38.1 18.0 %all-to-all-start.2 = ((bf16[128,4,1024]{2,0,1:T(8,128)(2,1)}), bf16[128,4,1024]{2,0,1:T(8,128)(2,1)S(1)}, u32[]{:S(2)}, u32[]{:S(2)}) async-start(bf16[128,4,1024]{2,0,1:T(8,128)(2,1)} %copy.38), calls=%async_computation.2 | async-start | bytes 2097152 | tf_op jit(solution)/shard_map/all_to_all | solution.py:38
  56.1 34.7 %all-to-all-start.4 = ((bf16[128,4,1024]{0,2,1:T(8,128)(2,1)}), bf16[128,4,1024]{0,2,1:T(8,128)(2,1)S(1)}, u32[]{:S(2)}, u32[]{:S(2)}) async-start(bf16[128,4,1024]{0,2,1:T(8,128)(2,1)} %bitcast.18), calls=%async_computation.4 | async-start | bytes 2097152 | tf_op jit(solution)/shard_map/all_to_all | solution.py:48
  90.8 7.9 %all-to-all-start.3 = ((bf16[4,128,128]{1,2,0:T(8,128)(2,1)}), bf16[4,128,128]{1,2,0:T(8,128)(2,1)S(1)}, u32[]{:S(2)}, u32[]{:S(2)}) async-start(bf16[4,128,128]{1,2,0:T(8,128)(2,1)} %copy.41), calls=%async_computation.3 | async-start | bytes 262144 | tf_op jit(solution)/shard_map/all_to_all | solution.py:92
  94.1 83.1 %reduce-scatter.2.cloned.1.call-start = ((), (), s32[]{:S(2)}) async-start(), calls=%async_computation.6 | async-start | bytes 2359296 | tf_op jit(solution)/shard_map/reduce_scatter | solution.py:102
Sparse Core Ops, SparseCore 0:
  107.5 69.7 reduce-scatter.1
where the time goes:
time: 230 us; the launch traced here: 229 us
  waiting for transfers between devices  99.4 us (43%)
  blocking collectives  46.3 us (20%)
  matrix products  32.2 us (14%)
  starting transfers between devices  18.1 us (8%)
  between operations  14.9 us (6%)
  local copies, waits for them, and re-layouts  13.1 us (6%)
  other arithmetic  4.76 us (2%)
    reduce_scatter x1, waiting for transfers between devices, shards(): lax.psum_scatter(weight_part, 'dp', scatter_dimension=0, tiled=True)  69.9 us
    psum x1, blocking collectives, shards(): squares = lax.psum(jnp.sum(own_rows * own_rows), ('seq', 'dp'))  39.8 us
    dot_general x1, matrix products, one_block(): jnp.einsum('hqk,qhd->kd', grad_scores, query_rows, preferred_element_type...  14.6 us
    all_to_all x1, waiting for transfers between devices, shards(): lax.all_to_all(grad_send, 'seq', split_axis=1, concat_axis=0, tiled=True)  12.9 us
    div x1, matrix products, one_block(): attention = exponent / jnp.sum(exponent, axis=2, keepdims=True)  10.2 us
    all_to_all x1, waiting for transfers between devices, shards(): lax.all_to_all(query_send, 'seq', split_axis=1, concat_axis=0, tiled=True)  9.75 us
    all_gather x1, blocking collectives, shards(): lax.all_gather(key_grad, 'seq', axis=0, tiled=True)  6.52 us
    dot_general x1, matrix products, one_block(): jnp.einsum('qhd,kd->hqk', grad_rows, value_window, preferred_element_type...  5.38 us
  transfers between devices with their start and end apart: 6, of which 5 were waited for; matrix products, arithmetic and copies ran while one was open for 18% of the time, Pallas kernels for 0%

commit v1 on v0

v1 whole, which is shorter than its diff:
```python
import functools
import math

import jax
import jax.numpy as jnp
from jax import lax
from jax.experimental import pallas as pl
from jax.experimental.pallas import tpu as pltpu
from jax.sharding import PartitionSpec as P

HD = 128
HQ = 32
KVH = 4
DW = 4096
GROUP = HQ // KVH

NEG_FILL = -1e30
AXES = ("seq", "dp")
F32 = jnp.float32
BF16 = jnp.bfloat16
CORES = 2
HALF = KVH // CORES
WIDE = HALF * HD
SMEM = pl.BlockSpec(memory_space=pltpu.SMEM)


def params():
    return pltpu.CompilerParams(vmem_limit_bytes=40 << 20)


def cost(flops, moved, exps=0):
    return pl.CostEstimate(flops=flops, bytes_accessed=moved, transcendentals=exps)


def attention_kernel(pair, place, lengths, q, g, k_prev, k_own, v_prev, v_own, out, bias):
    rows = q.shape[0]

    @pl.when(pl.program_id(0) == 0)
    def _():
        base = place[0] * rows
        query_pos = base + lax.broadcasted_iota(jnp.int32, (1, rows), 1)
        start = jnp.zeros((1, rows), jnp.int32)
        end = jnp.int32(0)
        for d in range(lengths.shape[1]):
            end = end + lengths[0, d]
            start = jnp.where(end <= query_pos, end, start)
        key_pos = base - rows + lax.broadcasted_iota(jnp.int32, (2 * rows, rows), 0)
        visible = (key_pos >= start) & (key_pos <= query_pos)
        one = jnp.where(visible, 0.0, NEG_FILL).astype(F32)
        for n in range(pair):
            bias[:, n * rows : (n + 1) * rows] = one

    key = jnp.concatenate([k_prev[...], k_own[...]], axis=0)
    value = jnp.concatenate([v_prev[...], v_own[...]], axis=0)
    scale = 1.0 / math.sqrt(HD)
    scale2 = scale * math.log2(math.e)
    nt = (((1,), (1,)), ((), ()))
    nn = (((1,), (0,)), ((), ()))
    total = None
    for h in range(0, GROUP, pair):
        heads = [slice((h + n) * HD, (h + n + 1) * HD) for n in range(pair)]
        q_rows = jnp.concatenate([q[:, head] for head in heads], axis=0)
        g_rows = jnp.concatenate([g[:, head] for head in heads], axis=0)
        scores = lax.dot_general(key, q_rows, nt, preferred_element_type=F32)
        weights = lax.dot_general(value, g_rows, nt, preferred_element_type=F32)
        scores = scores * scale2 + bias[...]
        exponent = jnp.exp2(scores - jnp.max(scores, axis=0, keepdims=True))
        inverse = 1.0 / jnp.sum(exponent, axis=0, keepdims=True)
        delta = jnp.sum(exponent * weights, axis=0, keepdims=True) * inverse
        grads = ((exponent * (inverse * scale)) * (weights - delta)).astype(BF16)
        part = lax.dot_general(grads, q_rows, nn, preferred_element_type=F32)
        total = part if total is None else total + part
    out[0] = total.astype(out.dtype)


def attention(place, lengths, q, g, k_prev, k_own, v_prev, v_own, heads, dtype):
    rows = q.shape[0]
    head = lambda i, p, l: (0, p[1] + i)
    size = heads * 2 * rows * GROUP * rows
    return pl.pallas_call(
        functools.partial(attention_kernel, 4),
        grid_spec=pltpu.PrefetchScalarGridSpec(
            num_scalar_prefetch=2,
            grid=(heads,),
            in_specs=[pl.BlockSpec((rows, GROUP * HD), head)] * 2
            + [pl.BlockSpec((rows, HD), head)] * 4,
            out_specs=pl.BlockSpec((1, 2 * rows, HD), lambda i, p, l: (i, 0, 0)),
            scratch_shapes=[pltpu.VMEM((2 * rows, 4 * rows), F32)],
        ),
        out_shape=jax.ShapeDtypeStruct((heads, 2 * rows, HD), dtype),
        compiler_params=params(),
        cost_estimate=cost(6 * size * HD, heads * rows * GROUP * HD * 4, size),
    )(place, lengths, q, g, k_prev, k_own, v_prev, v_own)


def pack_kernel(sizes, x_ref, out):
    nx, ny, nz = sizes
    block = DW // (nx * CORES * ny * nz)
    for x in range(nx):
        for y in range(ny):
            for z in range(nz):
                for c in range(CORES):
                    source = ((x * CORES + c) * nz + z) * ny + y
                    out[x * ny + y, z, :, c * block : (c + 1) * block] = x_ref[
                        :, source * block : (source + 1) * block
                    ]


def pack(features, sizes):
    nx, ny, nz = sizes
    rows = features.shape[0]
    shape = (nx * ny, nz, rows, DW // (nx * ny * nz))
    return pl.pallas_call(
        functools.partial(pack_kernel, sizes),
        out_shape=jax.ShapeDtypeStruct(shape, BF16),
        compiler_params=params(),
        cost_estimate=cost(0, 2 * rows * DW * 2),
    )(features)


def merge_kernel(place, mine, theirs, out):
    rows = mine.shape[1] // 2

    def write(even, odd):
        for h in range(HALF):
            cols = slice(h * HD, (h + 1) * HD)
            out[:rows, cols] = even[h, :rows]
            out[rows : 2 * rows, cols] = (
                even[h, rows:].astype(F32) + odd[h, :rows].astype(F32)
            ).astype(BF16)
            out[2 * rows :, cols] = odd[h, rows:]

    @pl.when(place[0] == 0)
    def _():
        write(mine, theirs)

    @pl.when(place[0] == 1)
    def _():
        write(theirs, mine)


def merge(place, mine, theirs):
    rows = mine.shape[1] // 2
    vmem = pl.BlockSpec(memory_space=pltpu.VMEM)
    return pl.pallas_call(
        merge_kernel,
        in_specs=[SMEM, vmem, vmem],
        out_specs=vmem,
        out_shape=jax.ShapeDtypeStruct((3 * rows, WIDE), BF16),
        compiler_params=params(),
        cost_estimate=cost(rows * WIDE, 7 * rows * WIDE * 2),
    )(place, mine, theirs)


def weight_kernel(nz, place, g0, g1, g2, g3, f_same, f_other, *rest):
    sends, (keep, key_mine, key_theirs, same, other) = rest[: nz - 1], rest[nz - 1 :]
    rows = g0.shape[0] // 3
    core, chip, z = place[0], place[1], place[2]
    chips = (g0, g1, g2, g3)
    for m in range(4):
        even = chips[m][rows : 2 * rows]
        odd = (chips[m][2 * rows :].astype(F32) + chips[m ^ 2][:rows].astype(F32)).astype(BF16)
        at = pl.ds(pl.multiple_of((chip ^ m) * rows, rows), rows)
        own = jnp.where(core == 0, even, odd)
        far = jnp.where(core == 0, odd, even)
        same[at] = own
        other[at] = far
        if m == 0:
            key_mine[...] = own
            key_theirs[...] = far
    tn = (((0,), (0,)), ((), ()))
    for m in (2, 3, 1, 0):
        block = z ^ m
        left = f_same[:, pl.ds(block, 1)].reshape(4 * rows, WIDE)
        right = f_other[:, pl.ds(block, 1)].reshape(4 * rows, WIDE)
        product = lax.dot_general(same[...], left, tn, preferred_element_type=F32)
        product += lax.dot_general(other[...], right, tn, preferred_element_type=F32)
        if m == 0:
            keep[...] = product
        else:
            sends[m - 1][...] = product.astype(BF16)


def weight(place, chips, f_same, f_other):
    rows = chips[0].shape[0] // 3
    nz = f_same.shape[1]
    vmem = pl.BlockSpec(memory_space=pltpu.VMEM)
    square = (WIDE, f_same.shape[3])
    shapes = [jax.ShapeDtypeStruct(square, BF16)] * (nz - 1)
    shapes += [jax.ShapeDtypeStruct(square, F32)] + [jax.ShapeDtypeStruct((rows, WIDE), BF16)] * 2
    return pl.pallas_call(
        functools.partial(weight_kernel, nz),
        in_specs=[SMEM] + [vmem] * 6,
        out_specs=[vmem] * len(shapes),
        out_shape=shapes,
        scratch_shapes=[pltpu.VMEM((4 * rows, WIDE), BF16)] * 2,
        compiler_params=params(),
        cost_estimate=cost(2 * 8 * rows * WIDE * 4 * WIDE, 4 << 20),
    )(place, *chips, f_same, f_other)


def reduce_kernel(place, keep, r1, r2, r3, mine, theirs, squares):
    total = keep[...] + r1[...].astype(F32) + r2[...].astype(F32) + r3[...].astype(F32)
    half = total.shape[1] // 2
    low, high = total[:, :half], total[:, half:]
    mine[...] = jnp.where(place[0] == 0, low, high)
    theirs[...] = jnp.where(place[0] == 0, high, low)
    sums = jnp.sum(low * low + high * high, axis=0, keepdims=True)
    squares[...] = jnp.broadcast_to(sums[None], squares.shape)


def reduce_planes(place, keep, received, devices):
    cols, both = keep.shape
    vmem = pl.BlockSpec(memory_space=pltpu.VMEM)
    half = jax.ShapeDtypeStruct((cols, both // 2), F32)
    return pl.pallas_call(
        reduce_kernel,
        in_specs=[SMEM] + [vmem] * 4,
        out_specs=[vmem] * 3,
        out_shape=[half, half, jax.ShapeDtypeStruct((devices, 1, both // 2), F32)],
        compiler_params=params(),
        cost_estimate=cost(8 * cols * both, cols * both * 14),
    )(place, keep, *received)


def finish_kernel(place, squares, mine, theirs, key_mine, key_theirs, key_out, out):
    entries = DW * KVH * HD
    total = jnp.sum(jnp.sum(squares[...], axis=0, keepdims=True), axis=2, keepdims=True)
    root_mean = jnp.sqrt(total / entries + 1e-06)
    factor = jnp.minimum(1.0, 1.0 / root_mean)[0]
    first = place[0] == 0
    low = (mine[...] * factor).T
    high = (theirs[...] * factor).T
    out[:, :WIDE] = jnp.where(first, low, high)
    out[:, WIDE:] = jnp.where(first, high, low)
    key_out[0, :, :WIDE] = jnp.where(first, key_mine[...], key_theirs[...])
    key_out[0, :, WIDE:] = jnp.where(first, key_theirs[...], key_mine[...])


def finish(place, squares, mine, theirs, key_mine, key_theirs):
    rows = key_mine.shape[0]
    vmem = pl.BlockSpec(memory_space=pltpu.VMEM)
    return pl.pallas_call(
        finish_kernel,
        in_specs=[SMEM] + [vmem] * 5,
        out_specs=[vmem] * 2,
        out_shape=[
            jax.ShapeDtypeStruct((1, rows, KVH * HD), BF16),
            jax.ShapeDtypeStruct((mine.shape[1], KVH * HD), F32),
        ],
        compiler_params=params(),
        cost_estimate=cost(4 * rows * KVH * HD, 4 * rows * KVH * HD * 4),
    )(place, squares, mine, theirs, key_mine, key_theirs)


def planes(queries, keys, values, grad_out, features, doc_lengths):
    seq_count, dp_count = lax.axis_size("seq"), lax.axis_size("dp")
    devices = seq_count * dp_count
    nx, ny = seq_count // CORES, 2
    nz = dp_count // ny
    seq, dp = lax.axis_index("seq"), lax.axis_index("dp")
    core, x, y, z = seq % CORES, seq // CORES, dp % ny, dp // ny
    as_place = lambda *items: jnp.stack([jnp.asarray(i, jnp.int32) for i in items])

    def swap(array, mask):
        return lax.ppermute(array, AXES, [(i, i ^ mask) for i in range(devices)])

    core_mask, x_mask, y_mask, z_mask = dp_count, CORES * dp_count, 1, ny
    following = [(i, (i + 1) % seq_count) for i in range(seq_count)]
    k_own, v_own = keys[0], values[0]
    k_prev = lax.ppermute(k_own, "seq", following)
    v_prev = lax.ppermute(v_own, "seq", following)

    packed = pack(features[0], (nx, ny, nz))
    members = [
        [
            ((a * CORES + c) * nz + b) * ny + e
            for a in range(nx)
            for e in range(ny)
        ]
        for c in range(CORES)
        for b in range(nz)
    ]
    f_same = lax.all_to_all(packed, AXES, 0, 0, axis_index_groups=members, tiled=True)
    f_other = swap(f_same, core_mask)

    near = (queries[0], grad_out[0], k_prev, k_own, v_prev, v_own)
    to_send = attention(as_place(seq, (1 - core) * HALF), doc_lengths, *near, HALF, BF16)
    theirs = swap(to_send, core_mask)
    mine = attention(as_place(seq, core * HALF), doc_lengths, *near, HALF, BF16)
    place = as_place(core, x * ny + y, z)
    chip = merge(place, mine, theirs)
    chips = [chip, swap(chip, y_mask), swap(chip, x_mask), swap(chip, x_mask + y_mask)]

    *sends, keep, key_mine, key_send = weight(place, chips, f_same, f_other)
    received = [swap(part, (m + 1) * z_mask) for m, part in enumerate(sends)]
    key_other = swap(key_send, core_mask)
    rows_mine, rows_send, squares = reduce_planes(place, keep, received, devices)
    rows_other = swap(rows_send, core_mask)
    squares = lax.all_to_all(squares, AXES, 0, 0, tiled=True)
    return finish(place, squares, rows_mine, rows_other, key_mine, key_other)


def rings(queries, keys, values, grad_out, features, doc_lengths):
    seq_count = lax.axis_size("seq")
    rows = queries.shape[1]
    following = [(i, (i + 1) % seq_count) for i in range(seq_count)]
    preceding = [(i, (i - 1) % seq_count) for i in range(seq_count)]
    k_own, v_own = keys[0], values[0]
    k_prev = lax.ppermute(k_own, "seq", following)
    v_prev = lax.ppermute(v_own, "seq", following)
    seq = lax.axis_index("seq")
    place = jnp.stack([seq, jnp.zeros_like(seq)]).astype(jnp.int32)
    near = (queries[0], grad_out[0], k_prev, k_own, v_prev, v_own)
    parts = attention(place, doc_lengths, *near, KVH, F32)
    parts = parts.transpose(1, 0, 2).reshape(2 * rows, KVH * HD)
    after = lax.ppermute(parts[:rows], "seq", preceding)
    key_grad = (parts[rows:] + after).astype(BF16)
    columns = lax.all_to_all(features[0], "seq", split_axis=1, concat_axis=0, tiled=True)
    weight_part = lax.dot_general(
        columns,
        lax.all_gather(key_grad, "seq", axis=0, tiled=True),
        (((0,), (0,)), ((), ())),
        preferred_element_type=F32,
    )
    own_rows = lax.psum_scatter(weight_part, "dp", scatter_dimension=0, tiled=True)
    squares = lax.psum(jnp.sum(own_rows * own_rows), AXES)
    root_mean = jnp.sqrt(squares / (DW * KVH * HD) + 1e-06)
    return (key_grad[None], own_rows * jnp.minimum(1.0, 1.0 / root_mean))


def solution(mesh):
    in_specs = (
        P("dp", "seq", None),
        P("dp", "seq", None),
        P("dp", "seq", None),
        P("dp", "seq", None),
        P("dp", "seq", None),
        P("dp", None),
    )
    out_specs = (P("dp", "seq", None), P(("seq", "dp"), None))
    small = mesh.shape["seq"] == 2 * CORES and mesh.shape["dp"] == 8
    body = planes if small else rings
    return jax.shard_map(body, mesh=mesh, in_specs=in_specs, out_specs=out_specs, check_vma=False)
```

time: 230 us -> 79.1 us (0.34)
  waiting for transfers between devices: 99.4 us -> 30.8 us
  matrix products: 32.2 us -> 0 us
  blocking collectives: 46.3 us -> 19.2 us
  between operations: 14.9 us -> 0.74 us
  Pallas kernels: 0 us -> 12.3 us
  local copies, waits for them, and re-layouts: 13.1 us -> 1.89 us
  starting transfers between devices: 18.1 us -> 13.5 us
  other arithmetic: 4.76 us -> 0.23 us
    reduce_scatter x1 -> x0, waiting for transfers between devices: 69.9 us -> none  [shards(): lax.psum_scatter(weight_part, 'dp', scatter_dimension=0, tiled=True)]
    psum x1 -> x0, blocking collectives: 39.8 us -> none  [shards(): squares = lax.psum(jnp.sum(own_rows * own_rows), ('seq', 'dp'))]
    ppermute x0 -> x12, waiting for transfers between devices: none -> 23.8 us  [the longest x10 19 us: swap(): return lax.ppermute(array, AXES, [(i, i ^ mask) for i in range(devices)])]
    all_to_all x5 -> x1, waiting for transfers between devices: 29.5 us -> 7.03 us  [planes(): squares = lax.all_to_all(squares, AXES, 0, 0, tiled=True)]
    dot_general x3 -> x0, matrix products: 22 us -> none  [the longest x1 14.6 us: one_block(): jnp.einsum('hqk,qhd->kd', grad_scores, query_rows, preferred_element_type...]
    all_to_all x0 -> x1, blocking collectives: none -> 19.2 us  [planes(): lax.all_to_all(packed, AXES, 0, 0, axis_index_groups=members, tiled=True)]
    all_to_all x5 -> x1, starting transfers between devices: 18.1 us -> 3.87 us  [planes(): squares = lax.all_to_all(squares, AXES, 0, 0, tiled=True)]
    pallas_call x0 -> x7, Pallas kernels: none -> 12.3 us  [the longest x2 6.67 us: attention(): pl.pallas_call(functools.partial(attention_kernel, 4), grid_spec=pltpu.Pr...]
  transfers between devices with their start and end apart: 6 -> 13, of which waited for: 5 -> 8; matrix products, arithmetic and copies ran while one was open for 18% -> 0% of each run, Pallas kernels for 0% -> 9%
where the time goes in v1:
time: 79.1 us; the launch traced here: 78.7 us
  waiting for transfers between devices  30.8 us (39%)
  blocking collectives  19.2 us (24%)
  starting transfers between devices  13.5 us (17%)
  Pallas kernels  12.3 us (16%)
  local copies, waits for them, and re-layouts  1.89 us (2%)
    all_to_all x1, blocking collectives, planes(): lax.all_to_all(packed, AXES, 0, 0, axis_index_groups=members, tiled=True)  19.2 us
    ppermute x10, waiting for transfers between devices, swap(): return lax.ppermute(array, AXES, [(i, i ^ mask) for i in range(devices)])  19 us
    ppermute x10, starting transfers between devices, swap(): return lax.ppermute(array, AXES, [(i, i ^ mask) for i in range(devices)])  8.59 us
    all_to_all x1, waiting for transfers between devices, planes(): squares = lax.all_to_all(squares, AXES, 0, 0, tiled=True)  7.03 us
    pallas_call x2, Pallas kernels, attention(): pl.pallas_call(functools.partial(attention_kernel, 4), grid_spec=pltpu.Pr...  6.67 us
    all_to_all x1, starting transfers between devices, planes(): squares = lax.all_to_all(squares, AXES, 0, 0, tiled=True)  3.87 us
    ppermute x1, waiting for transfers between devices, planes(): k_prev = lax.ppermute(k_own, 'seq', following)  3.21 us
    pallas_call x1, Pallas kernels, weight(): pl.pallas_call(functools.partial(weight_kernel, nz), in_specs=[SMEM] + [v...  2.11 us
  transfers between devices with their start and end apart: 13, of which 8 were waited for; matrix products, arithmetic and copies ran while one was open for 0% of the time, Pallas kernels for 9%

profile of v1, /device:TPU:0, one launch (start us, length us, event | category | flops | bytes accessed | tf_op | source)
XLA Modules:
  0.0 78.7 jit_solution(14660584106800316167)
XLA Ops:
  0.6 0.0 copy-start.2
  0.6 1.2 %copy-done.2 = bf16[1,128,4096]{2,1,0:T(8,128)(2,1)S(1)} copy-done((bf16[1,128,4096]{2,1,0:T(8,128)(2,1)S(1)}, bf16[1,128,4096]{2,1,0:T(8,128)(2,1)}, u32[]{:S(2)}) %copy-start.2) | copy-done | bytes 1048600
  1.9 0.0 copy-start.3
  1.9 0.0 copy-start.4
  1.9 0.2 shard_map.80
  2.0 0.0 copy-start
  2.1 0.0 copy-start.1
  2.1 19.2 %all_to_all.10.f_same = bf16[4,4,128,256]{3,2,1,0:T(8,128)(2,1)S(1)} all-to-all(bf16[4,4,128,256]{3,2,1,0:T(8,128)(2,1)S(1)} %shard_map.80), channel_id=1, replica_groups={{0,1,16,17},{2,3,18,19},{4,5,20,21},{6,7,22,23},{8,9,24,25},{10,11,26,2..., dimensions={0} | all-to-all | bytes 2097152 | tf_op jit(solution)/shard_map/all_to_all | solution.py:284
  21.3 0.0 collective-permute-start.6
  21.3 0.0 copy-done.3
  21.3 0.5 collective-permute-start
  21.8 0.0 copy-done.4
  21.8 0.5 collective-permute-start.1
  22.3 0.1 pad_add_fusion.1.place
  22.4 0.1 pad_add_fusion.2.place
  22.5 3.2 %collective-permute-done.k_prev = bf16[128,512]{1,0:T(8,128)(2,1)S(1)} collective-permute-done((bf16[128,512]{1,0:T(8,128)(2,1)S(1)}, bf16[128,512]{1,0:T(8,128)(2,1)S(1)}, u32[]{:S(2)}, u32[]{:S(2)}) %collective-permute-start) | collective-permute-done | bytes 131104 | tf_op jit(solution)/shard_map/ppermute | solution.py:271
  25.7 1.5 %collective-permute-done.1.v_prev = bf16[128,512]{1,0:T(8,128)(2,1)} collective-permute-done((bf16[128,512]{1,0:T(8,128)(2,1)S(1)}, bf16[128,512]{1,0:T(8,128)(2,1)}, u32[]{:S(2)}, u32[]{:S(2)}) %collective-permute-start.1) | collective-permute-done | bytes 131104 | tf_op jit(solution)/shard_map/ppermute | solution.py:272
  27.2 0.0 copy-start.5
  27.2 0.0 copy-done
  27.2 0.0 copy-done.1
  27.2 0.6 copy-done.5
  27.9 3.3 %shard_map.78 = bf16[2,256,128]{2,1,0:T(8,128)(2,1)S(1)} custom-call(s32[2]{0:T(128)S(1)} %pad_add_fusion.2.place, s32[1,8]{1,0:T(1,128)S(1)} %copy-done.5, bf16[128,4096]{1,0:T(8,128)(2,1)S(1)} %bitcast.11, bf16[128,4096]{1,0:T(8,128)(2,1)S(1)} %bitcast.13, bf16[128,512]{1,0:T(8,128)(2,1)S(1)} %collective-permute-done.k_prev, ...), custom_call_target="tpu_custom_call" | custom-call | flops 402653184 | bytes 1048576 | tf_op jit(solution)/shard_map/pallas_call | solution.py:80
  31.2 0.1 collective-permute-start.2
  31.3 0.1 pad_add_fusion.place
  31.4 3.3 %shard_map.77.mine = bf16[2,256,128]{2,1,0:T(8,128)(2,1)S(1)} custom-call(s32[2]{0:T(128)S(1)} %pad_add_fusion.1.place, s32[1,8]{1,0:T(1,128)S(1)} %copy-done.5, bf16[128,4096]{1,0:T(8,128)(2,1)S(1)} %bitcast.12, bf16[128,4096]{1,0:T(8,128)(2,1)S(1)} %bitcast.14, bf16[128,512]{1,0:T(8,128)(2,1)S(1)} %collective-permute-done.k_prev, ...), custom_call_target="tpu_custom_call" | custom-call | flops 402653184 | bytes 1048576 | tf_op jit(solution)/shard_map/pallas_call | solution.py:80
  34.7 0.0 collective-permute-done.2.theirs
  34.7 0.6 shard_map.79.g0
  35.3 1.0 %collective-permute-start.5 = (bf16[384,256]{1,0:T(8,128)(2,1)S(1)}, bf16[384,256]{1,0:T(8,128)(2,1)S(1)}, u32[]{:S(2)}, u32[]{:S(2)}) collective-permute-start(bf16[384,256]{1,0:T(8,128)(2,1)S(1)} %shard_map.79.g0), channel_id=1, source_target_pairs={{0,17},{1,16},{2,19},{3,18},{4,21},{5,20},{6,23},{7,22},{8,25},{9,... | collective-permute-start | bytes 589832 | tf_op jit(solution)/shard_map/ppermute | solution.py:266
  36.3 1.5 %collective-permute-start.4 = (bf16[384,256]{1,0:T(8,128)(2,1)S(1)}, bf16[384,256]{1,0:T(8,128)(2,1)S(1)}, u32[]{:S(2)}, u32[]{:S(2)}) collective-permute-start(bf16[384,256]{1,0:T(8,128)(2,1)S(1)} %shard_map.79.g0), channel_id=1, source_target_pairs={{0,16},{1,17},{2,18},{3,19},{4,20},{5,21},{6,22},{7,23},{8,24},{9,... | collective-permute-start | bytes 589832 | tf_op jit(solution)/shard_map/ppermute | solution.py:266
  37.8 1.1 %collective-permute-start.3 = (bf16[384,256]{1,0:T(8,128)(2,1)S(1)}, bf16[384,256]{1,0:T(8,128)(2,1)S(1)}, u32[]{:S(2)}, u32[]{:S(2)}) collective-permute-start(bf16[384,256]{1,0:T(8,128)(2,1)S(1)} %shard_map.79.g0), channel_id=1, source_target_pairs={{0,1},{1,0},{2,3},{3,2},{4,5},{5,4},{6,7},{7,6},{8,9},{9,8},{10,11... | collective-permute-start | bytes 589832 | tf_op jit(solution)/shard_map/ppermute | solution.py:266
  38.9 5.1 %collective-permute-done.5.g3 = bf16[384,256]{1,0:T(8,128)(2,1)S(1)} collective-permute-done((bf16[384,256]{1,0:T(8,128)(2,1)S(1)}, bf16[384,256]{1,0:T(8,128)(2,1)S(1)}, u32[]{:S(2)}, u32[]{:S(2)}) %collective-permute-start.5) | collective-permute-done | bytes 196640 | tf_op jit(solution)/shard_map/ppermute | solution.py:266
  44.0 3.3 %collective-permute-done.4.g2 = bf16[384,256]{1,0:T(8,128)(2,1)S(1)} collective-permute-done((bf16[384,256]{1,0:T(8,128)(2,1)S(1)}, bf16[384,256]{1,0:T(8,128)(2,1)S(1)}, u32[]{:S(2)}, u32[]{:S(2)}) %collective-permute-start.4) | collective-permute-done | bytes 196640 | tf_op jit(solution)/shard_map/ppermute | solution.py:266
  47.3 0.5 collective-permute-done.3.g1
  47.8 0.0 collective-permute-done.6.f_other
  47.8 2.1 %shard_map.81 = (bf16[256,256]{1,0:T(8,128)(2,1)S(1)}, bf16[256,256]{1,0:T(8,128)(2,1)S(1)}, bf16[256,256]{1,0:T(8,128)(2,1)S(1)}, f32[256,256]{1,0:T(8,128)S(1)...) custom-call(s32[3]{0:T(128)S(1)} %pad_add_fusion.place, bf16[384,256]{1,0:T(8,128)(2,1)S(1)} %shard_map.79.g0, ...), custom_call_target="tpu_custom_call" | custom-call | flops 536870912 | bytes 4194304 | tf_op jit(solution)/shard_map/pallas_call | solution.py:191
  49.9 1.6 %collective-permute-start.7 = (bf16[256,256]{1,0:T(8,128)(2,1)S(1)}, bf16[256,256]{1,0:T(8,128)(2,1)S(1)}, u32[]{:S(2)}, u32[]{:S(2)}) collective-permute-start(bf16[256,256]{1,0:T(8,128)(2,1)S(1)} %get-tuple-element.12), channel_id=1, source_target_pairs={{0,2},{1,3},{2,0},{3,1},{4,6},{5,7},{6,4},{7,5},{8,10},{9,11},{10,... | collective-permute-start | bytes 393224 | tf_op jit(solution)/shard_map/ppermute | solution.py:266
  51.6 2.6 %collective-permute-start.8 = (bf16[256,256]{1,0:T(8,128)(2,1)S(1)}, bf16[256,256]{1,0:T(8,128)(2,1)S(1)}, u32[]{:S(2)}, u32[]{:S(2)}) collective-permute-start(bf16[256,256]{1,0:T(8,128)(2,1)S(1)} %get-tuple-element.13), channel_id=1, source_target_pairs={{0,4},{1,5},{2,6},{3,7},{4,0},{5,1},{6,2},{7,3},{8,12},{9,13},{10,... | collective-permute-start | bytes 393224 | tf_op jit(solution)/shard_map/ppermute | solution.py:266
  54.1 0.2 collective-permute-start.9
  54.4 2.8 %collective-permute-done.7.r1 = bf16[256,256]{1,0:T(8,128)(2,1)S(1)} collective-permute-done((bf16[256,256]{1,0:T(8,128)(2,1)S(1)}, bf16[256,256]{1,0:T(8,128)(2,1)S(1)}, u32[]{:S(2)}, u32[]{:S(2)}) %collective-permute-start.7) | collective-permute-done | bytes 131104 | tf_op jit(solution)/shard_map/ppermute | solution.py:266
  57.2 7.3 %collective-permute-done.8.r2 = bf16[256,256]{1,0:T(8,128)(2,1)S(1)} collective-permute-done((bf16[256,256]{1,0:T(8,128)(2,1)S(1)}, bf16[256,256]{1,0:T(8,128)(2,1)S(1)}, u32[]{:S(2)}, u32[]{:S(2)}) %collective-permute-start.8) | collective-permute-done | bytes 131104 | tf_op jit(solution)/shard_map/ppermute | solution.py:266
  64.5 0.0 collective-permute-done.9.r3
  64.5 1.3 %shard_map.82 = (f32[256,128]{1,0:T(8,128)S(1)}, f32[256,128]{1,0:T(8,128)S(1)}, f32[32,1,128]{2,1,0:T(1,128)}) custom-call(s32[3]{0:T(128)S(1)} %pad_add_fusion.place, f32[256,256]{1,0:T(8,128)S(1)} %get-tuple-element.11.keep, bf16[256,256]{1,0:T(8,128)(2,1)S(1)} %collective-permute-done.7.r1, bf16[256,256]{1,0:T(8,128)(2,1)S(1)} %collective-permute-done.8.r2, ...), custom_call_target="tpu_custom_call" | custom-call | flops 524288 | bytes 917504 | tf_op jit(solution)/shard_map/pallas_call | solution.py:216
  65.8 0.0 collective-permute-start.10
  65.8 0.5 collective-permute-start.11
  66.3 3.9 %all-to-all-start.1 = ((f32[32,1,128]{2,1,0:T(1,128)}), f32[32,1,128]{2,1,0:T(1,128)S(1)}, u32[]{:S(2)}, u32[]{:S(2)}) async-start(f32[32,1,128]{2,1,0:T(1,128)} %get-tuple-element.15), calls=%async_computation.1 | async-start | bytes 32768 | tf_op jit(solution)/shard_map/all_to_all | solution.py:300
  70.1 0.0 collective-permute-done.11.key_theirs
  70.2 7.0 %all-to-all-done.1.squares = f32[32,1,128]{2,1,0:T(1,128)S(1)} async-done(((f32[32,1,128]{2,1,0:T(1,128)}), f32[32,1,128]{2,1,0:T(1,128)S(1)}, u32[]{:S(2)}, u32[]{:S(2)}) %all-to-all-start.1) | async-done | bytes 16416 | tf_op jit(solution)/shard_map/all_to_all | solution.py:300
  77.2 0.0 collective-permute-done.10.theirs
  77.2 1.5 %shard_map.83 = (bf16[1,128,512]{2,1,0:T(8,128)(2,1)}, f32[128,512]{1,0:T(8,128)}) custom-call(s32[3]{0:T(128)S(1)} %pad_add_fusion.place, f32[32,1,128]{2,1,0:T(1,128)S(1)} %all-to-all-done.1.squares, f32[256,128]{1,0:T(8,128)S(1)} %get-tuple-element.16.mine, f32[256,128]{1,0:T(8,128)S(1)} %collective-permute-done.10.theirs, ...), custom_call_target="tpu_custom_call" | custom-call | flops 262144 | bytes 1048576 | tf_op jit(solution)/shard_map/pallas_call | solution.py:243
Async XLA Ops:
  0.6 1.2 %copy-start.2 = (bf16[1,128,4096]{2,1,0:T(8,128)(2,1)S(1)}, bf16[1,128,4096]{2,1,0:T(8,128)(2,1)}, u32[]{:S(2)}) copy-start(bf16[1,128,4096]{2,1,0:T(8,128)(2,1)} %param.10) | copy-start | bytes 3145732
  1.9 19.5 %copy-start.3 = (bf16[1,128,512]{2,1,0:T(8,128)(2,1)S(1)}, bf16[1,128,512]{2,1,0:T(8,128)(2,1)}, u32[]{:S(2)}) copy-start(bf16[1,128,512]{2,1,0:T(8,128)(2,1)} %param.7) | copy-start | bytes 393220
  1.9 20.0 %copy-start.4 = (bf16[1,128,512]{2,1,0:T(8,128)(2,1)S(1)}, bf16[1,128,512]{2,1,0:T(8,128)(2,1)}, u32[]{:S(2)}) copy-start(bf16[1,128,512]{2,1,0:T(8,128)(2,1)} %param.8) | copy-start | bytes 393220
  2.0 25.2 %copy-start = (bf16[1,128,4096]{2,1,0:T(8,128)(2,1)S(1)}, bf16[1,128,4096]{2,1,0:T(8,128)(2,1)}, u32[]{:S(2)}) copy-start(bf16[1,128,4096]{2,1,0:T(8,128)(2,1)} %param.6) | copy-start | bytes 3145732
  2.1 25.2 %copy-start.1 = (bf16[1,128,4096]{2,1,0:T(8,128)(2,1)S(1)}, bf16[1,128,4096]{2,1,0:T(8,128)(2,1)}, u32[]{:S(2)}) copy-start(bf16[1,128,4096]{2,1,0:T(8,128)(2,1)} %param.9) | copy-start | bytes 3145732
  21.3 26.5 %collective-permute-start.6 = (bf16[4,4,128,256]{3,2,1,0:T(8,128)(2,1)S(1)}, bf16[4,4,128,256]{3,2,1,0:T(8,128)(2,1)}, u32[]{:S(2)}, u32[]{:S(2)}) collective-permute-start(bf16[4,4,128,256]{3,2,1,0:T(8,128)(2,1)S(1)} %all_to_all.10.f_same), channel_id=1, source_target_pairs={{0,8},{1,9},{2,10},{3,11},{4,12},{5,13},{6,14},{7,15},{8,0},{9,1},... | collective-permute-start | bytes 3145736 | tf_op jit(solution)/shard_map/ppermute | solution.py:266
  21.3 4.4 %collective-permute-start = (bf16[128,512]{1,0:T(8,128)(2,1)S(1)}, bf16[128,512]{1,0:T(8,128)(2,1)S(1)}, u32[]{:S(2)}, u32[]{:S(2)}) collective-permute-start(bf16[128,512]{1,0:T(8,128)(2,1)S(1)} %bitcast.16), channel_id=1, source_target_pairs={{0,8},{8,16},{16,24},{24,0},{1,9},{9,17},{17,25},{25,1},{2,10},{10... | collective-permute-start | bytes 393224 | tf_op jit(solution)/shard_map/ppermute | solution.py:271
  21.8 5.4 %collective-permute-start.1 = (bf16[128,512]{1,0:T(8,128)(2,1)S(1)}, bf16[128,512]{1,0:T(8,128)(2,1)}, u32[]{:S(2)}, u32[]{:S(2)}) collective-permute-start(bf16[128,512]{1,0:T(8,128)(2,1)S(1)} %bitcast.19), channel_id=1, source_target_pairs={{0,8},{8,16},{16,24},{24,0},{1,9},{9,17},{17,25},{25,1},{2,10},{10... | collective-permute-start | bytes 393224 | tf_op jit(solution)/shard_map/ppermute | solution.py:272
  27.2 0.7 copy-start.5
  31.2 3.5 %collective-permute-start.2 = (bf16[2,256,128]{2,1,0:T(8,128)(2,1)S(1)}, bf16[2,256,128]{2,1,0:T(8,128)(2,1)S(1)}, u32[]{:S(2)}, u32[]{:S(2)}) collective-permute-start(bf16[2,256,128]{2,1,0:T(8,128)(2,1)S(1)} %shard_map.78), channel_id=1, source_target_pairs={{0,8},{1,9},{2,10},{3,11},{4,12},{5,13},{6,14},{7,15},{8,0},{9,1},... | collective-permute-start | bytes 393224 | tf_op jit(solution)/shard_map/ppermute | solution.py:266
  35.3 8.7 %collective-permute-start.5 = (bf16[384,256]{1,0:T(8,128)(2,1)S(1)}, bf16[384,256]{1,0:T(8,128)(2,1)S(1)}, u32[]{:S(2)}, u32[]{:S(2)}) collective-permute-start(bf16[384,256]{1,0:T(8,128)(2,1)S(1)} %shard_map.79.g0), channel_id=1, source_target_pairs={{0,17},{1,16},{2,19},{3,18},{4,21},{5,20},{6,23},{7,22},{8,25},{9,... | collective-permute-start | bytes 589832 | tf_op jit(solution)/shard_map/ppermute | solution.py:266
  36.3 11.0 %collective-permute-start.4 = (bf16[384,256]{1,0:T(8,128)(2,1)S(1)}, bf16[384,256]{1,0:T(8,128)(2,1)S(1)}, u32[]{:S(2)}, u32[]{:S(2)}) collective-permute-start(bf16[384,256]{1,0:T(8,128)(2,1)S(1)} %shard_map.79.g0), channel_id=1, source_target_pairs={{0,16},{1,17},{2,18},{3,19},{4,20},{5,21},{6,22},{7,23},{8,24},{9,... | collective-permute-start | bytes 589832 | tf_op jit(solution)/shard_map/ppermute | solution.py:266
  37.8 10.0 %collective-permute-start.3 = (bf16[384,256]{1,0:T(8,128)(2,1)S(1)}, bf16[384,256]{1,0:T(8,128)(2,1)S(1)}, u32[]{:S(2)}, u32[]{:S(2)}) collective-permute-start(bf16[384,256]{1,0:T(8,128)(2,1)S(1)} %shard_map.79.g0), channel_id=1, source_target_pairs={{0,1},{1,0},{2,3},{3,2},{4,5},{5,4},{6,7},{7,6},{8,9},{9,8},{10,11... | collective-permute-start | bytes 589832 | tf_op jit(solution)/shard_map/ppermute | solution.py:266
  49.9 7.3 %collective-permute-start.7 = (bf16[256,256]{1,0:T(8,128)(2,1)S(1)}, bf16[256,256]{1,0:T(8,128)(2,1)S(1)}, u32[]{:S(2)}, u32[]{:S(2)}) collective-permute-start(bf16[256,256]{1,0:T(8,128)(2,1)S(1)} %get-tuple-element.12), channel_id=1, source_target_pairs={{0,2},{1,3},{2,0},{3,1},{4,6},{5,7},{6,4},{7,5},{8,10},{9,11},{10,... | collective-permute-start | bytes 393224 | tf_op jit(solution)/shard_map/ppermute | solution.py:266
  51.6 12.9 %collective-permute-start.8 = (bf16[256,256]{1,0:T(8,128)(2,1)S(1)}, bf16[256,256]{1,0:T(8,128)(2,1)S(1)}, u32[]{:S(2)}, u32[]{:S(2)}) collective-permute-start(bf16[256,256]{1,0:T(8,128)(2,1)S(1)} %get-tuple-element.13), channel_id=1, source_target_pairs={{0,4},{1,5},{2,6},{3,7},{4,0},{5,1},{6,2},{7,3},{8,12},{9,13},{10,... | collective-permute-start | bytes 393224 | tf_op jit(solution)/shard_map/ppermute | solution.py:266
  54.1 10.3 %collective-permute-start.9 = (bf16[256,256]{1,0:T(8,128)(2,1)S(1)}, bf16[256,256]{1,0:T(8,128)(2,1)S(1)}, u32[]{:S(2)}, u32[]{:S(2)}) collective-permute-start(bf16[256,256]{1,0:T(8,128)(2,1)S(1)} %get-tuple-element.14), channel_id=1, source_target_pairs={{0,6},{1,7},{2,4},{3,5},{4,2},{5,3},{6,0},{7,1},{8,14},{9,15},{10,... | collective-permute-start | bytes 393224 | tf_op jit(solution)/shard_map/ppermute | solution.py:266
  65.8 11.4 %collective-permute-start.10 = (f32[256,128]{1,0:T(8,128)S(1)}, f32[256,128]{1,0:T(8,128)S(1)}, u32[]{:S(2)}, u32[]{:S(2)}) collective-permute-start(f32[256,128]{1,0:T(8,128)S(1)} %get-tuple-element.17), channel_id=1, source_target_pairs={{0,8},{1,9},{2,10},{3,11},{4,12},{5,13},{6,14},{7,15},{8,0},{9,1},... | collective-permute-start | bytes 393224 | tf_op jit(solution)/shard_map/ppermute | solution.py:266
  65.8 4.4 %collective-permute-start.11 = (bf16[128,256]{1,0:T(8,128)(2,1)S(1)}, bf16[128,256]{1,0:T(8,128)(2,1)S(1)}, u32[]{:S(2)}, u32[]{:S(2)}) collective-permute-start(bf16[128,256]{1,0:T(8,128)(2,1)S(1)} %get-tuple-element.19), channel_id=1, source_target_pairs={{0,8},{1,9},{2,10},{3,11},{4,12},{5,13},{6,14},{7,15},{8,0},{9,1},... | collective-permute-start | bytes 196616 | tf_op jit(solution)/shard_map/ppermute | solution.py:266
  66.3 10.9 %all-to-all-start.1 = ((f32[32,1,128]{2,1,0:T(1,128)}), f32[32,1,128]{2,1,0:T(1,128)S(1)}, u32[]{:S(2)}, u32[]{:S(2)}) async-start(f32[32,1,128]{2,1,0:T(1,128)} %get-tuple-element.15), calls=%async_computation.1 | async-start | bytes 32768 | tf_op jit(solution)/shard_map/all_to_all | solution.py:300

commit v2 on v1

--- a/solution.py
+++ b/solution.py
@@ -93,29 +93,31 @@
     )(place, lengths, q, g, k_prev, k_own, v_prev, v_own)
 
 
-def pack_kernel(sizes, x_ref, out):
-    nx, ny, nz = sizes
-    block = DW // (nx * CORES * ny * nz)
-    for x in range(nx):
-        for y in range(ny):
-            for z in range(nz):
-                for c in range(CORES):
-                    source = ((x * CORES + c) * nz + z) * ny + y
-                    out[x * ny + y, z, :, c * block : (c + 1) * block] = x_ref[
-                        :, source * block : (source + 1) * block
-                    ]
-
-
-def pack(features, sizes):
+def pack_kernel(sizes, place, x_ref, *outs):
+    ny, nz = sizes
+    block = outs[0].shape[2] // CORES
+    x, y = place[1] // ny, place[1] % ny
+    for m, out in enumerate(outs):
+        for z in range(nz):
+            for c in range(CORES):
+                source = (((x ^ (m // ny)) * CORES + c) * nz + z) * ny + (y ^ (m % ny))
+                at = pl.ds(pl.multiple_of(source * block, block), block)
+                out[z, :, c * block : (c + 1) * block] = x_ref[:, at]
+
+
+def pack(place, features, sizes):
     nx, ny, nz = sizes
     rows = features.shape[0]
-    shape = (nx * ny, nz, rows, DW // (nx * ny * nz))
-    return pl.pallas_call(
-        functools.partial(pack_kernel, sizes),
-        out_shape=jax.ShapeDtypeStruct(shape, BF16),
-        compiler_params=params(),
-        cost_estimate=cost(0, 2 * rows * DW * 2),
-    )(features)
+    shape = jax.ShapeDtypeStruct((nz, rows, DW // (nx * ny * nz)), BF16)
+    vmem = pl.BlockSpec(memory_space=pltpu.VMEM)
+    return pl.pallas_call(
+        functools.partial(pack_kernel, (ny, nz)),
+        in_specs=[SMEM, vmem],
+        out_specs=[vmem] * (nx * ny),
+        out_shape=[shape] * (nx * ny),
+        compiler_params=params(),
+        cost_estimate=cost(0, 64 << 20),
+    )(place, features)
 
 
 def merge_kernel(place, mine, theirs, out):
@@ -152,27 +154,25 @@
     )(place, mine, theirs)
 
 
-def weight_kernel(nz, place, g0, g1, g2, g3, f_same, f_other, *rest):
-    sends, (keep, key_mine, key_theirs, same, other) = rest[: nz - 1], rest[nz - 1 :]
-    rows = g0.shape[0] // 3
-    core, chip, z = place[0], place[1], place[2]
-    chips = (g0, g1, g2, g3)
+def weight_kernel(nz, place, *refs):
+    chips, f_same, f_other = refs[:4], refs[4:8], refs[8]
+    sends, (keep, key_mine, key_theirs, same, other) = refs[9 : 8 + nz], refs[8 + nz :]
+    rows = chips[0].shape[0] // 3
+    core, z = place[0], place[2]
     for m in range(4):
         even = chips[m][rows : 2 * rows]
         odd = (chips[m][2 * rows :].astype(F32) + chips[m ^ 2][:rows].astype(F32)).astype(BF16)
-        at = pl.ds(pl.multiple_of((chip ^ m) * rows, rows), rows)
         own = jnp.where(core == 0, even, odd)
         far = jnp.where(core == 0, odd, even)
-        same[at] = own
-        other[at] = far
+        same[m * rows : (m + 1) * rows] = own
+        other[m * rows : (m + 1) * rows] = far
         if m == 0:
             key_mine[...] = own
             key_theirs[...] = far
     tn = (((0,), (0,)), ((), ()))
     for m in (2, 3, 1, 0):
-        block = z ^ m
-        left = f_same[:, pl.ds(block, 1)].reshape(4 * rows, WIDE)
-        right = f_other[:, pl.ds(block, 1)].reshape(4 * rows, WIDE)
+        left = jnp.concatenate([f[z ^ m] for f in f_same], axis=0)
+        right = jnp.concatenate([f_other[n, z ^ m] for n in range(4)], axis=0)
         product = lax.dot_general(same[...], left, tn, preferred_element_type=F32)
         product += lax.dot_general(other[...], right, tn, preferred_element_type=F32)
         if m == 0:
@@ -183,20 +183,20 @@
 
 def weight(place, chips, f_same, f_other):
     rows = chips[0].shape[0] // 3
-    nz = f_same.shape[1]
-    vmem = pl.BlockSpec(memory_space=pltpu.VMEM)
-    square = (WIDE, f_same.shape[3])
+    nz = f_same[0].shape[0]
+    vmem = pl.BlockSpec(memory_space=pltpu.VMEM)
+    square = (WIDE, f_same[0].shape[2])
     shapes = [jax.ShapeDtypeStruct(square, BF16)] * (nz - 1)
     shapes += [jax.ShapeDtypeStruct(square, F32)] + [jax.ShapeDtypeStruct((rows, WIDE), BF16)] * 2
     return pl.pallas_call(
         functools.partial(weight_kernel, nz),
-        in_specs=[SMEM] + [vmem] * 6,
+        in_specs=[SMEM] + [vmem] * 9,
         out_specs=[vmem] * len(shapes),
         out_shape=shapes,
         scratch_shapes=[pltpu.VMEM((4 * rows, WIDE), BF16)] * 2,
         compiler_params=params(),
         cost_estimate=cost(2 * 8 * rows * WIDE * 4 * WIDE, 4 << 20),
-    )(place, *chips, f_same, f_other)
+    )(place, *chips, *f_same, f_other)
 
 
 def reduce_kernel(place, keep, r1, r2, r3, mine, theirs, squares):
@@ -259,7 +259,7 @@
     nx, ny = seq_count // CORES, 2
     nz = dp_count // ny
     seq, dp = lax.axis_index("seq"), lax.axis_index("dp")
-    core, x, y, z = seq % CORES, seq // CORES, dp % ny, dp // ny
+    core, x, y, z = seq & 1, seq >> 1, dp & 1, dp >> 1
     as_place = lambda *items: jnp.stack([jnp.asarray(i, jnp.int32) for i in items])
 
     def swap(array, mask):
@@ -271,29 +271,22 @@
     k_prev = lax.ppermute(k_own, "seq", following)
     v_prev = lax.ppermute(v_own, "seq", following)
 
-    packed = pack(features[0], (nx, ny, nz))
-    members = [
-        [
-            ((a * CORES + c) * nz + b) * ny + e
-            for a in range(nx)
-            for e in range(ny)
-        ]
-        for c in range(CORES)
-        for b in range(nz)
-    ]
-    f_same = lax.all_to_all(packed, AXES, 0, 0, axis_index_groups=members, tiled=True)
-    f_other = swap(f_same, core_mask)
+    place = as_place(core, x * ny + y, z)
+    masks = [0, y_mask, x_mask, x_mask + y_mask]
+    packed = pack(place, features[0], (nx, ny, nz))
+    f_same = [packed[0]] + [swap(part, mask) for part, mask in zip(packed[1:], masks[1:])]
 
     near = (queries[0], grad_out[0], k_prev, k_own, v_prev, v_own)
     to_send = attention(as_place(seq, (1 - core) * HALF), doc_lengths, *near, HALF, BF16)
     theirs = swap(to_send, core_mask)
     mine = attention(as_place(seq, core * HALF), doc_lengths, *near, HALF, BF16)
-    place = as_place(core, x * ny + y, z)
     chip = merge(place, mine, theirs)
-    chips = [chip, swap(chip, y_mask), swap(chip, x_mask), swap(chip, x_mask + y_mask)]
+    chips = [chip] + [swap(chip, mask) for mask in masks[1:]]
+    f_ready, _ = lax.optimization_barrier((f_same, chip))
+    f_other = swap(jnp.stack(f_ready), core_mask)
 
     *sends, keep, key_mine, key_send = weight(place, chips, f_same, f_other)
-    received = [swap(part, (m + 1) * z_mask) for m, part in enumerate(sends)]
+    received = [swap(sends[m], (m + 1) * z_mask) for m in (1, 2, 0)]
     key_other = swap(key_send, core_mask)
     rows_mine, rows_send, squares = reduce_planes(place, keep, received, devices)
     rows_other = swap(rows_send, core_mask)

time: 79.1 us -> 63.9 us (0.81)
  blocking collectives: 19.2 us -> 0 us
  starting transfers between devices: 13.5 us -> 20.4 us
  waiting for transfers between devices: 30.8 us -> 26.2 us
  local copies, waits for them, and re-layouts: 1.89 us -> 4.92 us
  Pallas kernels: 12.3 us -> 11 us
    all_to_all x1 -> x0, blocking collectives: 19.2 us -> none  [planes(): lax.all_to_all(packed, AXES, 0, 0, axis_index_groups=members, tiled=True)]
    ppermute x10 -> x13, starting transfers between devices: 8.59 us -> 12 us  [swap(): return lax.ppermute(array, AXES, [(i, i ^ mask) for i in range(devices)])]
    ppermute x1, waiting for transfers between devices: 3.21 us -> 0.01 us  [planes(): k_prev = lax.ppermute(k_own, 'seq', following)]
    unnamed x12 -> x18, local copies, waits for them, and re-layouts: 1.89 us -> 4.92 us
    ppermute x1, starting transfers between devices: 0.52 us -> 2.6 us  [planes(): v_prev = lax.ppermute(v_own, 'seq', following)]
    ppermute x1, waiting for transfers between devices: 1.51 us -> 0.01 us  [planes(): v_prev = lax.ppermute(v_own, 'seq', following)]
    all_to_all x1, starting transfers between devices: 3.87 us -> 5.33 us  [planes(): squares = lax.all_to_all(squares, AXES, 0, 0, tiled=True)]
    pallas_call x2, Pallas kernels: 6.67 us -> 5.45 us  [attention(): pl.pallas_call(functools.partial(attention_kernel, 4), grid_spec=pltpu.Pr...]
  transfers between devices with their start and end apart: 13 -> 16, of which waited for: 8 -> 7; matrix products, arithmetic and copies ran while one was open for 0% -> 0% of each run, Pallas kernels for 9% -> 11%
where the time goes in v2:
time: 63.9 us; the launch traced here: 63.7 us
  waiting for transfers between devices  26.2 us (41%)
  starting transfers between devices  20.4 us (32%)
  Pallas kernels  11 us (17%)
  local copies, waits for them, and re-layouts  4.92 us (8%)
  between operations  0.77 us (1%)
    ppermute x13, waiting for transfers between devices, swap(): return lax.ppermute(array, AXES, [(i, i ^ mask) for i in range(devices)])  19.2 us
    ppermute x13, starting transfers between devices, swap(): return lax.ppermute(array, AXES, [(i, i ^ mask) for i in range(devices)])  12 us
    all_to_all x1, waiting for transfers between devices, planes(): squares = lax.all_to_all(squares, AXES, 0, 0, tiled=True)  7.03 us
    pallas_call x2, Pallas kernels, attention(): pl.pallas_call(functools.partial(attention_kernel, 4), grid_spec=pltpu.Pr...  5.45 us
    all_to_all x1, starting transfers between devices, planes(): squares = lax.all_to_all(squares, AXES, 0, 0, tiled=True)  5.33 us
    unnamed x18, local copies, waits for them, and re-layouts  4.92 us
    ppermute x1, starting transfers between devices, planes(): v_prev = lax.ppermute(v_own, 'seq', following)  2.6 us
    pallas_call x1, Pallas kernels, finish(): pl.pallas_call(finish_kernel, in_specs=[SMEM] + [vmem] * 5, out_specs=[vm...  1.51 us
  transfers between devices with their start and end apart: 16, of which 7 were waited for; matrix products, arithmetic and copies ran while one was open for 0% of the time, Pallas kernels for 11%

profile of v2, /device:TPU:0, one launch (start us, length us, event | category | flops | bytes accessed | tf_op | source)
XLA Modules:
  0.0 63.7 jit_solution(2545051962296980467)
XLA Ops:
  0.6 0.0 copy-start
  0.6 0.5 collective-permute-start
  1.1 2.6 %collective-permute-start.1 = (bf16[128,512]{1,0:T(8,128)(2,1)}, bf16[128,512]{1,0:T(8,128)(2,1)S(1)}, u32[]{:S(2)}, u32[]{:S(2)}) collective-permute-start(bf16[128,512]{1,0:T(8,128)(2,1)} %bitcast.27), channel_id=1, source_target_pairs={{0,8},{8,16},{16,24},{24,0},{1,9},{9,17},{17,25},{25,1},{2,10},{10... | collective-permute-start | bytes 393224 | tf_op jit(solution)/shard_map/ppermute | solution.py:272
  3.7 0.1 pad_add_fusion.place
  3.8 0.0 copy-start.3
  3.8 1.2 %copy-done.3 = bf16[1,128,4096]{2,1,0:T(8,128)(2,1)S(1)} copy-done((bf16[1,128,4096]{2,1,0:T(8,128)(2,1)S(1)}, bf16[1,128,4096]{2,1,0:T(8,128)(2,1)}, u32[]{:S(2)}) %copy-start.3) | copy-done | bytes 1048600
  5.0 0.8 %shard_map.80 = (bf16[4,128,256]{2,1,0:T(8,128)(2,1)S(1)}, bf16[4,128,256]{2,1,0:T(8,128)(2,1)S(1)}, bf16[4,128,256]{2,1,0:T(8,128)(2,1)S(1)}, bf16[4,128,256]{2,1,0:T(8,128)(2,1)S(1)}) custom-call(s32[3]{0:T(128)S(1)} %pad_add_fusion.place, bf16[128,4096]{1,0:T(8,128)(2,1)S(1)} %bitcast.19), custom_call_target="tpu_custom_call" | custom-call | bytes 67108864 | tf_op jit(solution)/shard_map/pallas_call | solution.py:113
  5.9 1.6 %collective-permute-start.6 = (bf16[4,128,256]{2,1,0:T(8,128)(2,1)S(1)}, bf16[4,128,256]{2,1,0:T(8,128)(2,1)S(1)}, u32[]{:S(2)}, u32[]{:S(2)}) collective-permute-start(bf16[4,128,256]{2,1,0:T(8,128)(2,1)S(1)} %get-tuple-element.20), channel_id=1, source_target_pairs={{0,1},{1,0},{2,3},{3,2},{4,5},{5,4},{6,7},{7,6},{8,9},{9,8},{10,11... | collective-permute-start | bytes 786440 | tf_op jit(solution)/shard_map/ppermute | solution.py:266
  7.5 0.5 collective-permute-start.7
  8.0 1.4 %collective-permute-start.8 = (bf16[4,128,256]{2,1,0:T(8,128)(2,1)S(1)}, bf16[4,128,256]{2,1,0:T(8,128)(2,1)S(1)}, u32[]{:S(2)}, u32[]{:S(2)}) collective-permute-start(bf16[4,128,256]{2,1,0:T(8,128)(2,1)S(1)} %get-tuple-element.22), channel_id=1, source_target_pairs={{0,17},{1,16},{2,19},{3,18},{4,21},{5,20},{6,23},{7,22},{8,25},{9,... | collective-permute-start | bytes 786440 | tf_op jit(solution)/shard_map/ppermute | solution.py:266
  9.4 0.1 pad_add_fusion.2.place
  9.5 0.0 collective-permute-done.k_prev
  9.5 0.0 collective-permute-done.1.v_prev
  9.5 0.0 copy-start.8
  9.5 0.0 copy-done
  9.5 0.6 %copy-done.8 = s32[1,8]{1,0:T(1,128)S(1)} copy-done((s32[1,8]{1,0:T(1,128)S(1)}, s32[1,8]{1,0:T(1,128)}, u32[]{:S(2)}) %copy-start.8) | copy-done | bytes 56
  10.2 0.0 copy-start.1
  10.2 1.2 %copy-done.1 = bf16[1,128,4096]{2,1,0:T(8,128)(2,1)S(1)} copy-done((bf16[1,128,4096]{2,1,0:T(8,128)(2,1)S(1)}, bf16[1,128,4096]{2,1,0:T(8,128)(2,1)}, u32[]{:S(2)}) %copy-start.1) | copy-done | bytes 1048600
  11.4 0.0 copy-start.4
  11.4 0.9 %copy-done.4 = bf16[1,128,512]{2,1,0:T(8,128)(2,1)S(1)} copy-done((bf16[1,128,512]{2,1,0:T(8,128)(2,1)S(1)}, bf16[1,128,512]{2,1,0:T(8,128)(2,1)}, u32[]{:S(2)}) %copy-start.4) | copy-done | bytes 131096
  12.3 0.0 copy-start.6
  12.3 0.9 %copy-done.6 = bf16[1,128,512]{2,1,0:T(8,128)(2,1)S(1)} copy-done((bf16[1,128,512]{2,1,0:T(8,128)(2,1)S(1)}, bf16[1,128,512]{2,1,0:T(8,128)(2,1)}, u32[]{:S(2)}) %copy-start.6) | copy-done | bytes 131096
  13.2 0.0 copy-start.2
  13.2 0.0 copy-start.5
  13.2 0.0 copy-start.7
  13.2 2.7 %shard_map.78 = bf16[2,256,128]{2,1,0:T(8,128)(2,1)S(1)} custom-call(s32[2]{0:T(128)S(1)} %pad_add_fusion.2.place, s32[1,8]{1,0:T(1,128)S(1)} %copy-done.8, bf16[128,4096]{1,0:T(8,128)(2,1)S(1)} %bitcast.15, bf16[128,4096]{1,0:T(8,128)(2,1)S(1)} %bitcast.17, bf16[128,512]{1,0:T(8,128)(2,1)S(1)} %collective-permute-done.k_prev, ...), custom_call_target="tpu_custom_call" | custom-call | flops 402653184 | bytes 1048576 | tf_op jit(solution)/shard_map/pallas_call | solution.py:80
  15.9 0.1 collective-permute-start.2
  16.0 0.1 pad_add_fusion.1.place
  16.1 0.0 copy-done.2
  16.1 0.0 copy-done.5
  16.1 0.0 copy-done.7
  16.1 2.7 %shard_map.77.mine = bf16[2,256,128]{2,1,0:T(8,128)(2,1)S(1)} custom-call(s32[2]{0:T(128)S(1)} %pad_add_fusion.1.place, s32[1,8]{1,0:T(1,128)S(1)} %copy-done.8, bf16[128,4096]{1,0:T(8,128)(2,1)S(1)} %bitcast.16, bf16[128,4096]{1,0:T(8,128)(2,1)S(1)} %bitcast.18, bf16[128,512]{1,0:T(8,128)(2,1)S(1)} %collective-permute-done.k_prev, ...), custom_call_target="tpu_custom_call" | custom-call | flops 402653184 | bytes 1048576 | tf_op jit(solution)/shard_map/pallas_call | solution.py:80
  18.8 0.0 collective-permute-done.2.theirs
  18.9 0.6 shard_map.79.refs_0_
  19.4 0.0 collective-permute-done.6.refs_5_
  19.5 0.0 collective-permute-done.7.refs_6_
  19.5 1.6 %collective-permute-done.8.refs_7_ = bf16[4,128,256]{2,1,0:T(8,128)(2,1)S(1)} collective-permute-done((bf16[4,128,256]{2,1,0:T(8,128)(2,1)S(1)}, bf16[4,128,256]{2,1,0:T(8,128)(2,1)S(1)}, u32[]{:S(2)}, u32[]{:S(2)}) %collective-permute-start.8) | collective-permute-done | bytes 262176 | tf_op jit(solution)/shard_map/ppermute | solution.py:266
  21.0 0.1 pad_maximum_fusion
  21.2 0.1 collective-permute-start.9
  21.2 1.6 %collective-permute-start.3 = (bf16[384,256]{1,0:T(8,128)(2,1)S(1)}, bf16[384,256]{1,0:T(8,128)(2,1)S(1)}, u32[]{:S(2)}, u32[]{:S(2)}) collective-permute-start(bf16[384,256]{1,0:T(8,128)(2,1)S(1)} %shard_map.79.refs_0_), channel_id=1, source_target_pairs={{0,1},{1,0},{2,3},{3,2},{4,5},{5,4},{6,7},{7,6},{8,9},{9,8},{10,11... | collective-permute-start | bytes 589832 | tf_op jit(solution)/shard_map/ppermute | solution.py:266
  22.8 0.5 collective-permute-start.4
  23.4 1.4 %collective-permute-start.5 = (bf16[384,256]{1,0:T(8,128)(2,1)S(1)}, bf16[384,256]{1,0:T(8,128)(2,1)S(1)}, u32[]{:S(2)}, u32[]{:S(2)}) collective-permute-start(bf16[384,256]{1,0:T(8,128)(2,1)S(1)} %shard_map.79.refs_0_), channel_id=1, source_target_pairs={{0,17},{1,16},{2,19},{3,18},{4,21},{5,20},{6,23},{7,22},{8,25},{9,... | collective-permute-start | bytes 589832 | tf_op jit(solution)/shard_map/ppermute | solution.py:266
  24.8 3.8 %collective-permute-done.3.refs_1_ = bf16[384,256]{1,0:T(8,128)(2,1)S(1)} collective-permute-done((bf16[384,256]{1,0:T(8,128)(2,1)S(1)}, bf16[384,256]{1,0:T(8,128)(2,1)S(1)}, u32[]{:S(2)}, u32[]{:S(2)}) %collective-permute-start.3) | collective-permute-done | bytes 196640 | tf_op jit(solution)/shard_map/ppermute | solution.py:266
  28.6 2.0 %collective-permute-done.4.refs_2_ = bf16[384,256]{1,0:T(8,128)(2,1)S(1)} collective-permute-done((bf16[384,256]{1,0:T(8,128)(2,1)S(1)}, bf16[384,256]{1,0:T(8,128)(2,1)S(1)}, u32[]{:S(2)}, u32[]{:S(2)}) %collective-permute-start.4) | collective-permute-done | bytes 196640 | tf_op jit(solution)/shard_map/ppermute | solution.py:266
  30.6 3.4 %collective-permute-done.5.refs_3_ = bf16[384,256]{1,0:T(8,128)(2,1)S(1)} collective-permute-done((bf16[384,256]{1,0:T(8,128)(2,1)S(1)}, bf16[384,256]{1,0:T(8,128)(2,1)S(1)}, u32[]{:S(2)}, u32[]{:S(2)}) %collective-permute-start.5) | collective-permute-done | bytes 196640 | tf_op jit(solution)/shard_map/ppermute | solution.py:266
  33.9 0.0 collective-permute-done.9.refs_8_
  34.0 1.3 %shard_map.81 = (bf16[256,256]{1,0:T(8,128)(2,1)S(1)}, bf16[256,256]{1,0:T(8,128)(2,1)S(1)}, bf16[256,256]{1,0:T(8,128)(2,1)S(1)}, f32[256,256]{1,0:T(8,128)S(1)...) custom-call(s32[3]{0:T(128)S(1)} %pad_add_fusion.place, bf16[384,256]{1,0:T(8,128)(2,1)S(1)} %shard_map.79.refs_0_, ...), custom_call_target="tpu_custom_call" | custom-call | flops 536870912 | bytes 4194304 | tf_op jit(solution)/shard_map/pallas_call | solution.py:191
  35.3 2.7 %collective-permute-start.10 = (bf16[256,256]{1,0:T(8,128)(2,1)S(1)}, bf16[256,256]{1,0:T(8,128)(2,1)S(1)}, u32[]{:S(2)}, u32[]{:S(2)}) collective-permute-start(bf16[256,256]{1,0:T(8,128)(2,1)S(1)} %get-tuple-element.28), channel_id=1, source_target_pairs={{0,4},{1,5},{2,6},{3,7},{4,0},{5,1},{6,2},{7,3},{8,12},{9,13},{10,... | collective-permute-start | bytes 393224 | tf_op jit(solution)/shard_map/ppermute | solution.py:266
  37.9 1.3 %collective-permute-start.11 = (bf16[256,256]{1,0:T(8,128)(2,1)S(1)}, bf16[256,256]{1,0:T(8,128)(2,1)S(1)}, u32[]{:S(2)}, u32[]{:S(2)}) collective-permute-start(bf16[256,256]{1,0:T(8,128)(2,1)S(1)} %get-tuple-element.29), channel_id=1, source_target_pairs={{0,6},{1,7},{2,4},{3,5},{4,2},{5,3},{6,0},{7,1},{8,14},{9,15},{10,... | collective-permute-start | bytes 393224 | tf_op jit(solution)/shard_map/ppermute | solution.py:266
  39.3 0.2 collective-permute-start.12
  39.5 8.3 %collective-permute-done.10.r1 = bf16[256,256]{1,0:T(8,128)(2,1)S(1)} collective-permute-done((bf16[256,256]{1,0:T(8,128)(2,1)S(1)}, bf16[256,256]{1,0:T(8,128)(2,1)S(1)}, u32[]{:S(2)}, u32[]{:S(2)}) %collective-permute-start.10) | collective-permute-done | bytes 131104 | tf_op jit(solution)/shard_map/ppermute | solution.py:266
  47.8 0.0 collective-permute-done.11.r2
  47.8 0.2 collective-permute-done.12.r3
  48.0 1.3 %shard_map.82 = (f32[256,128]{1,0:T(8,128)S(1)}, f32[256,128]{1,0:T(8,128)S(1)}, f32[32,1,128]{2,1,0:T(1,128)}) custom-call(s32[3]{0:T(128)S(1)} %pad_add_fusion.place, f32[256,256]{1,0:T(8,128)S(1)} %get-tuple-element.27.keep, bf16[256,256]{1,0:T(8,128)(2,1)S(1)} %collective-permute-done.10.r1, bf16[256,256]{1,0:T(8,128)(2,1)S(1)} %collective-permute-done.11.r2, ...), custom_call_target="tpu_custom_call" | custom-call | flops 524288 | bytes 917504 | tf_op jit(solution)/shard_map/pallas_call | solution.py:216
  49.3 0.0 collective-permute-start.13
  49.3 0.5 collective-permute-start.14
  49.8 5.3 %all-to-all-start = ((f32[32,1,128]{2,1,0:T(1,128)}), f32[32,1,128]{2,1,0:T(1,128)S(1)}, u32[]{:S(2)}, u32[]{:S(2)}) async-start(f32[32,1,128]{2,1,0:T(1,128)} %get-tuple-element.31), calls=%async_computation | async-start | bytes 32768 | tf_op jit(solution)/shard_map/all_to_all | solution.py:293
  55.1 0.0 collective-permute-done.14.key_theirs
  55.1 7.0 %all-to-all-done.squares = f32[32,1,128]{2,1,0:T(1,128)S(1)} async-done(((f32[32,1,128]{2,1,0:T(1,128)}), f32[32,1,128]{2,1,0:T(1,128)S(1)}, u32[]{:S(2)}, u32[]{:S(2)}) %all-to-all-start) | async-done | bytes 16416 | tf_op jit(solution)/shard_map/all_to_all | solution.py:293
  62.2 0.0 collective-permute-done.13.theirs
  62.2 1.5 %shard_map.83 = (bf16[1,128,512]{2,1,0:T(8,128)(2,1)}, f32[128,512]{1,0:T(8,128)}) custom-call(s32[3]{0:T(128)S(1)} %pad_add_fusion.place, f32[32,1,128]{2,1,0:T(1,128)S(1)} %all-to-all-done.squares, f32[256,128]{1,0:T(8,128)S(1)} %get-tuple-element.32.mine, f32[256,128]{1,0:T(8,128)S(1)} %collective-permute-done.13.theirs, ...), custom_call_target="tpu_custom_call" | custom-call | flops 262144 | bytes 1048576 | tf_op jit(solution)/shard_map/pallas_call | solution.py:243
Async XLA Ops:
  0.6 8.9 %copy-start = (bf16[1,128,4096]{2,1,0:T(8,128)(2,1)S(1)}, bf16[1,128,4096]{2,1,0:T(8,128)(2,1)}, u32[]{:S(2)}) copy-start(bf16[1,128,4096]{2,1,0:T(8,128)(2,1)} %param.6) | copy-start | bytes 3145732
  0.6 8.9 %collective-permute-start = (bf16[128,512]{1,0:T(8,128)(2,1)}, bf16[128,512]{1,0:T(8,128)(2,1)S(1)}, u32[]{:S(2)}, u32[]{:S(2)}) collective-permute-start(bf16[128,512]{1,0:T(8,128)(2,1)} %bitcast.24), channel_id=1, source_target_pairs={{0,8},{8,16},{16,24},{24,0},{1,9},{9,17},{17,25},{25,1},{2,10},{10... | collective-permute-start | bytes 393224 | tf_op jit(solution)/shard_map/ppermute | solution.py:271
  1.1 8.4 %collective-permute-start.1 = (bf16[128,512]{1,0:T(8,128)(2,1)}, bf16[128,512]{1,0:T(8,128)(2,1)S(1)}, u32[]{:S(2)}, u32[]{:S(2)}) collective-permute-start(bf16[128,512]{1,0:T(8,128)(2,1)} %bitcast.27), channel_id=1, source_target_pairs={{0,8},{8,16},{16,24},{24,0},{1,9},{9,17},{17,25},{25,1},{2,10},{10... | collective-permute-start | bytes 393224 | tf_op jit(solution)/shard_map/ppermute | solution.py:272
  3.8 1.2 %copy-start.3 = (bf16[1,128,4096]{2,1,0:T(8,128)(2,1)S(1)}, bf16[1,128,4096]{2,1,0:T(8,128)(2,1)}, u32[]{:S(2)}) copy-start(bf16[1,128,4096]{2,1,0:T(8,128)(2,1)} %param.10) | copy-start | bytes 3145732
  5.9 13.6 %collective-permute-start.6 = (bf16[4,128,256]{2,1,0:T(8,128)(2,1)S(1)}, bf16[4,128,256]{2,1,0:T(8,128)(2,1)S(1)}, u32[]{:S(2)}, u32[]{:S(2)}) collective-permute-start(bf16[4,128,256]{2,1,0:T(8,128)(2,1)S(1)} %get-tuple-element.20), channel_id=1, source_target_pairs={{0,1},{1,0},{2,3},{3,2},{4,5},{5,4},{6,7},{7,6},{8,9},{9,8},{10,11... | collective-permute-start | bytes 786440 | tf_op jit(solution)/shard_map/ppermute | solution.py:266
  7.5 12.0 %collective-permute-start.7 = (bf16[4,128,256]{2,1,0:T(8,128)(2,1)S(1)}, bf16[4,128,256]{2,1,0:T(8,128)(2,1)S(1)}, u32[]{:S(2)}, u32[]{:S(2)}) collective-permute-start(bf16[4,128,256]{2,1,0:T(8,128)(2,1)S(1)} %get-tuple-element.21), channel_id=1, source_target_pairs={{0,16},{1,17},{2,18},{3,19},{4,20},{5,21},{6,22},{7,23},{8,24},{9,... | collective-permute-start | bytes 786440 | tf_op jit(solution)/shard_map/ppermute | solution.py:266
  8.0 13.0 %collective-permute-start.8 = (bf16[4,128,256]{2,1,0:T(8,128)(2,1)S(1)}, bf16[4,128,256]{2,1,0:T(8,128)(2,1)S(1)}, u32[]{:S(2)}, u32[]{:S(2)}) collective-permute-start(bf16[4,128,256]{2,1,0:T(8,128)(2,1)S(1)} %get-tuple-element.22), channel_id=1, source_target_pairs={{0,17},{1,16},{2,19},{3,18},{4,21},{5,20},{6,23},{7,22},{8,25},{9,... | collective-permute-start | bytes 786440 | tf_op jit(solution)/shard_map/ppermute | solution.py:266
  9.5 0.7 %copy-start.8 = (s32[1,8]{1,0:T(1,128)S(1)}, s32[1,8]{1,0:T(1,128)}, u32[]{:S(2)}) copy-start(s32[1,8]{1,0:T(1,128)} %lengths.3) | copy-start | bytes 100
  10.2 1.2 %copy-start.1 = (bf16[1,128,4096]{2,1,0:T(8,128)(2,1)S(1)}, bf16[1,128,4096]{2,1,0:T(8,128)(2,1)}, u32[]{:S(2)}) copy-start(bf16[1,128,4096]{2,1,0:T(8,128)(2,1)} %param.9) | copy-start | bytes 3145732
  11.4 0.9 %copy-start.4 = (bf16[1,128,512]{2,1,0:T(8,128)(2,1)S(1)}, bf16[1,128,512]{2,1,0:T(8,128)(2,1)}, u32[]{:S(2)}) copy-start(bf16[1,128,512]{2,1,0:T(8,128)(2,1)} %param.7) | copy-start | bytes 393220
  12.3 0.9 %copy-start.6 = (bf16[1,128,512]{2,1,0:T(8,128)(2,1)S(1)}, bf16[1,128,512]{2,1,0:T(8,128)(2,1)}, u32[]{:S(2)}) copy-start(bf16[1,128,512]{2,1,0:T(8,128)(2,1)} %param.8) | copy-start | bytes 393220
  13.2 2.9 %copy-start.2 = (bf16[1,128,4096]{2,1,0:T(8,128)(2,1)S(1)}, bf16[1,128,4096]{2,1,0:T(8,128)(2,1)}, u32[]{:S(2)}) copy-start(bf16[1,128,4096]{2,1,0:T(8,128)(2,1)} %param.9) | copy-start | bytes 3145732
  13.2 2.9 %copy-start.5 = (bf16[1,128,512]{2,1,0:T(8,128)(2,1)S(1)}, bf16[1,128,512]{2,1,0:T(8,128)(2,1)}, u32[]{:S(2)}) copy-start(bf16[1,128,512]{2,1,0:T(8,128)(2,1)} %param.7) | copy-start | bytes 393220
  13.2 2.9 %copy-start.7 = (bf16[1,128,512]{2,1,0:T(8,128)(2,1)S(1)}, bf16[1,128,512]{2,1,0:T(8,128)(2,1)}, u32[]{:S(2)}) copy-start(bf16[1,128,512]{2,1,0:T(8,128)(2,1)} %param.8) | copy-start | bytes 393220
  15.9 2.9 %collective-permute-start.2 = (bf16[2,256,128]{2,1,0:T(8,128)(2,1)S(1)}, bf16[2,256,128]{2,1,0:T(8,128)(2,1)S(1)}, u32[]{:S(2)}, u32[]{:S(2)}) collective-permute-start(bf16[2,256,128]{2,1,0:T(8,128)(2,1)S(1)} %shard_map.78), channel_id=1, source_target_pairs={{0,8},{1,9},{2,10},{3,11},{4,12},{5,13},{6,14},{7,15},{8,0},{9,1},... | collective-permute-start | bytes 393224 | tf_op jit(solution)/shard_map/ppermute | solution.py:266
  21.2 12.8 %collective-permute-start.9 = (bf16[4,4,128,256]{3,2,1,0:T(8,128)(2,1)S(1)}, bf16[4,4,128,256]{3,2,1,0:T(8,128)(2,1)S(1)}, u32[]{:S(2)}, u32[]{:S(2)}) collective-permute-start(bf16[4,4,128,256]{3,2,1,0:T(8,128)(2,1)S(1)} %pad_maximum_fusion), channel_id=1, source_target_pairs={{0,8},{1,9},{2,10},{3,11},{4,12},{5,13},{6,14},{7,15},{8,0},{9,1},... | collective-permute-start | bytes 3145736 | tf_op jit(solution)/shard_map/ppermute | solution.py:266
  21.2 7.3 %collective-permute-start.3 = (bf16[384,256]{1,0:T(8,128)(2,1)S(1)}, bf16[384,256]{1,0:T(8,128)(2,1)S(1)}, u32[]{:S(2)}, u32[]{:S(2)}) collective-permute-start(bf16[384,256]{1,0:T(8,128)(2,1)S(1)} %shard_map.79.refs_0_), channel_id=1, source_target_pairs={{0,1},{1,0},{2,3},{3,2},{4,5},{5,4},{6,7},{7,6},{8,9},{9,8},{10,11... | collective-permute-start | bytes 589832 | tf_op jit(solution)/shard_map/ppermute | solution.py:266
  22.8 7.7 %collective-permute-start.4 = (bf16[384,256]{1,0:T(8,128)(2,1)S(1)}, bf16[384,256]{1,0:T(8,128)(2,1)S(1)}, u32[]{:S(2)}, u32[]{:S(2)}) collective-permute-start(bf16[384,256]{1,0:T(8,128)(2,1)S(1)} %shard_map.79.refs_0_), channel_id=1, source_target_pairs={{0,16},{1,17},{2,18},{3,19},{4,20},{5,21},{6,22},{7,23},{8,24},{9,... | collective-permute-start | bytes 589832 | tf_op jit(solution)/shard_map/ppermute | solution.py:266
  23.4 10.6 %collective-permute-start.5 = (bf16[384,256]{1,0:T(8,128)(2,1)S(1)}, bf16[384,256]{1,0:T(8,128)(2,1)S(1)}, u32[]{:S(2)}, u32[]{:S(2)}) collective-permute-start(bf16[384,256]{1,0:T(8,128)(2,1)S(1)} %shard_map.79.refs_0_), channel_id=1, source_target_pairs={{0,17},{1,16},{2,19},{3,18},{4,21},{5,20},{6,23},{7,22},{8,25},{9,... | collective-permute-start | bytes 589832 | tf_op jit(solution)/shard_map/ppermute | solution.py:266
  35.3 12.5 %collective-permute-start.10 = (bf16[256,256]{1,0:T(8,128)(2,1)S(1)}, bf16[256,256]{1,0:T(8,128)(2,1)S(1)}, u32[]{:S(2)}, u32[]{:S(2)}) collective-permute-start(bf16[256,256]{1,0:T(8,128)(2,1)S(1)} %get-tuple-element.28), channel_id=1, source_target_pairs={{0,4},{1,5},{2,6},{3,7},{4,0},{5,1},{6,2},{7,3},{8,12},{9,13},{10,... | collective-permute-start | bytes 393224 | tf_op jit(solution)/shard_map/ppermute | solution.py:266
  37.9 9.8 %collective-permute-start.11 = (bf16[256,256]{1,0:T(8,128)(2,1)S(1)}, bf16[256,256]{1,0:T(8,128)(2,1)S(1)}, u32[]{:S(2)}, u32[]{:S(2)}) collective-permute-start(bf16[256,256]{1,0:T(8,128)(2,1)S(1)} %get-tuple-element.29), channel_id=1, source_target_pairs={{0,6},{1,7},{2,4},{3,5},{4,2},{5,3},{6,0},{7,1},{8,14},{9,15},{10,... | collective-permute-start | bytes 393224 | tf_op jit(solution)/shard_map/ppermute | solution.py:266
  39.3 8.7 %collective-permute-start.12 = (bf16[256,256]{1,0:T(8,128)(2,1)S(1)}, bf16[256,256]{1,0:T(8,128)(2,1)S(1)}, u32[]{:S(2)}, u32[]{:S(2)}) collective-permute-start(bf16[256,256]{1,0:T(8,128)(2,1)S(1)} %get-tuple-element.30), channel_id=1, source_target_pairs={{0,2},{1,3},{2,0},{3,1},{4,6},{5,7},{6,4},{7,5},{8,10},{9,11},{10,... | collective-permute-start | bytes 393224 | tf_op jit(solution)/shard_map/ppermute | solution.py:266
  49.3 12.9 %collective-permute-start.13 = (f32[256,128]{1,0:T(8,128)S(1)}, f32[256,128]{1,0:T(8,128)S(1)}, u32[]{:S(2)}, u32[]{:S(2)}) collective-permute-start(f32[256,128]{1,0:T(8,128)S(1)} %get-tuple-element.33), channel_id=1, source_target_pairs={{0,8},{1,9},{2,10},{3,11},{4,12},{5,13},{6,14},{7,15},{8,0},{9,1},... | collective-permute-start | bytes 393224 | tf_op jit(solution)/shard_map/ppermute | solution.py:266
  49.3 5.9 %collective-permute-start.14 = (bf16[128,256]{1,0:T(8,128)(2,1)S(1)}, bf16[128,256]{1,0:T(8,128)(2,1)S(1)}, u32[]{:S(2)}, u32[]{:S(2)}) collective-permute-start(bf16[128,256]{1,0:T(8,128)(2,1)S(1)} %get-tuple-element.35), channel_id=1, source_target_pairs={{0,8},{1,9},{2,10},{3,11},{4,12},{5,13},{6,14},{7,15},{8,0},{9,1},... | collective-permute-start | bytes 196616 | tf_op jit(solution)/shard_map/ppermute | solution.py:266
  49.8 12.4 %all-to-all-start = ((f32[32,1,128]{2,1,0:T(1,128)}), f32[32,1,128]{2,1,0:T(1,128)S(1)}, u32[]{:S(2)}, u32[]{:S(2)}) async-start(f32[32,1,128]{2,1,0:T(1,128)} %get-tuple-element.31), calls=%async_computation | async-start | bytes 32768 | tf_op jit(solution)/shard_map/all_to_all | solution.py:293

commit v3 on v2

v3 whole, which is shorter than its diff:
```python
import functools
import math

import jax
import jax.numpy as jnp
from jax import lax
from jax.experimental import pallas as pl
from jax.experimental.pallas import tpu as pltpu
from jax.sharding import PartitionSpec as P

HD = 128
HQ = 32
KVH = 4
DW = 4096
GROUP = HQ // KVH

NEG_FILL = -1e30
AXES = ("seq", "dp")
F32 = jnp.float32
BF16 = jnp.bfloat16
CORES = 2
HALF = KVH // CORES
WIDE = HALF * HD


def params(mib=40):
    return pltpu.CompilerParams(vmem_limit_bytes=mib << 20)


def cost(flops, moved, exps=0):
    return pl.CostEstimate(flops=flops, bytes_accessed=moved, transcendentals=exps)


def position():
    seq, dp = lax.axis_index("seq"), lax.axis_index("dp")
    return seq & 1, seq >> 1, dp & 1, dp >> 1


def first_head(which):
    if which is None:
        return 0
    core = lax.axis_index("seq") & 1
    return (core if which == 0 else 1 - core) * HALF


def attention_kernel(which, heads, lengths, q, g, k_prev, k_own, v_prev, v_own, out, *scratch):
    ends, q_buf, g_buf, k_buf, v_buf, bias, sems = scratch
    rows = q.shape[0]
    pair = bias.shape[1] // rows
    first = first_head(which)
    waits = [[] for _ in range(heads)]
    length_copy = pltpu.make_async_copy(lengths, ends, sems.at[6 * heads])
    length_copy.start()
    for h in range(heads):
        wide = pl.ds(pl.multiple_of((first + h) * GROUP * HD, GROUP * HD), GROUP * HD)
        one = pl.ds(pl.multiple_of((first + h) * HD, HD), HD)
        moves = [
            (k_prev.at[:, one], k_buf.at[h, :rows]),
            (k_own.at[:, one], k_buf.at[h, rows:]),
            (q.at[:, wide], q_buf.at[h]),
            (v_prev.at[:, one], v_buf.at[h, :rows]),
            (v_own.at[:, one], v_buf.at[h, rows:]),
            (g.at[:, wide], g_buf.at[h]),
        ]
        for n, (source, target) in enumerate(moves):
            copy = pltpu.make_async_copy(source, target, sems.at[6 * h + n])
            copy.start()
            waits[h].append(copy)
    length_copy.wait()
    base = lax.axis_index("seq") * rows
    query_pos = base + lax.broadcasted_iota(jnp.int32, (1, rows), 1)
    start = jnp.zeros((1, rows), jnp.int32)
    end = jnp.int32(0)
    for d in range(ends.shape[1]):
        end = end + ends[0, d]
        start = jnp.where(end <= query_pos, end, start)
    key_pos = base - rows + lax.broadcasted_iota(jnp.int32, (2 * rows, rows), 0)
    visible = (key_pos >= start) & (key_pos <= query_pos)
    hidden = jnp.where(visible, 0.0, NEG_FILL).astype(F32)
    for n in range(pair):
        bias[:, n * rows : (n + 1) * rows] = hidden

    scale = 1.0 / math.sqrt(HD)
    scale2 = scale * math.log2(math.e)
    nt = (((1,), (1,)), ((), ()))
    nn = (((1,), (0,)), ((), ()))
    for r in range(heads):
        for copy in waits[r]:
            copy.wait()
        key, value = k_buf[r], v_buf[r]
        total = None
        for h in range(0, GROUP, pair):
            cols = [slice((h + n) * HD, (h + n + 1) * HD) for n in range(pair)]
            q_rows = jnp.concatenate([q_buf[r, :, c] for c in cols], axis=0)
            g_rows = jnp.concatenate([g_buf[r, :, c] for c in cols], axis=0)
            scores = lax.dot_general(key, q_rows, nt, preferred_element_type=F32)
            weights = lax.dot_general(value, g_rows, nt, preferred_element_type=F32)
            scores = scores * scale2 + bias[...]
            exponent = jnp.exp2(scores - jnp.max(scores, axis=0, keepdims=True))
            inverse = 1.0 / jnp.sum(exponent, axis=0, keepdims=True)
            delta = jnp.sum(exponent * weights, axis=0, keepdims=True) * inverse
            grads = ((exponent * (inverse * scale)) * (weights - delta)).astype(BF16)
            part = lax.dot_general(grads, q_rows, nn, preferred_element_type=F32)
            total = part if total is None else total + part
        out[r] = total.astype(out.dtype)


def attention(which, lengths, q, g, k_prev, k_own, v_prev, v_own, heads, dtype):
    rows = q.shape[0]
    size = heads * 2 * rows * GROUP * rows
    return pl.pallas_call(
        functools.partial(attention_kernel, which, heads),
        in_specs=[pl.BlockSpec(memory_space=pl.ANY)] * 7,
        out_specs=pl.BlockSpec(memory_space=pltpu.VMEM),
        out_shape=jax.ShapeDtypeStruct((heads, 2 * rows, HD), dtype),
        scratch_shapes=[
            pltpu.SMEM(lengths.shape, jnp.int32),
            pltpu.VMEM((heads, rows, GROUP * HD), BF16),
            pltpu.VMEM((heads, rows, GROUP * HD), BF16),
            pltpu.VMEM((heads, 2 * rows, HD), BF16),
            pltpu.VMEM((heads, 2 * rows, HD), BF16),
            pltpu.VMEM((2 * rows, 4 * rows), F32),
            pltpu.SemaphoreType.DMA((6 * heads + 1,)),
        ],
        compiler_params=params(54),
        cost_estimate=cost(6 * size * HD, heads * rows * GROUP * HD * 4, size),
    )(lengths, q, g, k_prev, k_own, v_prev, v_own)


def pack_kernel(sizes, x_ref, *outs):
    ny, nz = sizes
    block = outs[0].shape[2] // CORES
    core, x, y, z_own = position()
    for m, out in enumerate(outs):
        for z in range(nz):
            for c in range(CORES):
                source = (((x ^ (m // ny)) * CORES + c) * nz + z) * ny + (y ^ (m % ny))
                at = pl.ds(pl.multiple_of(source * block, block), block)
                out[z, :, c * block : (c + 1) * block] = x_ref[:, at]


def pack(features, sizes):
    nx, ny, nz = sizes
    rows = features.shape[0]
    shape = jax.ShapeDtypeStruct((nz, rows, DW // (nx * ny * nz)), BF16)
    vmem = pl.BlockSpec(memory_space=pltpu.VMEM)
    return pl.pallas_call(
        functools.partial(pack_kernel, (ny, nz)),
        in_specs=[vmem],
        out_specs=[vmem] * (nx * ny),
        out_shape=[shape] * (nx * ny),
        compiler_params=params(),
        cost_estimate=cost(0, 64 << 20),
    )(features)


def merge_kernel(mine, theirs, out):
    rows = mine.shape[1] // 2
    core = position()[0]

    def write(even, odd):
        for h in range(HALF):
            cols = slice(h * HD, (h + 1) * HD)
            out[:rows, cols] = even[h, :rows]
            out[rows : 2 * rows, cols] = (
                even[h, rows:].astype(F32) + odd[h, :rows].astype(F32)
            ).astype(BF16)
            out[2 * rows :, cols] = odd[h, rows:]

    @pl.when(core == 0)
    def _():
        write(mine, theirs)

    @pl.when(core == 1)
    def _():
        write(theirs, mine)


def merge(mine, theirs):
    rows = mine.shape[1] // 2
    vmem = pl.BlockSpec(memory_space=pltpu.VMEM)
    return pl.pallas_call(
        merge_kernel,
        in_specs=[vmem, vmem],
        out_specs=vmem,
        out_shape=jax.ShapeDtypeStruct((3 * rows, WIDE), BF16),
        compiler_params=params(),
        cost_estimate=cost(rows * WIDE, 7 * rows * WIDE * 2),
    )(mine, theirs)


def weight_kernel(nz, *refs):
    chips, f_same, f_other = refs[:4], refs[4:8], refs[8:12]
    sends, (keep, key_mine, key_theirs, same, other) = refs[12 : 11 + nz], refs[11 + nz :]
    rows = chips[0].shape[0] // 3
    core, x, y, z = position()
    for m in range(4):
        even = chips[m][rows : 2 * rows]
        odd = (chips[m][2 * rows :].astype(F32) + chips[m ^ 2][:rows].astype(F32)).astype(BF16)
        own = jnp.where(core == 0, even, odd)
        far = jnp.where(core == 0, odd, even)
        same[m * rows : (m + 1) * rows] = own
        other[m * rows : (m + 1) * rows] = far
        if m == 0:
            key_mine[...] = own
            key_theirs[...] = far
    tn = (((0,), (0,)), ((), ()))
    for m in (2, 3, 1, 0):
        left = jnp.concatenate([f[z ^ m] for f in f_same], axis=0)
        right = jnp.concatenate([f[z ^ m] for f in f_other], axis=0)
        product = lax.dot_general(same[...], left, tn, preferred_element_type=F32)
        product += lax.dot_general(other[...], right, tn, preferred_element_type=F32)
        if m == 0:
            keep[...] = product
        else:
            sends[m - 1][...] = product.astype(BF16)


def weight(chips, f_same, f_other):
    rows = chips[0].shape[0] // 3
    nz = f_same[0].shape[0]
    vmem = pl.BlockSpec(memory_space=pltpu.VMEM)
    square = (WIDE, f_same[0].shape[2])
    shapes = [jax.ShapeDtypeStruct(square, BF16)] * (nz - 1)
    shapes += [jax.ShapeDtypeStruct(square, F32)] + [jax.ShapeDtypeStruct((rows, WIDE), BF16)] * 2
    return pl.pallas_call(
        functools.partial(weight_kernel, nz),
        in_specs=[vmem] * 12,
        out_specs=[vmem] * len(shapes),
        out_shape=shapes,
        scratch_shapes=[pltpu.VMEM((4 * rows, WIDE), BF16)] * 2,
        compiler_params=params(),
        cost_estimate=cost(2 * 8 * rows * WIDE * 4 * WIDE, 4 << 20),
    )(*chips, *f_same, *f_other)


def reduce_kernel(keep, r1, r2, r3, mine, theirs, squares):
    total = keep[...] + r1[...].astype(F32) + r2[...].astype(F32) + r3[...].astype(F32)
    half = total.shape[1] // 2
    core = position()[0]
    low, high = total[:, :half], total[:, half:]
    mine[...] = jnp.where(core == 0, low, high)
    theirs[...] = jnp.where(core == 0, high, low)
    sums = jnp.sum(low * low + high * high, axis=0, keepdims=True)
    squares[...] = jnp.broadcast_to(sums[None], squares.shape)


def reduce_planes(keep, received, devices):
    cols, both = keep.shape
    vmem = pl.BlockSpec(memory_space=pltpu.VMEM)
    half = jax.ShapeDtypeStruct((cols, both // 2), F32)
    return pl.pallas_call(
        reduce_kernel,
        in_specs=[vmem] * 4,
        out_specs=[vmem] * 3,
        out_shape=[half, half, jax.ShapeDtypeStruct((devices, 1, both // 2), F32)],
        compiler_params=params(),
        cost_estimate=cost(8 * cols * both, cols * both * 14),
    )(keep, *received)


def finish_kernel(squares, mine, theirs, key_mine, key_theirs, key_out, out):
    entries = DW * KVH * HD
    total = jnp.sum(jnp.sum(squares[...], axis=0, keepdims=True), axis=2, keepdims=True)
    root_mean = jnp.sqrt(total / entries + 1e-06)
    factor = jnp.minimum(1.0, 1.0 / root_mean)[0]
    first = position()[0] == 0
    low = (mine[...] * factor).T
    high = (theirs[...] * factor).T
    out[:, :WIDE] = jnp.where(first, low, high)
    out[:, WIDE:] = jnp.where(first, high, low)
    key_out[0, :, :WIDE] = jnp.where(first, key_mine[...], key_theirs[...])
    key_out[0, :, WIDE:] = jnp.where(first, key_theirs[...], key_mine[...])


def finish(squares, mine, theirs, key_mine, key_theirs):
    rows = key_mine.shape[0]
    vmem = pl.BlockSpec(memory_space=pltpu.VMEM)
    return pl.pallas_call(
        finish_kernel,
        in_specs=[vmem] * 5,
        out_specs=[vmem] * 2,
        out_shape=[
            jax.ShapeDtypeStruct((1, rows, KVH * HD), BF16),
            jax.ShapeDtypeStruct((mine.shape[1], KVH * HD), F32),
        ],
        compiler_params=params(),
        cost_estimate=cost(4 * rows * KVH * HD, 4 * rows * KVH * HD * 4),
    )(squares, mine, theirs, key_mine, key_theirs)


def planes(queries, keys, values, grad_out, features, doc_lengths):
    seq_count, dp_count = lax.axis_size("seq"), lax.axis_size("dp")
    devices = seq_count * dp_count
    nx, ny = seq_count // CORES, 2
    nz = dp_count // ny

    def swap(array, mask):
        return lax.ppermute(array, AXES, [(i, i ^ mask) for i in range(devices)])

    core_mask, x_mask, y_mask, z_mask = dp_count, CORES * dp_count, 1, ny
    following = [(i, (i + 1) % seq_count) for i in range(seq_count)]
    k_own, v_own = keys[0], values[0]
    k_prev = lax.ppermute(k_own, "seq", following)
    v_prev = lax.ppermute(v_own, "seq", following)

    masks = [0, y_mask, x_mask, x_mask + y_mask]
    packed = pack(features[0], (nx, ny, nz))
    f_same = [packed[0]] + [swap(part, mask) for part, mask in zip(packed[1:], masks[1:])]

    near = (queries[0], grad_out[0], k_prev, k_own, v_prev, v_own)
    to_send = attention(1, doc_lengths, *near, HALF, BF16)
    theirs = swap(to_send, core_mask)
    mine = attention(0, doc_lengths, *near, HALF, BF16)
    chip = merge(mine, theirs)
    chips = [chip] + [swap(chip, mask) for mask in masks[1:]]
    f_own, _ = lax.optimization_barrier((f_same[0], to_send))
    f_own = swap(f_own, core_mask)
    f_ready, _ = lax.optimization_barrier((f_same[1:], chip))
    f_other = [f_own] + [swap(part, core_mask) for part in f_ready]

    *sends, keep, key_mine, key_send = weight(chips, f_same, f_other)
    received = [swap(sends[m], (m + 1) * z_mask) for m in (1, 2, 0)]
    key_other = swap(key_send, core_mask)
    rows_mine, rows_send, squares = reduce_planes(keep, received, devices)
    rows_other = swap(rows_send, core_mask)
    squares = lax.all_to_all(squares, AXES, 0, 0, tiled=True)
    return finish(squares, rows_mine, rows_other, key_mine, key_other)


def rings(queries, keys, values, grad_out, features, doc_lengths):
    seq_count = lax.axis_size("seq")
    rows = queries.shape[1]
    following = [(i, (i + 1) % seq_count) for i in range(seq_count)]
    preceding = [(i, (i - 1) % seq_count) for i in range(seq_count)]
    k_own, v_own = keys[0], values[0]
    k_prev = lax.ppermute(k_own, "seq", following)
    v_prev = lax.ppermute(v_own, "seq", following)
    near = (queries[0], grad_out[0], k_prev, k_own, v_prev, v_own)
    parts = attention(None, doc_lengths, *near, KVH, F32)
    parts = parts.transpose(1, 0, 2).reshape(2 * rows, KVH * HD)
    after = lax.ppermute(parts[:rows], "seq", preceding)
    key_grad = (parts[rows:] + after).astype(BF16)
    columns = lax.all_to_all(features[0], "seq", split_axis=1, concat_axis=0, tiled=True)
    weight_part = lax.dot_general(
        columns,
        lax.all_gather(key_grad, "seq", axis=0, tiled=True),
        (((0,), (0,)), ((), ())),
        preferred_element_type=F32,
    )
    own_rows = lax.psum_scatter(weight_part, "dp", scatter_dimension=0, tiled=True)
    squares = lax.psum(jnp.sum(own_rows * own_rows), AXES)
    root_mean = jnp.sqrt(squares / (DW * KVH * HD) + 1e-06)
    return (key_grad[None], own_rows * jnp.minimum(1.0, 1.0 / root_mean))


def solution(mesh):
    in_specs = (
        P("dp", "seq", None),
        P("dp", "seq", None),
        P("dp", "seq", None),
        P("dp", "seq", None),
        P("dp", "seq", None),
        P("dp", None),
    )
    out_specs = (P("dp", "seq", None), P(("seq", "dp"), None))
    small = mesh.shape["seq"] == 2 * CORES and mesh.shape["dp"] == 8
    body = planes if small else rings
    return jax.shard_map(body, mesh=mesh, in_specs=in_specs, out_specs=out_specs, check_vma=False)
```

time: 63.9 us -> 59.4 us (0.930)
  waiting for transfers between devices: 26.2 us -> 23.3 us
  local copies, waits for them, and re-layouts: 4.92 us -> 2.81 us
  starting transfers between devices: 20.4 us -> 22.1 us
  Pallas kernels: 11 us -> 10.3 us
    ppermute x13 -> x16, waiting for transfers between devices: 19.2 us -> 16.2 us  [swap(): return lax.ppermute(array, AXES, [(i, i ^ mask) for i in range(devices)])]
    ppermute x13 -> x16, starting transfers between devices: 12 us -> 14.2 us  [swap(): return lax.ppermute(array, AXES, [(i, i ^ mask) for i in range(devices)])]
    unnamed x18 -> x8, local copies, waits for them, and re-layouts: 4.92 us -> 2.81 us
    pallas_call x7, Pallas kernels: 11 us -> 10.3 us  [the longest x2 7.51 us: attention(): pl.pallas_call(functools.partial(attention_kernel, which, heads), in_spec...]
  transfers between devices with their start and end apart: 16 -> 19, of which waited for: 7 -> 6; matrix products, arithmetic and copies ran while one was open for 0% -> 0% of each run, Pallas kernels for 11% -> 13%
where the time goes in v3:
time: 59.4 us; the launch traced here: 59.2 us
  waiting for transfers between devices  23.3 us (39%)
  starting transfers between devices  22.1 us (37%)
  Pallas kernels  10.3 us (17%)
  local copies, waits for them, and re-layouts  2.81 us (5%)
  between operations  0.75 us (1%)
    ppermute x16, waiting for transfers between devices, swap(): return lax.ppermute(array, AXES, [(i, i ^ mask) for i in range(devices)])  16.2 us
    ppermute x16, starting transfers between devices, swap(): return lax.ppermute(array, AXES, [(i, i ^ mask) for i in range(devices)])  14.2 us
    pallas_call x2, Pallas kernels, attention(): pl.pallas_call(functools.partial(attention_kernel, which, heads), in_spec...  7.51 us
    all_to_all x1, waiting for transfers between devices, planes(): squares = lax.all_to_all(squares, AXES, 0, 0, tiled=True)  7.03 us
    all_to_all x1, starting transfers between devices, planes(): squares = lax.all_to_all(squares, AXES, 0, 0, tiled=True)  4.77 us
    unnamed x8, local copies, waits for them, and re-layouts  2.81 us
    ppermute x1, starting transfers between devices, planes(): v_prev = lax.ppermute(v_own, 'seq', following)  2.6 us
  transfers between devices with their start and end apart: 19, of which 6 were waited for; matrix products, arithmetic and copies ran while one was open for 0% of the time, Pallas kernels for 13%

profile of v3, /device:TPU:0, one launch (start us, length us, event | category | flops | bytes accessed | tf_op | source)
XLA Modules:
  0.0 59.2 jit_solution(12144365171351927580)
XLA Ops:
  0.6 0.5 collective-permute-start
  1.1 2.6 %collective-permute-start.1 = (bf16[128,512]{1,0:T(8,128)(2,1)}, bf16[128,512]{1,0:T(8,128)(2,1)S(1)}, u32[]{:S(2)}, u32[]{:S(2)}) collective-permute-start(bf16[128,512]{1,0:T(8,128)(2,1)} %bitcast.13), channel_id=1, source_target_pairs={{0,8},{8,16},{16,24},{24,0},{1,9},{9,17},{17,25},{25,1},{2,10},{10... | collective-permute-start | bytes 393224 | tf_op jit(solution)/shard_map/ppermute | solution.py:305
  3.7 0.0 copy-start
  3.7 1.2 %copy-done = bf16[1,128,4096]{2,1,0:T(8,128)(2,1)S(1)} copy-done((bf16[1,128,4096]{2,1,0:T(8,128)(2,1)S(1)}, bf16[1,128,4096]{2,1,0:T(8,128)(2,1)}, u32[]{:S(2)}) %copy-start) | copy-done | bytes 1048600
  5.0 0.3 shard_map.80
  5.2 1.6 %collective-permute-start.6 = (bf16[4,128,256]{2,1,0:T(8,128)(2,1)S(1)}, bf16[4,128,256]{2,1,0:T(8,128)(2,1)S(1)}, u32[]{:S(2)}, u32[]{:S(2)}) collective-permute-start(bf16[4,128,256]{2,1,0:T(8,128)(2,1)S(1)} %get-tuple-element.20), channel_id=1, source_target_pairs={{0,1},{1,0},{2,3},{3,2},{4,5},{5,4},{6,7},{7,6},{8,9},{9,8},{10,11... | collective-permute-start | bytes 786440 | tf_op jit(solution)/shard_map/ppermute | solution.py:299
  6.8 0.5 collective-permute-start.7
  7.4 1.4 %collective-permute-start.8 = (bf16[4,128,256]{2,1,0:T(8,128)(2,1)S(1)}, bf16[4,128,256]{2,1,0:T(8,128)(2,1)S(1)}, u32[]{:S(2)}, u32[]{:S(2)}) collective-permute-start(bf16[4,128,256]{2,1,0:T(8,128)(2,1)S(1)} %get-tuple-element.22), channel_id=1, source_target_pairs={{0,17},{1,16},{2,19},{3,18},{4,21},{5,20},{6,23},{7,22},{8,25},{9,... | collective-permute-start | bytes 786440 | tf_op jit(solution)/shard_map/ppermute | solution.py:299
  8.8 0.0 collective-permute-done.k_prev
  8.8 0.0 copy-start.2
  8.8 0.0 collective-permute-done.1.v_prev
  8.8 0.0 copy-start.3
  8.8 0.6 %copy-done.2 = bf16[128,512]{1,0:T(8,128)(2,1)} copy-done((bf16[128,512]{1,0:T(8,128)(2,1)}, bf16[128,512]{1,0:T(8,128)(2,1)S(1)}, u32[]{:S(2)}) %copy-start.2) | copy-done | bytes 131096
  9.4 0.0 copy-done.3
  9.5 3.8 %shard_map.78 = bf16[2,256,128]{2,1,0:T(8,128)(2,1)} custom-call(s32[1,8]{1,0:T(1,128)} %lengths.3, bf16[128,4096]{1,0:T(8,128)(2,1)} %bitcast.6, bf16[128,4096]{1,0:T(8,128)(2,1)} %bitcast.8, bf16[128,512]{1,0:T(8,128)(2,1)} %copy-done.2, bf16[128,512]{1,0:T(8,128)(2,1)} %bitcast.11, bf16[128,512]{1,0:T(8,128)(2,1)} %copy-done.3, bf16[128,512]{1,0:T(8,128)(2,1)} %bitcast.14), custom_call_target="tpu_custom_call" | custom-call | flops 402653184 | bytes 1048576 | tf_op jit(solution)/shard_map/pallas_call | solution.py:111
  13.3 0.1 collective-permute-start.2
  13.3 0.5 collective-permute-start.9
  13.8 3.8 %shard_map.77.mine = bf16[2,256,128]{2,1,0:T(8,128)(2,1)} custom-call(s32[1,8]{1,0:T(1,128)} %lengths.3, bf16[128,4096]{1,0:T(8,128)(2,1)} %bitcast.7, bf16[128,4096]{1,0:T(8,128)(2,1)} %bitcast.9, bf16[128,512]{1,0:T(8,128)(2,1)} %copy-done.2, bf16[128,512]{1,0:T(8,128)(2,1)} %bitcast.12, bf16[128,512]{1,0:T(8,128)(2,1)} %copy-done.3, bf16[128,512]{1,0:T(8,128)(2,1)} %bitcast.15), custom_call_target="tpu_custom_call" | custom-call | flops 402653184 | bytes 1048576 | tf_op jit(solution)/shard_map/pallas_call | solution.py:111
  17.6 0.0 collective-permute-done.2.theirs
  17.6 0.0 copy-start.1
  17.6 0.9 %copy-done.1 = bf16[2,256,128]{2,1,0:T(8,128)(2,1)S(1)} copy-done((bf16[2,256,128]{2,1,0:T(8,128)(2,1)S(1)}, bf16[2,256,128]{2,1,0:T(8,128)(2,1)}, u32[]{:S(2)}) %copy-start.1) | copy-done | bytes 131096
  18.6 1.9 %collective-permute-start.5 = (bf16[384,256]{1,0:T(8,128)(2,1)S(1)}, bf16[384,256]{1,0:T(8,128)(2,1)S(1)}, u32[]{:S(2)}, u32[]{:S(2)}) collective-permute-start(bf16[384,256]{1,0:T(8,128)(2,1)S(1)} %shard_map.79.refs_0_), channel_id=1, source_target_pairs={{0,17},{1,16},{2,19},{3,18},{4,21},{5,20},{6,23},{7,22},{8,25},{9,... | collective-permute-start | bytes 589832 | tf_op jit(solution)/shard_map/ppermute | solution.py:299
  20.4 0.0 collective-permute-done.6.refs_5_
  20.4 0.0 collective-permute-done.7.refs_6_
  20.5 0.0 collective-permute-done.8.refs_7_
  20.5 0.1 collective-permute-start.10
  20.5 0.5 collective-permute-start.11
  21.0 0.1 collective-permute-start.12
  21.1 0.0 collective-permute-done.9.refs_8_
  21.1 1.3 %collective-permute-start.4 = (bf16[384,256]{1,0:T(8,128)(2,1)S(1)}, bf16[384,256]{1,0:T(8,128)(2,1)S(1)}, u32[]{:S(2)}, u32[]{:S(2)}) collective-permute-start(bf16[384,256]{1,0:T(8,128)(2,1)S(1)} %shard_map.79.refs_0_), channel_id=1, source_target_pairs={{0,16},{1,17},{2,18},{3,19},{4,20},{5,21},{6,22},{7,23},{8,24},{9,... | collective-permute-start | bytes 589832 | tf_op jit(solution)/shard_map/ppermute | solution.py:299
  22.4 4.9 %collective-permute-done.5.refs_3_ = bf16[384,256]{1,0:T(8,128)(2,1)S(1)} collective-permute-done((bf16[384,256]{1,0:T(8,128)(2,1)S(1)}, bf16[384,256]{1,0:T(8,128)(2,1)S(1)}, u32[]{:S(2)}, u32[]{:S(2)}) %collective-permute-start.5) | collective-permute-done | bytes 196640 | tf_op jit(solution)/shard_map/ppermute | solution.py:299
  27.3 1.5 %collective-permute-start.3 = (bf16[384,256]{1,0:T(8,128)(2,1)S(1)}, bf16[384,256]{1,0:T(8,128)(2,1)S(1)}, u32[]{:S(2)}, u32[]{:S(2)}) collective-permute-start(bf16[384,256]{1,0:T(8,128)(2,1)S(1)} %shard_map.79.refs_0_), channel_id=1, source_target_pairs={{0,1},{1,0},{2,3},{3,2},{4,5},{5,4},{6,7},{7,6},{8,9},{9,8},{10,11... | collective-permute-start | bytes 589832 | tf_op jit(solution)/shard_map/ppermute | solution.py:299
  28.8 1.9 %collective-permute-done.4.refs_2_ = bf16[384,256]{1,0:T(8,128)(2,1)S(1)} collective-permute-done((bf16[384,256]{1,0:T(8,128)(2,1)S(1)}, bf16[384,256]{1,0:T(8,128)(2,1)S(1)}, u32[]{:S(2)}, u32[]{:S(2)}) %collective-permute-start.4) | collective-permute-done | bytes 196640 | tf_op jit(solution)/shard_map/ppermute | solution.py:299
  30.7 2.3 %collective-permute-done.3.refs_1_ = bf16[384,256]{1,0:T(8,128)(2,1)S(1)} collective-permute-done((bf16[384,256]{1,0:T(8,128)(2,1)S(1)}, bf16[384,256]{1,0:T(8,128)(2,1)S(1)}, u32[]{:S(2)}, u32[]{:S(2)}) %collective-permute-start.3) | collective-permute-done | bytes 196640 | tf_op jit(solution)/shard_map/ppermute | solution.py:299
  32.9 0.0 collective-permute-done.10.refs_9_
  32.9 0.0 collective-permute-done.11.refs_10_
  32.9 0.0 collective-permute-done.12.refs_11_
  33.0 0.8 %shard_map.81 = (bf16[256,256]{1,0:T(8,128)(2,1)S(1)}, bf16[256,256]{1,0:T(8,128)(2,1)S(1)}, bf16[256,256]{1,0:T(8,128)(2,1)S(1)}, f32[256,256]{1,0:T(8,128)S(1)...) custom-call(bf16[384,256]{1,0:T(8,128)(2,1)S(1)} %shard_map.79.refs_0_, ...), custom_call_target="tpu_custom_call" | custom-call | flops 536870912 | bytes 4194304 | tf_op jit(solution)/shard_map/pallas_call | solution.py:226
  33.7 2.7 %collective-permute-start.13 = (bf16[256,256]{1,0:T(8,128)(2,1)S(1)}, bf16[256,256]{1,0:T(8,128)(2,1)S(1)}, u32[]{:S(2)}, u32[]{:S(2)}) collective-permute-start(bf16[256,256]{1,0:T(8,128)(2,1)S(1)} %get-tuple-element.28), channel_id=1, source_target_pairs={{0,4},{1,5},{2,6},{3,7},{4,0},{5,1},{6,2},{7,3},{8,12},{9,13},{10,... | collective-permute-start | bytes 393224 | tf_op jit(solution)/shard_map/ppermute | solution.py:299
  36.4 1.3 %collective-permute-start.14 = (bf16[256,256]{1,0:T(8,128)(2,1)S(1)}, bf16[256,256]{1,0:T(8,128)(2,1)S(1)}, u32[]{:S(2)}, u32[]{:S(2)}) collective-permute-start(bf16[256,256]{1,0:T(8,128)(2,1)S(1)} %get-tuple-element.29), channel_id=1, source_target_pairs={{0,6},{1,7},{2,4},{3,5},{4,2},{5,3},{6,0},{7,1},{8,14},{9,15},{10,... | collective-permute-start | bytes 393224 | tf_op jit(solution)/shard_map/ppermute | solution.py:299
  37.7 0.2 collective-permute-start.15
  38.0 6.7 %collective-permute-done.13.r1 = bf16[256,256]{1,0:T(8,128)(2,1)S(1)} collective-permute-done((bf16[256,256]{1,0:T(8,128)(2,1)S(1)}, bf16[256,256]{1,0:T(8,128)(2,1)S(1)}, u32[]{:S(2)}, u32[]{:S(2)}) %collective-permute-start.13) | collective-permute-done | bytes 131104 | tf_op jit(solution)/shard_map/ppermute | solution.py:299
  44.7 0.0 collective-permute-done.14.r2
  44.7 0.5 collective-permute-done.15.r3
  45.2 0.7 %shard_map.82 = (f32[256,128]{1,0:T(8,128)S(1)}, f32[256,128]{1,0:T(8,128)S(1)}, f32[32,1,128]{2,1,0:T(1,128)}) custom-call(f32[256,256]{1,0:T(8,128)S(1)} %get-tuple-element.27.keep, bf16[256,256]{1,0:T(8,128)(2,1)S(1)} %collective-permute-done.13.r1, bf16[256,256]{1,0:T(8,128)(2,1)S(1)} %collective-permute-done.14.r2, ...), custom_call_target="tpu_custom_call" | custom-call | flops 524288 | bytes 917504 | tf_op jit(solution)/shard_map/pallas_call | solution.py:252
  45.9 0.0 collective-permute-start.16
  45.9 0.5 collective-permute-start.17
  46.4 4.8 %all-to-all-start = ((f32[32,1,128]{2,1,0:T(1,128)}), f32[32,1,128]{2,1,0:T(1,128)S(1)}, u32[]{:S(2)}, u32[]{:S(2)}) async-start(f32[32,1,128]{2,1,0:T(1,128)} %get-tuple-element.31), calls=%async_computation | async-start | bytes 32768 | tf_op jit(solution)/shard_map/all_to_all | solution.py:327
  51.2 0.0 collective-permute-done.17.key_theirs
  51.2 7.0 %all-to-all-done.squares = f32[32,1,128]{2,1,0:T(1,128)S(1)} async-done(((f32[32,1,128]{2,1,0:T(1,128)}), f32[32,1,128]{2,1,0:T(1,128)S(1)}, u32[]{:S(2)}, u32[]{:S(2)}) %all-to-all-start) | async-done | bytes 16416 | tf_op jit(solution)/shard_map/all_to_all | solution.py:327
  58.2 0.0 collective-permute-done.16.theirs
  58.2 1.0 %shard_map.83 = (bf16[1,128,512]{2,1,0:T(8,128)(2,1)}, f32[128,512]{1,0:T(8,128)}) custom-call(f32[32,1,128]{2,1,0:T(1,128)S(1)} %all-to-all-done.squares, f32[256,128]{1,0:T(8,128)S(1)} %get-tuple-element.32.mine, f32[256,128]{1,0:T(8,128)S(1)} %collective-permute-done.16.theirs, bf16[128,256]{1,0:T(8,128)(2,1)S(1)} %get-tuple-element.34.key_mine, ...), custom_call_target="tpu_custom_call" | custom-call | flops 262144 | bytes 1048576 | tf_op jit(solution)/shard_map/pallas_call | solution.py:279
  (1 shorter events, 0.0 us)
Async XLA Ops:
  0.6 8.2 %collective-permute-start = (bf16[128,512]{1,0:T(8,128)(2,1)}, bf16[128,512]{1,0:T(8,128)(2,1)S(1)}, u32[]{:S(2)}, u32[]{:S(2)}) collective-permute-start(bf16[128,512]{1,0:T(8,128)(2,1)} %bitcast.10), channel_id=1, source_target_pairs={{0,8},{8,16},{16,24},{24,0},{1,9},{9,17},{17,25},{25,1},{2,10},{10... | collective-permute-start | bytes 393224 | tf_op jit(solution)/shard_map/ppermute | solution.py:304
  1.1 7.7 %collective-permute-start.1 = (bf16[128,512]{1,0:T(8,128)(2,1)}, bf16[128,512]{1,0:T(8,128)(2,1)S(1)}, u32[]{:S(2)}, u32[]{:S(2)}) collective-permute-start(bf16[128,512]{1,0:T(8,128)(2,1)} %bitcast.13), channel_id=1, source_target_pairs={{0,8},{8,16},{16,24},{24,0},{1,9},{9,17},{17,25},{25,1},{2,10},{10... | collective-permute-start | bytes 393224 | tf_op jit(solution)/shard_map/ppermute | solution.py:305
  3.7 1.2 %copy-start = (bf16[1,128,4096]{2,1,0:T(8,128)(2,1)S(1)}, bf16[1,128,4096]{2,1,0:T(8,128)(2,1)}, u32[]{:S(2)}) copy-start(bf16[1,128,4096]{2,1,0:T(8,128)(2,1)} %param.10) | copy-start | bytes 3145732
  5.2 15.2 %collective-permute-start.6 = (bf16[4,128,256]{2,1,0:T(8,128)(2,1)S(1)}, bf16[4,128,256]{2,1,0:T(8,128)(2,1)S(1)}, u32[]{:S(2)}, u32[]{:S(2)}) collective-permute-start(bf16[4,128,256]{2,1,0:T(8,128)(2,1)S(1)} %get-tuple-element.20), channel_id=1, source_target_pairs={{0,1},{1,0},{2,3},{3,2},{4,5},{5,4},{6,7},{7,6},{8,9},{9,8},{10,11... | collective-permute-start | bytes 786440 | tf_op jit(solution)/shard_map/ppermute | solution.py:299
  6.8 13.6 %collective-permute-start.7 = (bf16[4,128,256]{2,1,0:T(8,128)(2,1)S(1)}, bf16[4,128,256]{2,1,0:T(8,128)(2,1)S(1)}, u32[]{:S(2)}, u32[]{:S(2)}) collective-permute-start(bf16[4,128,256]{2,1,0:T(8,128)(2,1)S(1)} %get-tuple-element.21), channel_id=1, source_target_pairs={{0,16},{1,17},{2,18},{3,19},{4,20},{5,21},{6,22},{7,23},{8,24},{9,... | collective-permute-start | bytes 786440 | tf_op jit(solution)/shard_map/ppermute | solution.py:299
  7.4 13.1 %collective-permute-start.8 = (bf16[4,128,256]{2,1,0:T(8,128)(2,1)S(1)}, bf16[4,128,256]{2,1,0:T(8,128)(2,1)S(1)}, u32[]{:S(2)}, u32[]{:S(2)}) collective-permute-start(bf16[4,128,256]{2,1,0:T(8,128)(2,1)S(1)} %get-tuple-element.22), channel_id=1, source_target_pairs={{0,17},{1,16},{2,19},{3,18},{4,21},{5,20},{6,23},{7,22},{8,25},{9,... | collective-permute-start | bytes 786440 | tf_op jit(solution)/shard_map/ppermute | solution.py:299
  8.8 0.7 %copy-start.2 = (bf16[128,512]{1,0:T(8,128)(2,1)}, bf16[128,512]{1,0:T(8,128)(2,1)S(1)}, u32[]{:S(2)}) copy-start(bf16[128,512]{1,0:T(8,128)(2,1)S(1)} %collective-permute-done.k_prev) | copy-start | bytes 393220
  8.8 0.7 %copy-start.3 = (bf16[128,512]{1,0:T(8,128)(2,1)}, bf16[128,512]{1,0:T(8,128)(2,1)S(1)}, u32[]{:S(2)}) copy-start(bf16[128,512]{1,0:T(8,128)(2,1)S(1)} %collective-permute-done.1.v_prev) | copy-start | bytes 393220
  13.3 4.3 %collective-permute-start.2 = (bf16[2,256,128]{2,1,0:T(8,128)(2,1)}, bf16[2,256,128]{2,1,0:T(8,128)(2,1)S(1)}, u32[]{:S(2)}, u32[]{:S(2)}) collective-permute-start(bf16[2,256,128]{2,1,0:T(8,128)(2,1)} %shard_map.78), channel_id=1, source_target_pairs={{0,8},{1,9},{2,10},{3,11},{4,12},{5,13},{6,14},{7,15},{8,0},{9,1},... | collective-permute-start | bytes 393224 | tf_op jit(solution)/shard_map/ppermute | solution.py:299
  13.3 7.8 %collective-permute-start.9 = (bf16[4,128,256]{2,1,0:T(8,128)(2,1)S(1)}, bf16[4,128,256]{2,1,0:T(8,128)(2,1)S(1)}, u32[]{:S(2)}, u32[]{:S(2)}) collective-permute-start(bf16[4,128,256]{2,1,0:T(8,128)(2,1)S(1)} %get-tuple-element.23.refs_4_), channel_id=1, source_target_pairs={{0,8},{1,9},{2,10},{3,11},{4,12},{5,13},{6,14},{7,15},{8,0},{9,1},... | collective-permute-start | bytes 786440 | tf_op jit(solution)/shard_map/ppermute | solution.py:299
  17.6 0.9 %copy-start.1 = (bf16[2,256,128]{2,1,0:T(8,128)(2,1)S(1)}, bf16[2,256,128]{2,1,0:T(8,128)(2,1)}, u32[]{:S(2)}) copy-start(bf16[2,256,128]{2,1,0:T(8,128)(2,1)} %shard_map.77.mine) | copy-start | bytes 393220
  18.6 8.7 %collective-permute-start.5 = (bf16[384,256]{1,0:T(8,128)(2,1)S(1)}, bf16[384,256]{1,0:T(8,128)(2,1)S(1)}, u32[]{:S(2)}, u32[]{:S(2)}) collective-permute-start(bf16[384,256]{1,0:T(8,128)(2,1)S(1)} %shard_map.79.refs_0_), channel_id=1, source_target_pairs={{0,17},{1,16},{2,19},{3,18},{4,21},{5,20},{6,23},{7,22},{8,25},{9,... | collective-permute-start | bytes 589832 | tf_op jit(solution)/shard_map/ppermute | solution.py:299
  20.5 12.5 %collective-permute-start.10 = (bf16[4,128,256]{2,1,0:T(8,128)(2,1)S(1)}, bf16[4,128,256]{2,1,0:T(8,128)(2,1)S(1)}, u32[]{:S(2)}, u32[]{:S(2)}) collective-permute-start(bf16[4,128,256]{2,1,0:T(8,128)(2,1)S(1)} %collective-permute-done.6.refs_5_), channel_id=1, source_target_pairs={{0,8},{1,9},{2,10},{3,11},{4,12},{5,13},{6,14},{7,15},{8,0},{9,1},... | collective-permute-start | bytes 786440 | tf_op jit(solution)/shard_map/ppermute | solution.py:299
  20.5 12.4 %collective-permute-start.11 = (bf16[4,128,256]{2,1,0:T(8,128)(2,1)S(1)}, bf16[4,128,256]{2,1,0:T(8,128)(2,1)S(1)}, u32[]{:S(2)}, u32[]{:S(2)}) collective-permute-start(bf16[4,128,256]{2,1,0:T(8,128)(2,1)S(1)} %collective-permute-done.7.refs_6_), channel_id=1, source_target_pairs={{0,8},{1,9},{2,10},{3,11},{4,12},{5,13},{6,14},{7,15},{8,0},{9,1},... | collective-permute-start | bytes 786440 | tf_op jit(solution)/shard_map/ppermute | solution.py:299
  21.0 11.9 %collective-permute-start.12 = (bf16[4,128,256]{2,1,0:T(8,128)(2,1)S(1)}, bf16[4,128,256]{2,1,0:T(8,128)(2,1)S(1)}, u32[]{:S(2)}, u32[]{:S(2)}) collective-permute-start(bf16[4,128,256]{2,1,0:T(8,128)(2,1)S(1)} %collective-permute-done.8.refs_7_), channel_id=1, source_target_pairs={{0,8},{1,9},{2,10},{3,11},{4,12},{5,13},{6,14},{7,15},{8,0},{9,1},... | collective-permute-start | bytes 786440 | tf_op jit(solution)/shard_map/ppermute | solution.py:299
  21.1 9.5 %collective-permute-start.4 = (bf16[384,256]{1,0:T(8,128)(2,1)S(1)}, bf16[384,256]{1,0:T(8,128)(2,1)S(1)}, u32[]{:S(2)}, u32[]{:S(2)}) collective-permute-start(bf16[384,256]{1,0:T(8,128)(2,1)S(1)} %shard_map.79.refs_0_), channel_id=1, source_target_pairs={{0,16},{1,17},{2,18},{3,19},{4,20},{5,21},{6,22},{7,23},{8,24},{9,... | collective-permute-start | bytes 589832 | tf_op jit(solution)/shard_map/ppermute | solution.py:299
  27.3 5.7 %collective-permute-start.3 = (bf16[384,256]{1,0:T(8,128)(2,1)S(1)}, bf16[384,256]{1,0:T(8,128)(2,1)S(1)}, u32[]{:S(2)}, u32[]{:S(2)}) collective-permute-start(bf16[384,256]{1,0:T(8,128)(2,1)S(1)} %shard_map.79.refs_0_), channel_id=1, source_target_pairs={{0,1},{1,0},{2,3},{3,2},{4,5},{5,4},{6,7},{7,6},{8,9},{9,8},{10,11... | collective-permute-start | bytes 589832 | tf_op jit(solution)/shard_map/ppermute | solution.py:299
  33.7 10.9 %collective-permute-start.13 = (bf16[256,256]{1,0:T(8,128)(2,1)S(1)}, bf16[256,256]{1,0:T(8,128)(2,1)S(1)}, u32[]{:S(2)}, u32[]{:S(2)}) collective-permute-start(bf16[256,256]{1,0:T(8,128)(2,1)S(1)} %get-tuple-element.28), channel_id=1, source_target_pairs={{0,4},{1,5},{2,6},{3,7},{4,0},{5,1},{6,2},{7,3},{8,12},{9,13},{10,... | collective-permute-start | bytes 393224 | tf_op jit(solution)/shard_map/ppermute | solution.py:299
  36.4 8.3 %collective-permute-start.14 = (bf16[256,256]{1,0:T(8,128)(2,1)S(1)}, bf16[256,256]{1,0:T(8,128)(2,1)S(1)}, u32[]{:S(2)}, u32[]{:S(2)}) collective-permute-start(bf16[256,256]{1,0:T(8,128)(2,1)S(1)} %get-tuple-element.29), channel_id=1, source_target_pairs={{0,6},{1,7},{2,4},{3,5},{4,2},{5,3},{6,0},{7,1},{8,14},{9,15},{10,... | collective-permute-start | bytes 393224 | tf_op jit(solution)/shard_map/ppermute | solution.py:299
  37.7 7.4 %collective-permute-start.15 = (bf16[256,256]{1,0:T(8,128)(2,1)S(1)}, bf16[256,256]{1,0:T(8,128)(2,1)S(1)}, u32[]{:S(2)}, u32[]{:S(2)}) collective-permute-start(bf16[256,256]{1,0:T(8,128)(2,1)S(1)} %get-tuple-element.30), channel_id=1, source_target_pairs={{0,2},{1,3},{2,0},{3,1},{4,6},{5,7},{6,4},{7,5},{8,10},{9,11},{10,... | collective-permute-start | bytes 393224 | tf_op jit(solution)/shard_map/ppermute | solution.py:299
  45.9 12.3 %collective-permute-start.16 = (f32[256,128]{1,0:T(8,128)S(1)}, f32[256,128]{1,0:T(8,128)S(1)}, u32[]{:S(2)}, u32[]{:S(2)}) collective-permute-start(f32[256,128]{1,0:T(8,128)S(1)} %get-tuple-element.33), channel_id=1, source_target_pairs={{0,8},{1,9},{2,10},{3,11},{4,12},{5,13},{6,14},{7,15},{8,0},{9,1},... | collective-permute-start | bytes 393224 | tf_op jit(solution)/shard_map/ppermute | solution.py:299
  45.9 5.3 %collective-permute-start.17 = (bf16[128,256]{1,0:T(8,128)(2,1)S(1)}, bf16[128,256]{1,0:T(8,128)(2,1)S(1)}, u32[]{:S(2)}, u32[]{:S(2)}) collective-permute-start(bf16[128,256]{1,0:T(8,128)(2,1)S(1)} %get-tuple-element.35), channel_id=1, source_target_pairs={{0,8},{1,9},{2,10},{3,11},{4,12},{5,13},{6,14},{7,15},{8,0},{9,1},... | collective-permute-start | bytes 196616 | tf_op jit(solution)/shard_map/ppermute | solution.py:299
  46.4 11.8 %all-to-all-start = ((f32[32,1,128]{2,1,0:T(1,128)}), f32[32,1,128]{2,1,0:T(1,128)S(1)}, u32[]{:S(2)}, u32[]{:S(2)}) async-start(f32[32,1,128]{2,1,0:T(1,128)} %get-tuple-element.31), calls=%async_computation | async-start | bytes 32768 | tf_op jit(solution)/shard_map/all_to_all | solution.py:327

commit v4 on v3

--- a/solution.py
+++ b/solution.py
@@ -36,24 +36,21 @@
     return seq & 1, seq >> 1, dp & 1, dp >> 1
 
 
-def first_head(which):
-    if which is None:
-        return 0
-    core = lax.axis_index("seq") & 1
-    return (core if which == 0 else 1 - core) * HALF
-
-
-def attention_kernel(which, heads, lengths, q, g, k_prev, k_own, v_prev, v_own, out, *scratch):
+def attention_kernel(turn, lengths, q, g, k_prev, k_own, v_prev, v_own, *refs):
+    outs, scratch = refs[:2], refs[2:]
     ends, q_buf, g_buf, k_buf, v_buf, bias, sems = scratch
     rows = q.shape[0]
     pair = bias.shape[1] // rows
-    first = first_head(which)
+    heads = KVH
+    core = position()[0]
+    first = (1 - core) * HALF if turn else 0
     waits = [[] for _ in range(heads)]
     length_copy = pltpu.make_async_copy(lengths, ends, sems.at[6 * heads])
     length_copy.start()
     for h in range(heads):
-        wide = pl.ds(pl.multiple_of((first + h) * GROUP * HD, GROUP * HD), GROUP * HD)
-        one = pl.ds(pl.multiple_of((first + h) * HD, HD), HD)
+        head = (first + h) & (KVH - 1)
+        wide = pl.ds(pl.multiple_of(head * GROUP * HD, GROUP * HD), GROUP * HD)
+        one = pl.ds(pl.multiple_of(head * HD, HD), HD)
         moves = [
             (k_prev.at[:, one], k_buf.at[h, :rows]),
             (k_own.at[:, one], k_buf.at[h, rows:]),
@@ -102,17 +99,18 @@
             grads = ((exponent * (inverse * scale)) * (weights - delta)).astype(BF16)
             part = lax.dot_general(grads, q_rows, nn, preferred_element_type=F32)
             total = part if total is None else total + part
-        out[r] = total.astype(out.dtype)
-
-
-def attention(which, lengths, q, g, k_prev, k_own, v_prev, v_own, heads, dtype):
+        outs[r // HALF][r % HALF] = total.astype(outs[0].dtype)
+
+
+def attention(turn, lengths, q, g, k_prev, k_own, v_prev, v_own, dtype):
     rows = q.shape[0]
+    heads = KVH
     size = heads * 2 * rows * GROUP * rows
     return pl.pallas_call(
-        functools.partial(attention_kernel, which, heads),
+        functools.partial(attention_kernel, turn),
         in_specs=[pl.BlockSpec(memory_space=pl.ANY)] * 7,
-        out_specs=pl.BlockSpec(memory_space=pltpu.VMEM),
-        out_shape=jax.ShapeDtypeStruct((heads, 2 * rows, HD), dtype),
+        out_specs=[pl.BlockSpec(memory_space=pltpu.VMEM)] * 2,
+        out_shape=[jax.ShapeDtypeStruct((HALF, 2 * rows, HD), dtype)] * 2,
         scratch_shapes=[
             pltpu.SMEM(lengths.shape, jnp.int32),
             pltpu.VMEM((heads, rows, GROUP * HD), BF16),
@@ -154,18 +152,17 @@
     )(features)
 
 
-def merge_kernel(mine, theirs, out):
+def merge_kernel(mine, theirs, *outs):
     rows = mine.shape[1] // 2
     core = position()[0]
 
     def write(even, odd):
         for h in range(HALF):
-            cols = slice(h * HD, (h + 1) * HD)
-            out[:rows, cols] = even[h, :rows]
-            out[rows : 2 * rows, cols] = (
-                even[h, rows:].astype(F32) + odd[h, :rows].astype(F32)
-            ).astype(BF16)
-            out[2 * rows :, cols] = odd[h, rows:]
+            out = outs[h]
+            out[:rows] = even[h, :rows]
+            total = even[h, rows:].astype(F32) + odd[h, :rows].astype(F32)
+            out[rows : 2 * rows] = total.astype(BF16)
+            out[2 * rows :] = odd[h, rows:]
 
     @pl.when(core == 0)
     def _():
@@ -182,16 +179,18 @@
     return pl.pallas_call(
         merge_kernel,
         in_specs=[vmem, vmem],
-        out_specs=vmem,
-        out_shape=jax.ShapeDtypeStruct((3 * rows, WIDE), BF16),
+        out_specs=[vmem] * HALF,
+        out_shape=[jax.ShapeDtypeStruct((3 * rows, HD), BF16)] * HALF,
         compiler_params=params(),
         cost_estimate=cost(rows * WIDE, 7 * rows * WIDE * 2),
     )(mine, theirs)
 
 
 def weight_kernel(nz, *refs):
-    chips, f_same, f_other = refs[:4], refs[4:8], refs[8:12]
-    sends, (keep, key_mine, key_theirs, same, other) = refs[12 : 11 + nz], refs[11 + nz :]
+    chips = (refs[0], refs[1], refs[2], refs[3])
+    f_same = (refs[4], refs[5], refs[6], refs[7])
+    f_other = [refs[8].at[m] for m in range(4)]
+    sends, (keep, key_mine, key_theirs, same, other) = refs[9 : 8 + nz], refs[8 + nz :]
     rows = chips[0].shape[0] // 3
     core, x, y, z = position()
     for m in range(4):
@@ -220,73 +219,115 @@
     rows = chips[0].shape[0] // 3
     nz = f_same[0].shape[0]
     vmem = pl.BlockSpec(memory_space=pltpu.VMEM)
-    square = (WIDE, f_same[0].shape[2])
+    square = (HD, f_same[0].shape[2])
     shapes = [jax.ShapeDtypeStruct(square, BF16)] * (nz - 1)
-    shapes += [jax.ShapeDtypeStruct(square, F32)] + [jax.ShapeDtypeStruct((rows, WIDE), BF16)] * 2
+    shapes += [jax.ShapeDtypeStruct(square, F32)] + [jax.ShapeDtypeStruct((rows, HD), BF16)] * 2
     return pl.pallas_call(
         functools.partial(weight_kernel, nz),
-        in_specs=[vmem] * 12,
+        in_specs=[vmem] * 9,
         out_specs=[vmem] * len(shapes),
         out_shape=shapes,
-        scratch_shapes=[pltpu.VMEM((4 * rows, WIDE), BF16)] * 2,
-        compiler_params=params(),
-        cost_estimate=cost(2 * 8 * rows * WIDE * 4 * WIDE, 4 << 20),
-    )(*chips, *f_same, *f_other)
-
-
-def reduce_kernel(keep, r1, r2, r3, mine, theirs, squares):
-    total = keep[...] + r1[...].astype(F32) + r2[...].astype(F32) + r3[...].astype(F32)
-    half = total.shape[1] // 2
+        scratch_shapes=[pltpu.VMEM((4 * rows, HD), BF16)] * 2,
+        compiler_params=params(),
+        cost_estimate=cost(2 * 8 * rows * HD * 4 * WIDE, 4 << 20),
+    )(*[chips[m] for m in (0, 1, 2, 3)], *[f_same[m] for m in (0, 1, 2, 3)], *f_other)
+
+
+def squares_kernel(*refs):
+    squares = refs[-1]
+    sums = 0.0
+    for h in range(HALF):
+        keep, r1, r2, r3 = refs[4 * h : 4 * h + 4]
+        total = keep[...] + r1[...].astype(F32) + r2[...].astype(F32) + r3[...].astype(F32)
+        half = total.shape[1] // 2
+        low, high = total[:, :half], total[:, half:]
+        sums += jnp.sum(low * low + high * high, axis=0, keepdims=True)
+    squares[...] = jnp.broadcast_to(sums[None], squares.shape)
+
+
+def plane_squares(parts, devices):
+    cols, both = parts[0].shape
+    vmem = pl.BlockSpec(memory_space=pltpu.VMEM)
+    return pl.pallas_call(
+        squares_kernel,
+        in_specs=[vmem] * len(parts),
+        out_specs=vmem,
+        out_shape=jax.ShapeDtypeStruct((devices, 1, both // 2), F32),
+        compiler_params=params(),
+        cost_estimate=cost(16 * cols * both, cols * both * 20),
+    )(*parts)
+
+
+def rows_kernel(*refs):
+    mine, theirs = refs[-2:]
     core = position()[0]
-    low, high = total[:, :half], total[:, half:]
-    mine[...] = jnp.where(core == 0, low, high)
-    theirs[...] = jnp.where(core == 0, high, low)
-    sums = jnp.sum(low * low + high * high, axis=0, keepdims=True)
-    squares[...] = jnp.broadcast_to(sums[None], squares.shape)
-
-
-def reduce_planes(keep, received, devices):
-    cols, both = keep.shape
-    vmem = pl.BlockSpec(memory_space=pltpu.VMEM)
-    half = jax.ShapeDtypeStruct((cols, both // 2), F32)
-    return pl.pallas_call(
-        reduce_kernel,
-        in_specs=[vmem] * 4,
-        out_specs=[vmem] * 3,
-        out_shape=[half, half, jax.ShapeDtypeStruct((devices, 1, both // 2), F32)],
-        compiler_params=params(),
-        cost_estimate=cost(8 * cols * both, cols * both * 14),
-    )(keep, *received)
-
-
-def finish_kernel(squares, mine, theirs, key_mine, key_theirs, key_out, out):
+    for h in range(HALF):
+        keep, r1, r2, r3 = refs[4 * h : 4 * h + 4]
+        total = keep[...] + r1[...].astype(F32) + r2[...].astype(F32) + r3[...].astype(F32)
+        half = total.shape[1] // 2
+        low, high = total[:, :half].T, total[:, half:].T
+        cols = slice(h * HD, (h + 1) * HD)
+        mine[:, cols] = jnp.where(core == 0, low, high)
+        theirs[:, cols] = jnp.where(core == 0, high, low)
+
+
+def plane_rows(parts):
+    cols, both = parts[0].shape
+    vmem = pl.BlockSpec(memory_space=pltpu.VMEM)
+    return pl.pallas_call(
+        rows_kernel,
+        in_specs=[vmem] * len(parts),
+        out_specs=[vmem] * 2,
+        out_shape=[jax.ShapeDtypeStruct((both // 2, WIDE), F32)] * 2,
+        compiler_params=params(),
+        cost_estimate=cost(16 * cols * both, cols * both * 28),
+    )(*parts)
+
+
+def join_kernel(mine, theirs, *refs):
+    keys_mine, keys_theirs, (out, key_out) = refs[:HALF], refs[HALF : 2 * HALF], refs[2 * HALF :]
+    first = position()[0] == 0
+    out[:, :WIDE] = jnp.where(first, mine[...], theirs[...])
+    out[:, WIDE:] = jnp.where(first, theirs[...], mine[...])
+    for h in range(HALF):
+        own, far = keys_mine[h][...], keys_theirs[h][...]
+        key_out[0, :, h * HD : (h + 1) * HD] = jnp.where(first, own, far)
+        key_out[0, :, WIDE + h * HD : WIDE + (h + 1) * HD] = jnp.where(first, far, own)
+
+
+def join(mine, theirs, keys_mine, keys_theirs):
+    rows = keys_mine[0].shape[0]
+    vmem = pl.BlockSpec(memory_space=pltpu.VMEM)
+    return pl.pallas_call(
+        join_kernel,
+        in_specs=[vmem] * (2 + 2 * HALF),
+        out_specs=[vmem] * 2,
+        out_shape=[
+            jax.ShapeDtypeStruct((mine.shape[0], KVH * HD), F32),
+            jax.ShapeDtypeStruct((1, rows, KVH * HD), BF16),
+        ],
+        compiler_params=params(),
+        cost_estimate=cost(0, 12 * rows * KVH * HD),
+    )(mine, theirs, *keys_mine, *keys_theirs)
+
+
+def clip_kernel(squares, rows, out):
     entries = DW * KVH * HD
     total = jnp.sum(jnp.sum(squares[...], axis=0, keepdims=True), axis=2, keepdims=True)
     root_mean = jnp.sqrt(total / entries + 1e-06)
-    factor = jnp.minimum(1.0, 1.0 / root_mean)[0]
-    first = position()[0] == 0
-    low = (mine[...] * factor).T
-    high = (theirs[...] * factor).T
-    out[:, :WIDE] = jnp.where(first, low, high)
-    out[:, WIDE:] = jnp.where(first, high, low)
-    key_out[0, :, :WIDE] = jnp.where(first, key_mine[...], key_theirs[...])
-    key_out[0, :, WIDE:] = jnp.where(first, key_theirs[...], key_mine[...])
-
-
-def finish(squares, mine, theirs, key_mine, key_theirs):
-    rows = key_mine.shape[0]
-    vmem = pl.BlockSpec(memory_space=pltpu.VMEM)
-    return pl.pallas_call(
-        finish_kernel,
-        in_specs=[vmem] * 5,
-        out_specs=[vmem] * 2,
-        out_shape=[
-            jax.ShapeDtypeStruct((1, rows, KVH * HD), BF16),
-            jax.ShapeDtypeStruct((mine.shape[1], KVH * HD), F32),
-        ],
-        compiler_params=params(),
-        cost_estimate=cost(4 * rows * KVH * HD, 4 * rows * KVH * HD * 4),
-    )(squares, mine, theirs, key_mine, key_theirs)
+    out[...] = rows[...] * jnp.minimum(1.0, 1.0 / root_mean)[0]
+
+
+def clip(squares, rows):
+    vmem = pl.BlockSpec(memory_space=pltpu.VMEM)
+    return pl.pallas_call(
+        clip_kernel,
+        in_specs=[vmem] * 2,
+        out_specs=vmem,
+        out_shape=jax.ShapeDtypeStruct(rows.shape, F32),
+        compiler_params=params(),
+        cost_estimate=cost(rows.size, 8 * rows.size),
+    )(squares, rows)
 
 
 def planes(queries, keys, values, grad_out, features, doc_lengths):
@@ -309,23 +350,27 @@
     f_same = [packed[0]] + [swap(part, mask) for part, mask in zip(packed[1:], masks[1:])]
 
     near = (queries[0], grad_out[0], k_prev, k_own, v_prev, v_own)
-    to_send = attention(1, doc_lengths, *near, HALF, BF16)
+    to_send, mine = attention(True, doc_lengths, *near, BF16)
     theirs = swap(to_send, core_mask)
-    mine = attention(0, doc_lengths, *near, HALF, BF16)
-    chip = merge(mine, theirs)
-    chips = [chip] + [swap(chip, mask) for mask in masks[1:]]
-    f_own, _ = lax.optimization_barrier((f_same[0], to_send))
-    f_own = swap(f_own, core_mask)
-    f_ready, _ = lax.optimization_barrier((f_same[1:], chip))
-    f_other = [f_own] + [swap(part, core_mask) for part in f_ready]
-
-    *sends, keep, key_mine, key_send = weight(chips, f_same, f_other)
-    received = [swap(sends[m], (m + 1) * z_mask) for m in (1, 2, 0)]
-    key_other = swap(key_send, core_mask)
-    rows_mine, rows_send, squares = reduce_planes(keep, received, devices)
+    pieces = merge(mine, theirs)
+    chips = [[piece] + [swap(piece, mask) for mask in masks[1:]] for piece in pieces]
+    f_ready, _ = lax.optimization_barrier((f_same, pieces[0]))
+    far = swap(jnp.stack(f_ready), core_mask)
+    f_other = [far]
+
+    parts, keys_mine, keys_other = [], [], []
+    for h in range(HALF):
+        *sends, keep, key_mine, key_send = weight(chips[h], f_same, f_other)
+        parts += [keep] + [swap(sends[m], (m + 1) * z_mask) for m in (1, 2, 0)]
+        keys_mine.append(key_mine)
+        keys_other.append(swap(key_send, core_mask))
+    squares = plane_squares(parts, devices)
+    parts[0], squares = lax.optimization_barrier((parts[0], squares))
+    squares = lax.all_to_all(squares, AXES, 0, 0, tiled=True)
+    rows_mine, rows_send = plane_rows(parts)
     rows_other = swap(rows_send, core_mask)
-    squares = lax.all_to_all(squares, AXES, 0, 0, tiled=True)
-    return finish(squares, rows_mine, rows_other, key_mine, key_other)
+    rows, key_grad = join(rows_mine, rows_other, keys_mine, keys_other)
+    return key_grad, clip(squares, rows)
 
 
 def rings(queries, keys, values, grad_out, features, doc_lengths):
@@ -337,7 +382,7 @@
     k_prev = lax.ppermute(k_own, "seq", following)
     v_prev = lax.ppermute(v_own, "seq", following)
     near = (queries[0], grad_out[0], k_prev, k_own, v_prev, v_own)
-    parts = attention(None, doc_lengths, *near, KVH, F32)
+    parts = jnp.concatenate(attention(False, doc_lengths, *near, F32), axis=0)
     parts = parts.transpose(1, 0, 2).reshape(2 * rows, KVH * HD)
     after = lax.ppermute(parts[:rows], "seq", preceding)
     key_grad = (parts[rows:] + after).astype(BF16)

time: 59.4 us -> 58.3 us (0.981)
  waiting for transfers between devices: 23.3 us -> 16.5 us
  starting transfers between devices: 22.1 us -> 28.4 us
  Pallas kernels: 10.3 us -> 9.41 us
    ppermute x16 -> x20, starting transfers between devices: 14.2 us -> 20.5 us  [swap(): return lax.ppermute(array, AXES, [(i, i ^ mask) for i in range(devices)])]
    ppermute x16 -> x20, waiting for transfers between devices: 16.2 us -> 10.2 us  [swap(): return lax.ppermute(array, AXES, [(i, i ^ mask) for i in range(devices)])]
    pallas_call x6 -> x8, Pallas kernels: 10 us -> 9.14 us  [the longest x1 5.75 us: attention(): pl.pallas_call(functools.partial(attention_kernel, turn), in_specs=[pl.Bl...]
    all_to_all x1, waiting for transfers between devices: 7.03 us -> 6.31 us  [planes(): squares = lax.all_to_all(squares, AXES, 0, 0, tiled=True)]
  transfers between devices with their start and end apart: 19 -> 23, of which waited for: 6 -> 10; matrix products, arithmetic and copies ran while one was open for 0% -> 0% of each run, Pallas kernels for 13% -> 13%
where the time goes in v4:
time: 58.3 us; the launch traced here: 58 us
  starting transfers between devices  28.4 us (49%)
  waiting for transfers between devices  16.5 us (28%)
  Pallas kernels  9.41 us (16%)
  local copies, waits for them, and re-layouts  2.81 us (5%)
  between operations  0.77 us (1%)
    ppermute x20, starting transfers between devices, swap(): return lax.ppermute(array, AXES, [(i, i ^ mask) for i in range(devices)])  20.5 us
    ppermute x20, waiting for transfers between devices, swap(): return lax.ppermute(array, AXES, [(i, i ^ mask) for i in range(devices)])  10.2 us
    all_to_all x1, waiting for transfers between devices, planes(): squares = lax.all_to_all(squares, AXES, 0, 0, tiled=True)  6.31 us
    pallas_call x1, Pallas kernels, attention(): pl.pallas_call(functools.partial(attention_kernel, turn), in_specs=[pl.Bl...  5.75 us
    all_to_all x1, starting transfers between devices, planes(): squares = lax.all_to_all(squares, AXES, 0, 0, tiled=True)  4.79 us
    unnamed x8, local copies, waits for them, and re-layouts  2.81 us
    ppermute x1, starting transfers between devices, planes(): v_prev = lax.ppermute(v_own, 'seq', following)  2.6 us
  transfers between devices with their start and end apart: 23, of which 10 were waited for; matrix products, arithmetic and copies ran while one was open for 0% of the time, Pallas kernels for 13%

profile of v4, /device:TPU:0, one launch (start us, length us, event | category | flops | bytes accessed | tf_op | source)
XLA Modules:
  0.0 58.0 jit_solution(17198163704369030825)
XLA Ops:
  0.6 0.5 collective-permute-start
  1.1 2.6 %collective-permute-start.1 = (bf16[128,512]{1,0:T(8,128)(2,1)}, bf16[128,512]{1,0:T(8,128)(2,1)S(1)}, u32[]{:S(2)}, u32[]{:S(2)}) collective-permute-start(bf16[128,512]{1,0:T(8,128)(2,1)} %bitcast.18), channel_id=1, source_target_pairs={{0,8},{8,16},{16,24},{24,0},{1,9},{9,17},{17,25},{25,1},{2,10},{10... | collective-permute-start | bytes 393224 | tf_op jit(solution)/shard_map/ppermute | solution.py:346
  3.7 0.0 copy-start
  3.7 1.2 %copy-done = bf16[1,128,4096]{2,1,0:T(8,128)(2,1)S(1)} copy-done((bf16[1,128,4096]{2,1,0:T(8,128)(2,1)S(1)}, bf16[1,128,4096]{2,1,0:T(8,128)(2,1)}, u32[]{:S(2)}) %copy-start) | copy-done | bytes 1048600
  5.0 0.3 shard_map.79
  5.2 1.6 %collective-permute-start.6 = (bf16[4,128,256]{2,1,0:T(8,128)(2,1)S(1)}, bf16[4,128,256]{2,1,0:T(8,128)(2,1)S(1)}, u32[]{:S(2)}, u32[]{:S(2)}) collective-permute-start(bf16[4,128,256]{2,1,0:T(8,128)(2,1)S(1)} %get-tuple-element.36), channel_id=1, source_target_pairs={{0,1},{1,0},{2,3},{3,2},{4,5},{5,4},{6,7},{7,6},{8,9},{9,8},{10,11... | collective-permute-start | bytes 786440 | tf_op jit(solution)/shard_map/ppermute | solution.py:340
  6.8 0.5 collective-permute-start.7
  7.4 1.4 %collective-permute-start.8 = (bf16[4,128,256]{2,1,0:T(8,128)(2,1)S(1)}, bf16[4,128,256]{2,1,0:T(8,128)(2,1)S(1)}, u32[]{:S(2)}, u32[]{:S(2)}) collective-permute-start(bf16[4,128,256]{2,1,0:T(8,128)(2,1)S(1)} %get-tuple-element.38), channel_id=1, source_target_pairs={{0,17},{1,16},{2,19},{3,18},{4,21},{5,20},{6,23},{7,22},{8,25},{9,... | collective-permute-start | bytes 786440 | tf_op jit(solution)/shard_map/ppermute | solution.py:340
  8.8 0.0 collective-permute-done.k_prev
  8.8 0.0 copy-start.2
  8.8 0.0 collective-permute-done.1.v_prev
  8.8 0.0 copy-start.3
  8.8 0.6 %copy-done.2 = bf16[128,512]{1,0:T(8,128)(2,1)} copy-done((bf16[128,512]{1,0:T(8,128)(2,1)}, bf16[128,512]{1,0:T(8,128)(2,1)S(1)}, u32[]{:S(2)}) %copy-start.2) | copy-done | bytes 131096
  9.4 0.0 copy-done.3
  9.5 5.7 %shard_map.77 = (bf16[2,256,128]{2,1,0:T(8,128)(2,1)}, bf16[2,256,128]{2,1,0:T(8,128)(2,1)}) custom-call(s32[1,8]{1,0:T(1,128)} %lengths.1, bf16[128,4096]{1,0:T(8,128)(2,1)} %bitcast.14, bf16[128,4096]{1,0:T(8,128)(2,1)} %bitcast.15, bf16[128,512]{1,0:T(8,128)(2,1)} %copy-done.2, bf16[128,512]{1,0:T(8,128)(2,1)} %bitcast.17, bf16[128,512]{1,0:T(8,128)(2,1)} %copy-done.3, ...), custom_call_target="tpu_custom_call" | custom-call | flops 805306368 | bytes 2097152 | tf_op jit(solution)/shard_map/pallas_call | solution.py:109
  15.2 0.1 collective-permute-start.2
  15.3 1.5 %collective-permute-done.2.theirs = bf16[2,256,128]{2,1,0:T(8,128)(2,1)S(1)} collective-permute-done((bf16[2,256,128]{2,1,0:T(8,128)(2,1)}, bf16[2,256,128]{2,1,0:T(8,128)(2,1)S(1)}, u32[]{:S(2)}, u32[]{:S(2)}) %collective-permute-start.2) | collective-permute-done | bytes 131104 | tf_op jit(solution)/shard_map/ppermute | solution.py:340
  16.9 0.0 copy-start.1
  16.9 0.9 %copy-done.1 = bf16[2,256,128]{2,1,0:T(8,128)(2,1)S(1)} copy-done((bf16[2,256,128]{2,1,0:T(8,128)(2,1)S(1)}, bf16[2,256,128]{2,1,0:T(8,128)(2,1)}, u32[]{:S(2)}) %copy-start.1) | copy-done | bytes 131096
  17.8 0.0 collective-permute-done.6.refs_5_
  17.8 0.0 collective-permute-done.7.refs_6_
  17.8 2.6 %collective-permute-done.8.refs_7_ = bf16[4,128,256]{2,1,0:T(8,128)(2,1)S(1)} collective-permute-done((bf16[4,128,256]{2,1,0:T(8,128)(2,1)S(1)}, bf16[4,128,256]{2,1,0:T(8,128)(2,1)S(1)}, u32[]{:S(2)}, u32[]{:S(2)}) %collective-permute-start.8) | collective-permute-done | bytes 262176 | tf_op jit(solution)/shard_map/ppermute | solution.py:340
  20.4 0.1 pad_maximum_fusion
  20.5 0.1 collective-permute-start.9
  20.6 1.6 %collective-permute-start.13 = (bf16[384,128]{1,0:T(8,128)(2,1)S(1)}, bf16[384,128]{1,0:T(8,128)(2,1)S(1)}, u32[]{:S(2)}, u32[]{:S(2)}) collective-permute-start(bf16[384,128]{1,0:T(8,128)(2,1)S(1)} %get-tuple-element.47.refs_0_), channel_id=1, source_target_pairs={{0,1},{1,0},{2,3},{3,2},{4,5},{5,4},{6,7},{7,6},{8,9},{9,8},{10,11... | collective-permute-start | bytes 294920 | tf_op jit(solution)/shard_map/ppermute | solution.py:340
  22.2 0.5 collective-permute-start.14
  22.7 1.4 %collective-permute-start.15 = (bf16[384,128]{1,0:T(8,128)(2,1)S(1)}, bf16[384,128]{1,0:T(8,128)(2,1)S(1)}, u32[]{:S(2)}, u32[]{:S(2)}) collective-permute-start(bf16[384,128]{1,0:T(8,128)(2,1)S(1)} %get-tuple-element.47.refs_0_), channel_id=1, source_target_pairs={{0,17},{1,16},{2,19},{3,18},{4,21},{5,20},{6,23},{7,22},{8,25},{9,... | collective-permute-start | bytes 294920 | tf_op jit(solution)/shard_map/ppermute | solution.py:340
  24.1 1.5 %collective-permute-start.3 = (bf16[384,128]{1,0:T(8,128)(2,1)S(1)}, bf16[384,128]{1,0:T(8,128)(2,1)S(1)}, u32[]{:S(2)}, u32[]{:S(2)}) collective-permute-start(bf16[384,128]{1,0:T(8,128)(2,1)S(1)} %get-tuple-element.34.refs_0_), channel_id=1, source_target_pairs={{0,1},{1,0},{2,3},{3,2},{4,5},{5,4},{6,7},{7,6},{8,9},{9,8},{10,11... | collective-permute-start | bytes 294920 | tf_op jit(solution)/shard_map/ppermute | solution.py:340
  25.7 0.1 collective-permute-done.13.refs_1_
  25.8 1.3 %collective-permute-start.4 = (bf16[384,128]{1,0:T(8,128)(2,1)S(1)}, bf16[384,128]{1,0:T(8,128)(2,1)S(1)}, u32[]{:S(2)}, u32[]{:S(2)}) collective-permute-start(bf16[384,128]{1,0:T(8,128)(2,1)S(1)} %get-tuple-element.34.refs_0_), channel_id=1, source_target_pairs={{0,16},{1,17},{2,18},{3,19},{4,20},{5,21},{6,22},{7,23},{8,24},{9,... | collective-permute-start | bytes 294920 | tf_op jit(solution)/shard_map/ppermute | solution.py:340
  27.1 0.7 %collective-permute-done.14.refs_2_ = bf16[384,128]{1,0:T(8,128)(2,1)S(1)} collective-permute-done((bf16[384,128]{1,0:T(8,128)(2,1)S(1)}, bf16[384,128]{1,0:T(8,128)(2,1)S(1)}, u32[]{:S(2)}, u32[]{:S(2)}) %collective-permute-start.14) | collective-permute-done | bytes 98336 | tf_op jit(solution)/shard_map/ppermute | solution.py:340
  27.8 1.2 %collective-permute-start.5 = (bf16[384,128]{1,0:T(8,128)(2,1)S(1)}, bf16[384,128]{1,0:T(8,128)(2,1)S(1)}, u32[]{:S(2)}, u32[]{:S(2)}) collective-permute-start(bf16[384,128]{1,0:T(8,128)(2,1)S(1)} %get-tuple-element.34.refs_0_), channel_id=1, source_target_pairs={{0,17},{1,16},{2,19},{3,18},{4,21},{5,20},{6,23},{7,22},{8,25},{9,... | collective-permute-start | bytes 294920 | tf_op jit(solution)/shard_map/ppermute | solution.py:340
  29.1 0.1 collective-permute-done.15.refs_3_
  29.2 0.0 collective-permute-done.9.refs_8_
  29.2 0.5 shard_map.81
  29.7 2.7 %collective-permute-start.16 = (bf16[128,256]{1,0:T(8,128)(2,1)S(1)}, bf16[128,256]{1,0:T(8,128)(2,1)S(1)}, u32[]{:S(2)}, u32[]{:S(2)}) collective-permute-start(bf16[128,256]{1,0:T(8,128)(2,1)S(1)} %get-tuple-element.49), channel_id=1, source_target_pairs={{0,4},{1,5},{2,6},{3,7},{4,0},{5,1},{6,2},{7,3},{8,12},{9,13},{10,... | collective-permute-start | bytes 196616 | tf_op jit(solution)/shard_map/ppermute | solution.py:340
  32.4 1.3 %collective-permute-start.17 = (bf16[128,256]{1,0:T(8,128)(2,1)S(1)}, bf16[128,256]{1,0:T(8,128)(2,1)S(1)}, u32[]{:S(2)}, u32[]{:S(2)}) collective-permute-start(bf16[128,256]{1,0:T(8,128)(2,1)S(1)} %get-tuple-element.50), channel_id=1, source_target_pairs={{0,6},{1,7},{2,4},{3,5},{4,2},{5,3},{6,0},{7,1},{8,14},{9,15},{10,... | collective-permute-start | bytes 196616 | tf_op jit(solution)/shard_map/ppermute | solution.py:340
  33.7 0.0 collective-permute-done.3.refs_1_
  33.7 0.2 collective-permute-start.18
  34.0 0.0 collective-permute-done.4.refs_2_
  34.0 0.0 collective-permute-done.5.refs_3_
  34.0 0.5 shard_map.80
  34.5 2.9 %collective-permute-start.10 = (bf16[128,256]{1,0:T(8,128)(2,1)S(1)}, bf16[128,256]{1,0:T(8,128)(2,1)S(1)}, u32[]{:S(2)}, u32[]{:S(2)}) collective-permute-start(bf16[128,256]{1,0:T(8,128)(2,1)S(1)} %get-tuple-element.44), channel_id=1, source_target_pairs={{0,4},{1,5},{2,6},{3,7},{4,0},{5,1},{6,2},{7,3},{8,12},{9,13},{10,... | collective-permute-start | bytes 196616 | tf_op jit(solution)/shard_map/ppermute | solution.py:340
  37.3 1.3 %collective-permute-start.11 = (bf16[128,256]{1,0:T(8,128)(2,1)S(1)}, bf16[128,256]{1,0:T(8,128)(2,1)S(1)}, u32[]{:S(2)}, u32[]{:S(2)}) collective-permute-start(bf16[128,256]{1,0:T(8,128)(2,1)S(1)} %get-tuple-element.45), channel_id=1, source_target_pairs={{0,6},{1,7},{2,4},{3,5},{4,2},{5,3},{6,0},{7,1},{8,14},{9,15},{10,... | collective-permute-start | bytes 196616 | tf_op jit(solution)/shard_map/ppermute | solution.py:340
  38.7 0.0 collective-permute-done.16.refs_5_
  38.7 0.0 collective-permute-start.12
  38.7 0.5 collective-permute-done.17.refs_6_
  39.2 0.0 collective-permute-done.18.refs_7_
  39.2 3.5 %collective-permute-done.10.refs_1_ = bf16[128,256]{1,0:T(8,128)(2,1)S(1)} collective-permute-done((bf16[128,256]{1,0:T(8,128)(2,1)S(1)}, bf16[128,256]{1,0:T(8,128)(2,1)S(1)}, u32[]{:S(2)}, u32[]{:S(2)}) %collective-permute-start.10) | collective-permute-done | bytes 65568 | tf_op jit(solution)/shard_map/ppermute | solution.py:340
  42.6 0.9 %collective-permute-done.11.refs_2_ = bf16[128,256]{1,0:T(8,128)(2,1)S(1)} collective-permute-done((bf16[128,256]{1,0:T(8,128)(2,1)S(1)}, bf16[128,256]{1,0:T(8,128)(2,1)S(1)}, u32[]{:S(2)}, u32[]{:S(2)}) %collective-permute-start.11) | collective-permute-done | bytes 65568 | tf_op jit(solution)/shard_map/ppermute | solution.py:340
  43.6 0.3 collective-permute-done.12.refs_3_
  43.8 0.7 %shard_map.82 = f32[32,1,128]{2,1,0:T(1,128)} custom-call(f32[128,256]{1,0:T(8,128)S(1)} %get-tuple-element.52.refs_0_, bf16[128,256]{1,0:T(8,128)(2,1)S(1)} %collective-permute-done.10.refs_1_, bf16[128,256]{1,0:T(8,128)(2,1)S(1)} %collective-permute-done.11.refs_2_, bf16[128,256]{1,0:T(8,128)(2,1)S(1)} %collective-permute-done.12.refs_3_, ...), custom_call_target="tpu_custom_call" | custom-call | flops 524288 | bytes 655360 | tf_op jit(solution)/shard_map/pallas_call | solution.py:251
  44.5 0.1 shard_map.83
  44.7 0.1 collective-permute-start.19
  44.8 0.5 collective-permute-start.21
  45.3 0.1 collective-permute-start.20
  45.3 4.8 %all-to-all-start = ((f32[32,1,128]{2,1,0:T(1,128)}), f32[32,1,128]{2,1,0:T(1,128)S(1)}, u32[]{:S(2)}, u32[]{:S(2)}) async-start(f32[32,1,128]{2,1,0:T(1,128)} %shard_map.82), calls=%async_computation | async-start | bytes 32768 | tf_op jit(solution)/shard_map/all_to_all | solution.py:369
  50.1 0.0 collective-permute-done.21.refs_3_
  50.2 0.0 collective-permute-done.20.refs_2_
  50.2 0.0 collective-permute-done.19.theirs
  50.2 0.7 %shard_map.84 = (f32[128,512]{1,0:T(8,128)S(1)}, bf16[1,128,512]{2,1,0:T(8,128)(2,1)}) custom-call(f32[128,256]{1,0:T(8,128)S(1)} %get-tuple-element.53.mine, f32[128,256]{1,0:T(8,128)S(1)} %collective-permute-done.19.theirs, bf16[128,128]{1,0:T(8,128)(2,1)S(1)} %get-tuple-element.55.refs_0_, bf16[128,128]{1,0:T(8,128)(2,1)S(1)} %get-tuple-element.56.refs_1_, ...), custom_call_target="tpu_custom_call" | custom-call | bytes 786432 | tf_op jit(solution)/shard_map/pallas_call | solution.py:301
  50.9 6.3 %all-to-all-done.squares = f32[32,1,128]{2,1,0:T(1,128)S(1)} async-done(((f32[32,1,128]{2,1,0:T(1,128)}), f32[32,1,128]{2,1,0:T(1,128)S(1)}, u32[]{:S(2)}, u32[]{:S(2)}) %all-to-all-start) | async-done | bytes 16416 | tf_op jit(solution)/shard_map/all_to_all | solution.py:369
  57.2 0.8 %shard_map.85 = f32[128,512]{1,0:T(8,128)} custom-call(f32[32,1,128]{2,1,0:T(1,128)S(1)} %all-to-all-done.squares, f32[128,512]{1,0:T(8,128)S(1)} %get-tuple-element.61.rows), custom_call_target="tpu_custom_call" | custom-call | flops 65536 | bytes 524288 | tf_op jit(solution)/shard_map/pallas_call | solution.py:323
  (1 shorter events, 0.0 us)
Async XLA Ops:
  0.6 8.2 %collective-permute-start = (bf16[128,512]{1,0:T(8,128)(2,1)}, bf16[128,512]{1,0:T(8,128)(2,1)S(1)}, u32[]{:S(2)}, u32[]{:S(2)}) collective-permute-start(bf16[128,512]{1,0:T(8,128)(2,1)} %bitcast.16), channel_id=1, source_target_pairs={{0,8},{8,16},{16,24},{24,0},{1,9},{9,17},{17,25},{25,1},{2,10},{10... | collective-permute-start | bytes 393224 | tf_op jit(solution)/shard_map/ppermute | solution.py:345
  1.1 7.7 %collective-permute-start.1 = (bf16[128,512]{1,0:T(8,128)(2,1)}, bf16[128,512]{1,0:T(8,128)(2,1)S(1)}, u32[]{:S(2)}, u32[]{:S(2)}) collective-permute-start(bf16[128,512]{1,0:T(8,128)(2,1)} %bitcast.18), channel_id=1, source_target_pairs={{0,8},{8,16},{16,24},{24,0},{1,9},{9,17},{17,25},{25,1},{2,10},{10... | collective-permute-start | bytes 393224 | tf_op jit(solution)/shard_map/ppermute | solution.py:346
  3.7 1.2 %copy-start = (bf16[1,128,4096]{2,1,0:T(8,128)(2,1)S(1)}, bf16[1,128,4096]{2,1,0:T(8,128)(2,1)}, u32[]{:S(2)}) copy-start(bf16[1,128,4096]{2,1,0:T(8,128)(2,1)} %param.10) | copy-start | bytes 3145732
  5.2 12.6 %collective-permute-start.6 = (bf16[4,128,256]{2,1,0:T(8,128)(2,1)S(1)}, bf16[4,128,256]{2,1,0:T(8,128)(2,1)S(1)}, u32[]{:S(2)}, u32[]{:S(2)}) collective-permute-start(bf16[4,128,256]{2,1,0:T(8,128)(2,1)S(1)} %get-tuple-element.36), channel_id=1, source_target_pairs={{0,1},{1,0},{2,3},{3,2},{4,5},{5,4},{6,7},{7,6},{8,9},{9,8},{10,11... | collective-permute-start | bytes 786440 | tf_op jit(solution)/shard_map/ppermute | solution.py:340
  6.8 11.0 %collective-permute-start.7 = (bf16[4,128,256]{2,1,0:T(8,128)(2,1)S(1)}, bf16[4,128,256]{2,1,0:T(8,128)(2,1)S(1)}, u32[]{:S(2)}, u32[]{:S(2)}) collective-permute-start(bf16[4,128,256]{2,1,0:T(8,128)(2,1)S(1)} %get-tuple-element.37), channel_id=1, source_target_pairs={{0,16},{1,17},{2,18},{3,19},{4,20},{5,21},{6,22},{7,23},{8,24},{9,... | collective-permute-start | bytes 786440 | tf_op jit(solution)/shard_map/ppermute | solution.py:340
  7.4 13.0 %collective-permute-start.8 = (bf16[4,128,256]{2,1,0:T(8,128)(2,1)S(1)}, bf16[4,128,256]{2,1,0:T(8,128)(2,1)S(1)}, u32[]{:S(2)}, u32[]{:S(2)}) collective-permute-start(bf16[4,128,256]{2,1,0:T(8,128)(2,1)S(1)} %get-tuple-element.38), channel_id=1, source_target_pairs={{0,17},{1,16},{2,19},{3,18},{4,21},{5,20},{6,23},{7,22},{8,25},{9,... | collective-permute-start | bytes 786440 | tf_op jit(solution)/shard_map/ppermute | solution.py:340
  8.8 0.7 %copy-start.2 = (bf16[128,512]{1,0:T(8,128)(2,1)}, bf16[128,512]{1,0:T(8,128)(2,1)S(1)}, u32[]{:S(2)}) copy-start(bf16[128,512]{1,0:T(8,128)(2,1)S(1)} %collective-permute-done.k_prev) | copy-start | bytes 393220
  8.8 0.7 %copy-start.3 = (bf16[128,512]{1,0:T(8,128)(2,1)}, bf16[128,512]{1,0:T(8,128)(2,1)S(1)}, u32[]{:S(2)}) copy-start(bf16[128,512]{1,0:T(8,128)(2,1)S(1)} %collective-permute-done.1.v_prev) | copy-start | bytes 393220
  15.2 1.6 %collective-permute-start.2 = (bf16[2,256,128]{2,1,0:T(8,128)(2,1)}, bf16[2,256,128]{2,1,0:T(8,128)(2,1)S(1)}, u32[]{:S(2)}, u32[]{:S(2)}) collective-permute-start(bf16[2,256,128]{2,1,0:T(8,128)(2,1)} %get-tuple-element.33), channel_id=1, source_target_pairs={{0,8},{1,9},{2,10},{3,11},{4,12},{5,13},{6,14},{7,15},{8,0},{9,1},... | collective-permute-start | bytes 393224 | tf_op jit(solution)/shard_map/ppermute | solution.py:340
  16.9 0.9 %copy-start.1 = (bf16[2,256,128]{2,1,0:T(8,128)(2,1)S(1)}, bf16[2,256,128]{2,1,0:T(8,128)(2,1)}, u32[]{:S(2)}) copy-start(bf16[2,256,128]{2,1,0:T(8,128)(2,1)} %get-tuple-element.32.mine) | copy-start | bytes 393220
  20.5 8.7 %collective-permute-start.9 = (bf16[4,4,128,256]{3,2,1,0:T(8,128)(2,1)S(1)}, bf16[4,4,128,256]{3,2,1,0:T(8,128)(2,1)S(1)}, u32[]{:S(2)}, u32[]{:S(2)}) collective-permute-start(bf16[4,4,128,256]{3,2,1,0:T(8,128)(2,1)S(1)} %pad_maximum_fusion), channel_id=1, source_target_pairs={{0,8},{1,9},{2,10},{3,11},{4,12},{5,13},{6,14},{7,15},{8,0},{9,1},... | collective-permute-start | bytes 3145736 | tf_op jit(solution)/shard_map/ppermute | solution.py:340
  20.6 5.2 %collective-permute-start.13 = (bf16[384,128]{1,0:T(8,128)(2,1)S(1)}, bf16[384,128]{1,0:T(8,128)(2,1)S(1)}, u32[]{:S(2)}, u32[]{:S(2)}) collective-permute-start(bf16[384,128]{1,0:T(8,128)(2,1)S(1)} %get-tuple-element.47.refs_0_), channel_id=1, source_target_pairs={{0,1},{1,0},{2,3},{3,2},{4,5},{5,4},{6,7},{7,6},{8,9},{9,8},{10,11... | collective-permute-start | bytes 294920 | tf_op jit(solution)/shard_map/ppermute | solution.py:340
  22.2 5.6 %collective-permute-start.14 = (bf16[384,128]{1,0:T(8,128)(2,1)S(1)}, bf16[384,128]{1,0:T(8,128)(2,1)S(1)}, u32[]{:S(2)}, u32[]{:S(2)}) collective-permute-start(bf16[384,128]{1,0:T(8,128)(2,1)S(1)} %get-tuple-element.47.refs_0_), channel_id=1, source_target_pairs={{0,16},{1,17},{2,18},{3,19},{4,20},{5,21},{6,22},{7,23},{8,24},{9,... | collective-permute-start | bytes 294920 | tf_op jit(solution)/shard_map/ppermute | solution.py:340
  22.7 6.5 %collective-permute-start.15 = (bf16[384,128]{1,0:T(8,128)(2,1)S(1)}, bf16[384,128]{1,0:T(8,128)(2,1)S(1)}, u32[]{:S(2)}, u32[]{:S(2)}) collective-permute-start(bf16[384,128]{1,0:T(8,128)(2,1)S(1)} %get-tuple-element.47.refs_0_), channel_id=1, source_target_pairs={{0,17},{1,16},{2,19},{3,18},{4,21},{5,20},{6,23},{7,22},{8,25},{9,... | collective-permute-start | bytes 294920 | tf_op jit(solution)/shard_map/ppermute | solution.py:340
  24.1 9.6 %collective-permute-start.3 = (bf16[384,128]{1,0:T(8,128)(2,1)S(1)}, bf16[384,128]{1,0:T(8,128)(2,1)S(1)}, u32[]{:S(2)}, u32[]{:S(2)}) collective-permute-start(bf16[384,128]{1,0:T(8,128)(2,1)S(1)} %get-tuple-element.34.refs_0_), channel_id=1, source_target_pairs={{0,1},{1,0},{2,3},{3,2},{4,5},{5,4},{6,7},{7,6},{8,9},{9,8},{10,11... | collective-permute-start | bytes 294920 | tf_op jit(solution)/shard_map/ppermute | solution.py:340
  25.8 8.2 %collective-permute-start.4 = (bf16[384,128]{1,0:T(8,128)(2,1)S(1)}, bf16[384,128]{1,0:T(8,128)(2,1)S(1)}, u32[]{:S(2)}, u32[]{:S(2)}) collective-permute-start(bf16[384,128]{1,0:T(8,128)(2,1)S(1)} %get-tuple-element.34.refs_0_), channel_id=1, source_target_pairs={{0,16},{1,17},{2,18},{3,19},{4,20},{5,21},{6,22},{7,23},{8,24},{9,... | collective-permute-start | bytes 294920 | tf_op jit(solution)/shard_map/ppermute | solution.py:340
  27.8 6.1 %collective-permute-start.5 = (bf16[384,128]{1,0:T(8,128)(2,1)S(1)}, bf16[384,128]{1,0:T(8,128)(2,1)S(1)}, u32[]{:S(2)}, u32[]{:S(2)}) collective-permute-start(bf16[384,128]{1,0:T(8,128)(2,1)S(1)} %get-tuple-element.34.refs_0_), channel_id=1, source_target_pairs={{0,17},{1,16},{2,19},{3,18},{4,21},{5,20},{6,23},{7,22},{8,25},{9,... | collective-permute-start | bytes 294920 | tf_op jit(solution)/shard_map/ppermute | solution.py:340
  29.7 9.0 %collective-permute-start.16 = (bf16[128,256]{1,0:T(8,128)(2,1)S(1)}, bf16[128,256]{1,0:T(8,128)(2,1)S(1)}, u32[]{:S(2)}, u32[]{:S(2)}) collective-permute-start(bf16[128,256]{1,0:T(8,128)(2,1)S(1)} %get-tuple-element.49), channel_id=1, source_target_pairs={{0,4},{1,5},{2,6},{3,7},{4,0},{5,1},{6,2},{7,3},{8,12},{9,13},{10,... | collective-permute-start | bytes 196616 | tf_op jit(solution)/shard_map/ppermute | solution.py:340
  32.4 6.8 %collective-permute-start.17 = (bf16[128,256]{1,0:T(8,128)(2,1)S(1)}, bf16[128,256]{1,0:T(8,128)(2,1)S(1)}, u32[]{:S(2)}, u32[]{:S(2)}) collective-permute-start(bf16[128,256]{1,0:T(8,128)(2,1)S(1)} %get-tuple-element.50), channel_id=1, source_target_pairs={{0,6},{1,7},{2,4},{3,5},{4,2},{5,3},{6,0},{7,1},{8,14},{9,15},{10,... | collective-permute-start | bytes 196616 | tf_op jit(solution)/shard_map/ppermute | solution.py:340
  33.7 5.4 %collective-permute-start.18 = (bf16[128,256]{1,0:T(8,128)(2,1)S(1)}, bf16[128,256]{1,0:T(8,128)(2,1)S(1)}, u32[]{:S(2)}, u32[]{:S(2)}) collective-permute-start(bf16[128,256]{1,0:T(8,128)(2,1)S(1)} %get-tuple-element.51), channel_id=1, source_target_pairs={{0,2},{1,3},{2,0},{3,1},{4,6},{5,7},{6,4},{7,5},{8,10},{9,11},{10,... | collective-permute-start | bytes 196616 | tf_op jit(solution)/shard_map/ppermute | solution.py:340
  34.5 8.2 %collective-permute-start.10 = (bf16[128,256]{1,0:T(8,128)(2,1)S(1)}, bf16[128,256]{1,0:T(8,128)(2,1)S(1)}, u32[]{:S(2)}, u32[]{:S(2)}) collective-permute-start(bf16[128,256]{1,0:T(8,128)(2,1)S(1)} %get-tuple-element.44), channel_id=1, source_target_pairs={{0,4},{1,5},{2,6},{3,7},{4,0},{5,1},{6,2},{7,3},{8,12},{9,13},{10,... | collective-permute-start | bytes 196616 | tf_op jit(solution)/shard_map/ppermute | solution.py:340
  37.3 6.2 %collective-permute-start.11 = (bf16[128,256]{1,0:T(8,128)(2,1)S(1)}, bf16[128,256]{1,0:T(8,128)(2,1)S(1)}, u32[]{:S(2)}, u32[]{:S(2)}) collective-permute-start(bf16[128,256]{1,0:T(8,128)(2,1)S(1)} %get-tuple-element.45), channel_id=1, source_target_pairs={{0,6},{1,7},{2,4},{3,5},{4,2},{5,3},{6,0},{7,1},{8,14},{9,15},{10,... | collective-permute-start | bytes 196616 | tf_op jit(solution)/shard_map/ppermute | solution.py:340
  38.7 5.2 %collective-permute-start.12 = (bf16[128,256]{1,0:T(8,128)(2,1)S(1)}, bf16[128,256]{1,0:T(8,128)(2,1)S(1)}, u32[]{:S(2)}, u32[]{:S(2)}) collective-permute-start(bf16[128,256]{1,0:T(8,128)(2,1)S(1)} %get-tuple-element.46), channel_id=1, source_target_pairs={{0,2},{1,3},{2,0},{3,1},{4,6},{5,7},{6,4},{7,5},{8,10},{9,11},{10,... | collective-permute-start | bytes 196616 | tf_op jit(solution)/shard_map/ppermute | solution.py:340
  44.7 5.5 %collective-permute-start.19 = (f32[128,256]{1,0:T(8,128)S(1)}, f32[128,256]{1,0:T(8,128)S(1)}, u32[]{:S(2)}, u32[]{:S(2)}) collective-permute-start(f32[128,256]{1,0:T(8,128)S(1)} %get-tuple-element.54), channel_id=1, source_target_pairs={{0,8},{1,9},{2,10},{3,11},{4,12},{5,13},{6,14},{7,15},{8,0},{9,1},... | collective-permute-start | bytes 393224 | tf_op jit(solution)/shard_map/ppermute | solution.py:340
  44.8 5.4 %collective-permute-start.21 = (bf16[128,128]{1,0:T(8,128)(2,1)S(1)}, bf16[128,128]{1,0:T(8,128)(2,1)S(1)}, u32[]{:S(2)}, u32[]{:S(2)}) collective-permute-start(bf16[128,128]{1,0:T(8,128)(2,1)S(1)} %get-tuple-element.58), channel_id=1, source_target_pairs={{0,8},{1,9},{2,10},{3,11},{4,12},{5,13},{6,14},{7,15},{8,0},{9,1},... | collective-permute-start | bytes 98312 | tf_op jit(solution)/shard_map/ppermute | solution.py:340
  45.3 4.9 %collective-permute-start.20 = (bf16[128,128]{1,0:T(8,128)(2,1)S(1)}, bf16[128,128]{1,0:T(8,128)(2,1)S(1)}, u32[]{:S(2)}, u32[]{:S(2)}) collective-permute-start(bf16[128,128]{1,0:T(8,128)(2,1)S(1)} %get-tuple-element.57), channel_id=1, source_target_pairs={{0,8},{1,9},{2,10},{3,11},{4,12},{5,13},{6,14},{7,15},{8,0},{9,1},... | collective-permute-start | bytes 98312 | tf_op jit(solution)/shard_map/ppermute | solution.py:340
  45.3 11.8 %all-to-all-start = ((f32[32,1,128]{2,1,0:T(1,128)}), f32[32,1,128]{2,1,0:T(1,128)S(1)}, u32[]{:S(2)}, u32[]{:S(2)}) async-start(f32[32,1,128]{2,1,0:T(1,128)} %shard_map.82), calls=%async_computation | async-start | bytes 32768 | tf_op jit(solution)/shard_map/all_to_all | solution.py:369

commit v5 on v4

--- a/solution.py
+++ b/solution.py
@@ -259,7 +259,7 @@
 
 
 def rows_kernel(*refs):
-    mine, theirs = refs[-2:]
+    keys, (mine, theirs) = refs[4 * HALF : 5 * HALF], refs[-2:]
     core = position()[0]
     for h in range(HALF):
         keep, r1, r2, r3 = refs[4 * h : 4 * h + 4]
@@ -269,38 +269,39 @@
         cols = slice(h * HD, (h + 1) * HD)
         mine[:, cols] = jnp.where(core == 0, low, high)
         theirs[:, cols] = jnp.where(core == 0, high, low)
-
-
-def plane_rows(parts):
+        theirs[:, WIDE + h * HD : WIDE + (h + 1) * HD] = keys[h][...].astype(F32)
+
+
+def plane_rows(parts, keys):
     cols, both = parts[0].shape
     vmem = pl.BlockSpec(memory_space=pltpu.VMEM)
     return pl.pallas_call(
         rows_kernel,
-        in_specs=[vmem] * len(parts),
+        in_specs=[vmem] * (len(parts) + len(keys)),
         out_specs=[vmem] * 2,
-        out_shape=[jax.ShapeDtypeStruct((both // 2, WIDE), F32)] * 2,
+        out_shape=[jax.ShapeDtypeStruct((both // 2, n * WIDE), F32) for n in (1, 2)],
         compiler_params=params(),
         cost_estimate=cost(16 * cols * both, cols * both * 28),
-    )(*parts)
+    )(*parts, *keys)
 
 
 def join_kernel(mine, theirs, *refs):
-    keys_mine, keys_theirs, (out, key_out) = refs[:HALF], refs[HALF : 2 * HALF], refs[2 * HALF :]
+    keys, (out, key_out) = refs[:HALF], refs[HALF:]
     first = position()[0] == 0
-    out[:, :WIDE] = jnp.where(first, mine[...], theirs[...])
-    out[:, WIDE:] = jnp.where(first, theirs[...], mine[...])
-    for h in range(HALF):
-        own, far = keys_mine[h][...], keys_theirs[h][...]
-        key_out[0, :, h * HD : (h + 1) * HD] = jnp.where(first, own, far)
-        key_out[0, :, WIDE + h * HD : WIDE + (h + 1) * HD] = jnp.where(first, far, own)
-
-
-def join(mine, theirs, keys_mine, keys_theirs):
-    rows = keys_mine[0].shape[0]
+    rows, far = theirs[:, :WIDE], theirs[:, WIDE:].astype(BF16)
+    key = jnp.concatenate([k[...] for k in keys], axis=1)
+    out[:, :WIDE] = jnp.where(first, mine[...], rows)
+    out[:, WIDE:] = jnp.where(first, rows, mine[...])
+    key_out[0, :, :WIDE] = jnp.where(first, key, far)
+    key_out[0, :, WIDE:] = jnp.where(first, far, key)
+
+
+def join(mine, theirs, keys):
+    rows = keys[0].shape[0]
     vmem = pl.BlockSpec(memory_space=pltpu.VMEM)
     return pl.pallas_call(
         join_kernel,
-        in_specs=[vmem] * (2 + 2 * HALF),
+        in_specs=[vmem] * (2 + HALF),
         out_specs=[vmem] * 2,
         out_shape=[
             jax.ShapeDtypeStruct((mine.shape[0], KVH * HD), F32),
@@ -308,7 +309,7 @@
         ],
         compiler_params=params(),
         cost_estimate=cost(0, 12 * rows * KVH * HD),
-    )(mine, theirs, *keys_mine, *keys_theirs)
+    )(mine, theirs, *keys)
 
 
 def clip_kernel(squares, rows, out):
@@ -353,23 +354,23 @@
     to_send, mine = attention(True, doc_lengths, *near, BF16)
     theirs = swap(to_send, core_mask)
     pieces = merge(mine, theirs)
-    chips = [[piece] + [swap(piece, mask) for mask in masks[1:]] for piece in pieces]
     f_ready, _ = lax.optimization_barrier((f_same, pieces[0]))
-    far = swap(jnp.stack(f_ready), core_mask)
+    far, late = lax.optimization_barrier((swap(jnp.stack(f_ready), core_mask), pieces[1]))
     f_other = [far]
-
-    parts, keys_mine, keys_other = [], [], []
+    chips = [[piece] + [swap(piece, mask) for mask in masks[1:]] for piece in (pieces[0], late)]
+
+    parts, keys_mine, keys_send = [], [], []
     for h in range(HALF):
         *sends, keep, key_mine, key_send = weight(chips[h], f_same, f_other)
         parts += [keep] + [swap(sends[m], (m + 1) * z_mask) for m in (1, 2, 0)]
         keys_mine.append(key_mine)
-        keys_other.append(swap(key_send, core_mask))
+        keys_send.append(key_send)
     squares = plane_squares(parts, devices)
     parts[0], squares = lax.optimization_barrier((parts[0], squares))
     squares = lax.all_to_all(squares, AXES, 0, 0, tiled=True)
-    rows_mine, rows_send = plane_rows(parts)
+    rows_mine, rows_send = plane_rows(parts, keys_send)
     rows_other = swap(rows_send, core_mask)
-    rows, key_grad = join(rows_mine, rows_other, keys_mine, keys_other)
+    rows, key_grad = join(rows_mine, rows_other, keys_mine)
     return key_grad, clip(squares, rows)
 
 

time: 58.3 us -> 57.7 us (0.990)
  starting transfers between devices: 28.4 us -> 26.5 us
  waiting for transfers between devices: 16.5 us -> 17.8 us
    ppermute x20 -> x18, waiting for transfers between devices: 10.2 us -> 11.5 us  [swap(): return lax.ppermute(array, AXES, [(i, i ^ mask) for i in range(devices)])]
    ppermute x20 -> x18, starting transfers between devices: 20.5 us -> 19.3 us  [swap(): return lax.ppermute(array, AXES, [(i, i ^ mask) for i in range(devices)])]
    all_to_all x1, starting transfers between devices: 4.79 us -> 4.17 us  [planes(): squares = lax.all_to_all(squares, AXES, 0, 0, tiled=True)]
  transfers between devices with their start and end apart: 23 -> 21, of which waited for: 10 -> 8; matrix products, arithmetic and copies ran while one was open for 0% -> 0% of each run, Pallas kernels for 13% -> 13%
where the time goes in v5:
time: 57.7 us; the launch traced here: 57.5 us
  starting transfers between devices  26.5 us (46%)
  waiting for transfers between devices  17.8 us (31%)
  Pallas kernels  9.42 us (16%)
  local copies, waits for them, and re-layouts  2.81 us (5%)
  between operations  0.76 us (1%)
    ppermute x18, starting transfers between devices, swap(): return lax.ppermute(array, AXES, [(i, i ^ mask) for i in range(devices)])  19.3 us
    ppermute x18, waiting for transfers between devices, swap(): return lax.ppermute(array, AXES, [(i, i ^ mask) for i in range(devices)])  11.5 us
    all_to_all x1, waiting for transfers between devices, planes(): squares = lax.all_to_all(squares, AXES, 0, 0, tiled=True)  6.34 us
    pallas_call x1, Pallas kernels, attention(): pl.pallas_call(functools.partial(attention_kernel, turn), in_specs=[pl.Bl...  5.76 us
    all_to_all x1, starting transfers between devices, planes(): squares = lax.all_to_all(squares, AXES, 0, 0, tiled=True)  4.17 us
    unnamed x8, local copies, waits for them, and re-layouts  2.81 us
    ppermute x1, starting transfers between devices, planes(): v_prev = lax.ppermute(v_own, 'seq', following)  2.6 us
  transfers between devices with their start and end apart: 21, of which 8 were waited for; matrix products, arithmetic and copies ran while one was open for 0% of the time, Pallas kernels for 13%

profile of v5, /device:TPU:0, one launch (start us, length us, event | category | flops | bytes accessed | tf_op | source)
XLA Modules:
  0.0 57.5 jit_solution(2177882842947396699)
XLA Ops:
  0.6 0.5 collective-permute-start
  1.1 2.6 %collective-permute-start.1 = (bf16[128,512]{1,0:T(8,128)(2,1)}, bf16[128,512]{1,0:T(8,128)(2,1)S(1)}, u32[]{:S(2)}, u32[]{:S(2)}) collective-permute-start(bf16[128,512]{1,0:T(8,128)(2,1)} %bitcast.18), channel_id=1, source_target_pairs={{0,8},{8,16},{16,24},{24,0},{1,9},{9,17},{17,25},{25,1},{2,10},{10... | collective-permute-start | bytes 393224 | tf_op jit(solution)/shard_map/ppermute | solution.py:347
  3.7 0.0 copy-start
  3.7 1.2 %copy-done = bf16[1,128,4096]{2,1,0:T(8,128)(2,1)S(1)} copy-done((bf16[1,128,4096]{2,1,0:T(8,128)(2,1)S(1)}, bf16[1,128,4096]{2,1,0:T(8,128)(2,1)}, u32[]{:S(2)}) %copy-start) | copy-done | bytes 1048600
  5.0 0.3 shard_map.79
  5.2 1.6 %collective-permute-start.6 = (bf16[4,128,256]{2,1,0:T(8,128)(2,1)S(1)}, bf16[4,128,256]{2,1,0:T(8,128)(2,1)S(1)}, u32[]{:S(2)}, u32[]{:S(2)}) collective-permute-start(bf16[4,128,256]{2,1,0:T(8,128)(2,1)S(1)} %get-tuple-element.38), channel_id=1, source_target_pairs={{0,1},{1,0},{2,3},{3,2},{4,5},{5,4},{6,7},{7,6},{8,9},{9,8},{10,11... | collective-permute-start | bytes 786440 | tf_op jit(solution)/shard_map/ppermute | solution.py:341
  6.8 0.5 collective-permute-start.7
  7.4 1.4 %collective-permute-start.8 = (bf16[4,128,256]{2,1,0:T(8,128)(2,1)S(1)}, bf16[4,128,256]{2,1,0:T(8,128)(2,1)S(1)}, u32[]{:S(2)}, u32[]{:S(2)}) collective-permute-start(bf16[4,128,256]{2,1,0:T(8,128)(2,1)S(1)} %get-tuple-element.40), channel_id=1, source_target_pairs={{0,17},{1,16},{2,19},{3,18},{4,21},{5,20},{6,23},{7,22},{8,25},{9,... | collective-permute-start | bytes 786440 | tf_op jit(solution)/shard_map/ppermute | solution.py:341
  8.8 0.0 collective-permute-done.k_prev
  8.8 0.0 copy-start.2
  8.8 0.0 collective-permute-done.1.v_prev
  8.8 0.0 copy-start.3
  8.8 0.6 %copy-done.2 = bf16[128,512]{1,0:T(8,128)(2,1)} copy-done((bf16[128,512]{1,0:T(8,128)(2,1)}, bf16[128,512]{1,0:T(8,128)(2,1)S(1)}, u32[]{:S(2)}) %copy-start.2) | copy-done | bytes 131096
  9.4 0.0 copy-done.3
  9.5 5.8 %shard_map.77 = (bf16[2,256,128]{2,1,0:T(8,128)(2,1)}, bf16[2,256,128]{2,1,0:T(8,128)(2,1)}) custom-call(s32[1,8]{1,0:T(1,128)} %lengths.1, bf16[128,4096]{1,0:T(8,128)(2,1)} %bitcast.14, bf16[128,4096]{1,0:T(8,128)(2,1)} %bitcast.15, bf16[128,512]{1,0:T(8,128)(2,1)} %copy-done.2, bf16[128,512]{1,0:T(8,128)(2,1)} %bitcast.17, bf16[128,512]{1,0:T(8,128)(2,1)} %copy-done.3, ...), custom_call_target="tpu_custom_call" | custom-call | flops 805306368 | bytes 2097152 | tf_op jit(solution)/shard_map/pallas_call | solution.py:109
  15.3 0.1 collective-permute-start.2
  15.3 1.5 %collective-permute-done.2.theirs = bf16[2,256,128]{2,1,0:T(8,128)(2,1)S(1)} collective-permute-done((bf16[2,256,128]{2,1,0:T(8,128)(2,1)}, bf16[2,256,128]{2,1,0:T(8,128)(2,1)S(1)}, u32[]{:S(2)}, u32[]{:S(2)}) %collective-permute-start.2) | collective-permute-done | bytes 131104 | tf_op jit(solution)/shard_map/ppermute | solution.py:341
  16.9 0.0 copy-start.1
  16.9 0.9 %copy-done.1 = bf16[2,256,128]{2,1,0:T(8,128)(2,1)S(1)} copy-done((bf16[2,256,128]{2,1,0:T(8,128)(2,1)S(1)}, bf16[2,256,128]{2,1,0:T(8,128)(2,1)}, u32[]{:S(2)}) %copy-start.1) | copy-done | bytes 131096
  17.8 0.0 collective-permute-done.6.refs_5_
  17.8 0.0 collective-permute-done.7.refs_6_
  17.8 2.5 %collective-permute-done.8.refs_7_ = bf16[4,128,256]{2,1,0:T(8,128)(2,1)S(1)} collective-permute-done((bf16[4,128,256]{2,1,0:T(8,128)(2,1)S(1)}, bf16[4,128,256]{2,1,0:T(8,128)(2,1)S(1)}, u32[]{:S(2)}, u32[]{:S(2)}) %collective-permute-start.8) | collective-permute-done | bytes 262176 | tf_op jit(solution)/shard_map/ppermute | solution.py:341
  20.4 0.1 pad_maximum_fusion
  20.5 0.1 collective-permute-start.9
  20.6 1.6 %collective-permute-start.3 = (bf16[384,128]{1,0:T(8,128)(2,1)S(1)}, bf16[384,128]{1,0:T(8,128)(2,1)S(1)}, u32[]{:S(2)}, u32[]{:S(2)}) collective-permute-start(bf16[384,128]{1,0:T(8,128)(2,1)S(1)} %get-tuple-element.36.refs_0_), channel_id=1, source_target_pairs={{0,1},{1,0},{2,3},{3,2},{4,5},{5,4},{6,7},{7,6},{8,9},{9,8},{10,11... | collective-permute-start | bytes 294920 | tf_op jit(solution)/shard_map/ppermute | solution.py:341
  22.2 0.5 collective-permute-start.4
  22.7 1.4 %collective-permute-start.5 = (bf16[384,128]{1,0:T(8,128)(2,1)S(1)}, bf16[384,128]{1,0:T(8,128)(2,1)S(1)}, u32[]{:S(2)}, u32[]{:S(2)}) collective-permute-start(bf16[384,128]{1,0:T(8,128)(2,1)S(1)} %get-tuple-element.36.refs_0_), channel_id=1, source_target_pairs={{0,17},{1,16},{2,19},{3,18},{4,21},{5,20},{6,23},{7,22},{8,25},{9,... | collective-permute-start | bytes 294920 | tf_op jit(solution)/shard_map/ppermute | solution.py:341
  24.1 0.0 collective-permute-done.9.refs_8_
  24.1 1.5 %collective-permute-start.13 = (bf16[384,128]{1,0:T(8,128)(2,1)S(1)}, bf16[384,128]{1,0:T(8,128)(2,1)S(1)}, u32[]{:S(2)}, u32[]{:S(2)}) collective-permute-start(bf16[384,128]{1,0:T(8,128)(2,1)S(1)} %get-tuple-element.51.refs_0_), channel_id=1, source_target_pairs={{0,1},{1,0},{2,3},{3,2},{4,5},{5,4},{6,7},{7,6},{8,9},{9,8},{10,11... | collective-permute-start | bytes 294920 | tf_op jit(solution)/shard_map/ppermute | solution.py:341
  25.7 0.5 collective-permute-start.14
  26.2 0.0 collective-permute-done.3.refs_1_
  26.2 1.4 %collective-permute-start.15 = (bf16[384,128]{1,0:T(8,128)(2,1)S(1)}, bf16[384,128]{1,0:T(8,128)(2,1)S(1)}, u32[]{:S(2)}, u32[]{:S(2)}) collective-permute-start(bf16[384,128]{1,0:T(8,128)(2,1)S(1)} %get-tuple-element.51.refs_0_), channel_id=1, source_target_pairs={{0,17},{1,16},{2,19},{3,18},{4,21},{5,20},{6,23},{7,22},{8,25},{9,... | collective-permute-start | bytes 294920 | tf_op jit(solution)/shard_map/ppermute | solution.py:341
  27.6 0.2 collective-permute-done.4.refs_2_
  27.8 2.0 %collective-permute-done.5.refs_3_ = bf16[384,128]{1,0:T(8,128)(2,1)S(1)} collective-permute-done((bf16[384,128]{1,0:T(8,128)(2,1)S(1)}, bf16[384,128]{1,0:T(8,128)(2,1)S(1)}, u32[]{:S(2)}, u32[]{:S(2)}) %collective-permute-start.5) | collective-permute-done | bytes 98336 | tf_op jit(solution)/shard_map/ppermute | solution.py:341
  29.9 0.5 shard_map.80
  30.4 2.7 %collective-permute-start.10 = (bf16[128,256]{1,0:T(8,128)(2,1)S(1)}, bf16[128,256]{1,0:T(8,128)(2,1)S(1)}, u32[]{:S(2)}, u32[]{:S(2)}) collective-permute-start(bf16[128,256]{1,0:T(8,128)(2,1)S(1)} %get-tuple-element.48), channel_id=1, source_target_pairs={{0,4},{1,5},{2,6},{3,7},{4,0},{5,1},{6,2},{7,3},{8,12},{9,13},{10,... | collective-permute-start | bytes 196616 | tf_op jit(solution)/shard_map/ppermute | solution.py:341
  33.0 1.3 %collective-permute-start.11 = (bf16[128,256]{1,0:T(8,128)(2,1)S(1)}, bf16[128,256]{1,0:T(8,128)(2,1)S(1)}, u32[]{:S(2)}, u32[]{:S(2)}) collective-permute-start(bf16[128,256]{1,0:T(8,128)(2,1)S(1)} %get-tuple-element.49), channel_id=1, source_target_pairs={{0,6},{1,7},{2,4},{3,5},{4,2},{5,3},{6,0},{7,1},{8,14},{9,15},{10,... | collective-permute-start | bytes 196616 | tf_op jit(solution)/shard_map/ppermute | solution.py:341
  34.4 0.0 collective-permute-done.13.refs_1_
  34.4 0.2 collective-permute-start.12
  34.6 0.0 collective-permute-done.14.refs_2_
  34.6 0.0 collective-permute-done.15.refs_3_
  34.6 0.5 shard_map.81
  35.1 2.9 %collective-permute-start.16 = (bf16[128,256]{1,0:T(8,128)(2,1)S(1)}, bf16[128,256]{1,0:T(8,128)(2,1)S(1)}, u32[]{:S(2)}, u32[]{:S(2)}) collective-permute-start(bf16[128,256]{1,0:T(8,128)(2,1)S(1)} %get-tuple-element.53), channel_id=1, source_target_pairs={{0,4},{1,5},{2,6},{3,7},{4,0},{5,1},{6,2},{7,3},{8,12},{9,13},{10,... | collective-permute-start | bytes 196616 | tf_op jit(solution)/shard_map/ppermute | solution.py:341
  38.0 1.3 %collective-permute-start.17 = (bf16[128,256]{1,0:T(8,128)(2,1)S(1)}, bf16[128,256]{1,0:T(8,128)(2,1)S(1)}, u32[]{:S(2)}, u32[]{:S(2)}) collective-permute-start(bf16[128,256]{1,0:T(8,128)(2,1)S(1)} %get-tuple-element.54), channel_id=1, source_target_pairs={{0,6},{1,7},{2,4},{3,5},{4,2},{5,3},{6,0},{7,1},{8,14},{9,15},{10,... | collective-permute-start | bytes 196616 | tf_op jit(solution)/shard_map/ppermute | solution.py:341
  39.3 0.0 collective-permute-done.10.refs_1_
  39.3 0.0 collective-permute-start.18
  39.3 0.0 collective-permute-done.11.refs_2_
  39.4 0.0 collective-permute-done.12.refs_3_
  39.4 3.9 %collective-permute-done.16.refs_5_ = bf16[128,256]{1,0:T(8,128)(2,1)S(1)} collective-permute-done((bf16[128,256]{1,0:T(8,128)(2,1)S(1)}, bf16[128,256]{1,0:T(8,128)(2,1)S(1)}, u32[]{:S(2)}, u32[]{:S(2)}) %collective-permute-start.16) | collective-permute-done | bytes 65568 | tf_op jit(solution)/shard_map/ppermute | solution.py:341
  43.3 0.9 %collective-permute-done.17.refs_6_ = bf16[128,256]{1,0:T(8,128)(2,1)S(1)} collective-permute-done((bf16[128,256]{1,0:T(8,128)(2,1)S(1)}, bf16[128,256]{1,0:T(8,128)(2,1)S(1)}, u32[]{:S(2)}, u32[]{:S(2)}) %collective-permute-start.17) | collective-permute-done | bytes 65568 | tf_op jit(solution)/shard_map/ppermute | solution.py:341
  44.2 0.3 collective-permute-done.18.refs_7_
  44.5 0.7 %shard_map.82 = f32[32,1,128]{2,1,0:T(1,128)} custom-call(f32[128,256]{1,0:T(8,128)S(1)} %get-tuple-element.56.refs_0_, bf16[128,256]{1,0:T(8,128)(2,1)S(1)} %collective-permute-done.10.refs_1_, bf16[128,256]{1,0:T(8,128)(2,1)S(1)} %collective-permute-done.11.refs_2_, bf16[128,256]{1,0:T(8,128)(2,1)S(1)} %collective-permute-done.12.refs_3_, ...), custom_call_target="tpu_custom_call" | custom-call | flops 524288 | bytes 655360 | tf_op jit(solution)/shard_map/pallas_call | solution.py:251
  45.2 0.1 shard_map.83
  45.3 0.1 collective-permute-start.19
  45.4 4.2 %all-to-all-start = ((f32[32,1,128]{2,1,0:T(1,128)}), f32[32,1,128]{2,1,0:T(1,128)S(1)}, u32[]{:S(2)}, u32[]{:S(2)}) async-start(f32[32,1,128]{2,1,0:T(1,128)} %shard_map.82), calls=%async_computation | async-start | bytes 32768 | tf_op jit(solution)/shard_map/all_to_all | solution.py:370
  49.6 0.0 collective-permute-done.19.theirs
  49.6 0.7 %shard_map.84 = (f32[128,512]{1,0:T(8,128)S(1)}, bf16[1,128,512]{2,1,0:T(8,128)(2,1)}) custom-call(f32[128,256]{1,0:T(8,128)S(1)} %get-tuple-element.59.mine, f32[128,512]{1,0:T(8,128)S(1)} %collective-permute-done.19.theirs, bf16[128,128]{1,0:T(8,128)(2,1)S(1)} %get-tuple-element.61.refs_0_, bf16[128,128]{1,0:T(8,128)(2,1)S(1)} %get-tuple-element.62.refs_1_), custom_call_target="tpu_custom_call" | custom-call | bytes 786432 | tf_op jit(solution)/shard_map/pallas_call | solution.py:302
  50.3 6.3 %all-to-all-done.squares = f32[32,1,128]{2,1,0:T(1,128)S(1)} async-done(((f32[32,1,128]{2,1,0:T(1,128)}), f32[32,1,128]{2,1,0:T(1,128)S(1)}, u32[]{:S(2)}, u32[]{:S(2)}) %all-to-all-start) | async-done | bytes 16416 | tf_op jit(solution)/shard_map/all_to_all | solution.py:370
  56.6 0.8 %shard_map.85 = f32[128,512]{1,0:T(8,128)} custom-call(f32[32,1,128]{2,1,0:T(1,128)S(1)} %all-to-all-done.squares, f32[128,512]{1,0:T(8,128)S(1)} %get-tuple-element.65.rows), custom_call_target="tpu_custom_call" | custom-call | flops 65536 | bytes 524288 | tf_op jit(solution)/shard_map/pallas_call | solution.py:324
  (1 shorter events, 0.0 us)
Async XLA Ops:
  0.6 8.2 %collective-permute-start = (bf16[128,512]{1,0:T(8,128)(2,1)}, bf16[128,512]{1,0:T(8,128)(2,1)S(1)}, u32[]{:S(2)}, u32[]{:S(2)}) collective-permute-start(bf16[128,512]{1,0:T(8,128)(2,1)} %bitcast.16), channel_id=1, source_target_pairs={{0,8},{8,16},{16,24},{24,0},{1,9},{9,17},{17,25},{25,1},{2,10},{10... | collective-permute-start | bytes 393224 | tf_op jit(solution)/shard_map/ppermute | solution.py:346
  1.1 7.7 %collective-permute-start.1 = (bf16[128,512]{1,0:T(8,128)(2,1)}, bf16[128,512]{1,0:T(8,128)(2,1)S(1)}, u32[]{:S(2)}, u32[]{:S(2)}) collective-permute-start(bf16[128,512]{1,0:T(8,128)(2,1)} %bitcast.18), channel_id=1, source_target_pairs={{0,8},{8,16},{16,24},{24,0},{1,9},{9,17},{17,25},{25,1},{2,10},{10... | collective-permute-start | bytes 393224 | tf_op jit(solution)/shard_map/ppermute | solution.py:347
  3.7 1.2 %copy-start = (bf16[1,128,4096]{2,1,0:T(8,128)(2,1)S(1)}, bf16[1,128,4096]{2,1,0:T(8,128)(2,1)}, u32[]{:S(2)}) copy-start(bf16[1,128,4096]{2,1,0:T(8,128)(2,1)} %param.10) | copy-start | bytes 3145732
  5.2 12.6 %collective-permute-start.6 = (bf16[4,128,256]{2,1,0:T(8,128)(2,1)S(1)}, bf16[4,128,256]{2,1,0:T(8,128)(2,1)S(1)}, u32[]{:S(2)}, u32[]{:S(2)}) collective-permute-start(bf16[4,128,256]{2,1,0:T(8,128)(2,1)S(1)} %get-tuple-element.38), channel_id=1, source_target_pairs={{0,1},{1,0},{2,3},{3,2},{4,5},{5,4},{6,7},{7,6},{8,9},{9,8},{10,11... | collective-permute-start | bytes 786440 | tf_op jit(solution)/shard_map/ppermute | solution.py:341
  6.8 11.0 %collective-permute-start.7 = (bf16[4,128,256]{2,1,0:T(8,128)(2,1)S(1)}, bf16[4,128,256]{2,1,0:T(8,128)(2,1)S(1)}, u32[]{:S(2)}, u32[]{:S(2)}) collective-permute-start(bf16[4,128,256]{2,1,0:T(8,128)(2,1)S(1)} %get-tuple-element.39), channel_id=1, source_target_pairs={{0,16},{1,17},{2,18},{3,19},{4,20},{5,21},{6,22},{7,23},{8,24},{9,... | collective-permute-start | bytes 786440 | tf_op jit(solution)/shard_map/ppermute | solution.py:341
  7.4 13.0 %collective-permute-start.8 = (bf16[4,128,256]{2,1,0:T(8,128)(2,1)S(1)}, bf16[4,128,256]{2,1,0:T(8,128)(2,1)S(1)}, u32[]{:S(2)}, u32[]{:S(2)}) collective-permute-start(bf16[4,128,256]{2,1,0:T(8,128)(2,1)S(1)} %get-tuple-element.40), channel_id=1, source_target_pairs={{0,17},{1,16},{2,19},{3,18},{4,21},{5,20},{6,23},{7,22},{8,25},{9,... | collective-permute-start | bytes 786440 | tf_op jit(solution)/shard_map/ppermute | solution.py:341
  8.8 0.7 %copy-start.2 = (bf16[128,512]{1,0:T(8,128)(2,1)}, bf16[128,512]{1,0:T(8,128)(2,1)S(1)}, u32[]{:S(2)}) copy-start(bf16[128,512]{1,0:T(8,128)(2,1)S(1)} %collective-permute-done.k_prev) | copy-start | bytes 393220
  8.8 0.7 %copy-start.3 = (bf16[128,512]{1,0:T(8,128)(2,1)}, bf16[128,512]{1,0:T(8,128)(2,1)S(1)}, u32[]{:S(2)}) copy-start(bf16[128,512]{1,0:T(8,128)(2,1)S(1)} %collective-permute-done.1.v_prev) | copy-start | bytes 393220
  15.3 1.6 %collective-permute-start.2 = (bf16[2,256,128]{2,1,0:T(8,128)(2,1)}, bf16[2,256,128]{2,1,0:T(8,128)(2,1)S(1)}, u32[]{:S(2)}, u32[]{:S(2)}) collective-permute-start(bf16[2,256,128]{2,1,0:T(8,128)(2,1)} %get-tuple-element.35), channel_id=1, source_target_pairs={{0,8},{1,9},{2,10},{3,11},{4,12},{5,13},{6,14},{7,15},{8,0},{9,1},... | collective-permute-start | bytes 393224 | tf_op jit(solution)/shard_map/ppermute | solution.py:341
  16.9 0.9 %copy-start.1 = (bf16[2,256,128]{2,1,0:T(8,128)(2,1)S(1)}, bf16[2,256,128]{2,1,0:T(8,128)(2,1)}, u32[]{:S(2)}) copy-start(bf16[2,256,128]{2,1,0:T(8,128)(2,1)} %get-tuple-element.34.mine) | copy-start | bytes 393220
  20.5 3.6 %collective-permute-start.9 = (bf16[4,4,128,256]{3,2,1,0:T(8,128)(2,1)S(1)}, bf16[4,4,128,256]{3,2,1,0:T(8,128)(2,1)S(1)}, u32[]{:S(2)}, u32[]{:S(2)}) collective-permute-start(bf16[4,4,128,256]{3,2,1,0:T(8,128)(2,1)S(1)} %pad_maximum_fusion), channel_id=1, source_target_pairs={{0,8},{1,9},{2,10},{3,11},{4,12},{5,13},{6,14},{7,15},{8,0},{9,1},... | collective-permute-start | bytes 3145736 | tf_op jit(solution)/shard_map/ppermute | solution.py:341
  20.6 5.6 %collective-permute-start.3 = (bf16[384,128]{1,0:T(8,128)(2,1)S(1)}, bf16[384,128]{1,0:T(8,128)(2,1)S(1)}, u32[]{:S(2)}, u32[]{:S(2)}) collective-permute-start(bf16[384,128]{1,0:T(8,128)(2,1)S(1)} %get-tuple-element.36.refs_0_), channel_id=1, source_target_pairs={{0,1},{1,0},{2,3},{3,2},{4,5},{5,4},{6,7},{7,6},{8,9},{9,8},{10,11... | collective-permute-start | bytes 294920 | tf_op jit(solution)/shard_map/ppermute | solution.py:341
  22.2 5.6 %collective-permute-start.4 = (bf16[384,128]{1,0:T(8,128)(2,1)S(1)}, bf16[384,128]{1,0:T(8,128)(2,1)S(1)}, u32[]{:S(2)}, u32[]{:S(2)}) collective-permute-start(bf16[384,128]{1,0:T(8,128)(2,1)S(1)} %get-tuple-element.36.refs_0_), channel_id=1, source_target_pairs={{0,16},{1,17},{2,18},{3,19},{4,20},{5,21},{6,22},{7,23},{8,24},{9,... | collective-permute-start | bytes 294920 | tf_op jit(solution)/shard_map/ppermute | solution.py:341
  22.7 7.2 %collective-permute-start.5 = (bf16[384,128]{1,0:T(8,128)(2,1)S(1)}, bf16[384,128]{1,0:T(8,128)(2,1)S(1)}, u32[]{:S(2)}, u32[]{:S(2)}) collective-permute-start(bf16[384,128]{1,0:T(8,128)(2,1)S(1)} %get-tuple-element.36.refs_0_), channel_id=1, source_target_pairs={{0,17},{1,16},{2,19},{3,18},{4,21},{5,20},{6,23},{7,22},{8,25},{9,... | collective-permute-start | bytes 294920 | tf_op jit(solution)/shard_map/ppermute | solution.py:341
  24.1 10.2 %collective-permute-start.13 = (bf16[384,128]{1,0:T(8,128)(2,1)S(1)}, bf16[384,128]{1,0:T(8,128)(2,1)S(1)}, u32[]{:S(2)}, u32[]{:S(2)}) collective-permute-start(bf16[384,128]{1,0:T(8,128)(2,1)S(1)} %get-tuple-element.51.refs_0_), channel_id=1, source_target_pairs={{0,1},{1,0},{2,3},{3,2},{4,5},{5,4},{6,7},{7,6},{8,9},{9,8},{10,11... | collective-permute-start | bytes 294920 | tf_op jit(solution)/shard_map/ppermute | solution.py:341
  25.7 8.9 %collective-permute-start.14 = (bf16[384,128]{1,0:T(8,128)(2,1)S(1)}, bf16[384,128]{1,0:T(8,128)(2,1)S(1)}, u32[]{:S(2)}, u32[]{:S(2)}) collective-permute-start(bf16[384,128]{1,0:T(8,128)(2,1)S(1)} %get-tuple-element.51.refs_0_), channel_id=1, source_target_pairs={{0,16},{1,17},{2,18},{3,19},{4,20},{5,21},{6,22},{7,23},{8,24},{9,... | collective-permute-start | bytes 294920 | tf_op jit(solution)/shard_map/ppermute | solution.py:341
  26.2 8.4 %collective-permute-start.15 = (bf16[384,128]{1,0:T(8,128)(2,1)S(1)}, bf16[384,128]{1,0:T(8,128)(2,1)S(1)}, u32[]{:S(2)}, u32[]{:S(2)}) collective-permute-start(bf16[384,128]{1,0:T(8,128)(2,1)S(1)} %get-tuple-element.51.refs_0_), channel_id=1, source_target_pairs={{0,17},{1,16},{2,19},{3,18},{4,21},{5,20},{6,23},{7,22},{8,25},{9,... | collective-permute-start | bytes 294920 | tf_op jit(solution)/shard_map/ppermute | solution.py:341
  30.4 9.0 %collective-permute-start.10 = (bf16[128,256]{1,0:T(8,128)(2,1)S(1)}, bf16[128,256]{1,0:T(8,128)(2,1)S(1)}, u32[]{:S(2)}, u32[]{:S(2)}) collective-permute-start(bf16[128,256]{1,0:T(8,128)(2,1)S(1)} %get-tuple-element.48), channel_id=1, source_target_pairs={{0,4},{1,5},{2,6},{3,7},{4,0},{5,1},{6,2},{7,3},{8,12},{9,13},{10,... | collective-permute-start | bytes 196616 | tf_op jit(solution)/shard_map/ppermute | solution.py:341
  33.0 6.3 %collective-permute-start.11 = (bf16[128,256]{1,0:T(8,128)(2,1)S(1)}, bf16[128,256]{1,0:T(8,128)(2,1)S(1)}, u32[]{:S(2)}, u32[]{:S(2)}) collective-permute-start(bf16[128,256]{1,0:T(8,128)(2,1)S(1)} %get-tuple-element.49), channel_id=1, source_target_pairs={{0,6},{1,7},{2,4},{3,5},{4,2},{5,3},{6,0},{7,1},{8,14},{9,15},{10,... | collective-permute-start | bytes 196616 | tf_op jit(solution)/shard_map/ppermute | solution.py:341
  34.4 5.0 %collective-permute-start.12 = (bf16[128,256]{1,0:T(8,128)(2,1)S(1)}, bf16[128,256]{1,0:T(8,128)(2,1)S(1)}, u32[]{:S(2)}, u32[]{:S(2)}) collective-permute-start(bf16[128,256]{1,0:T(8,128)(2,1)S(1)} %get-tuple-element.50), channel_id=1, source_target_pairs={{0,2},{1,3},{2,0},{3,1},{4,6},{5,7},{6,4},{7,5},{8,10},{9,11},{10,... | collective-permute-start | bytes 196616 | tf_op jit(solution)/shard_map/ppermute | solution.py:341
  35.1 8.2 %collective-permute-start.16 = (bf16[128,256]{1,0:T(8,128)(2,1)S(1)}, bf16[128,256]{1,0:T(8,128)(2,1)S(1)}, u32[]{:S(2)}, u32[]{:S(2)}) collective-permute-start(bf16[128,256]{1,0:T(8,128)(2,1)S(1)} %get-tuple-element.53), channel_id=1, source_target_pairs={{0,4},{1,5},{2,6},{3,7},{4,0},{5,1},{6,2},{7,3},{8,12},{9,13},{10,... | collective-permute-start | bytes 196616 | tf_op jit(solution)/shard_map/ppermute | solution.py:341
  38.0 6.2 %collective-permute-start.17 = (bf16[128,256]{1,0:T(8,128)(2,1)S(1)}, bf16[128,256]{1,0:T(8,128)(2,1)S(1)}, u32[]{:S(2)}, u32[]{:S(2)}) collective-permute-start(bf16[128,256]{1,0:T(8,128)(2,1)S(1)} %get-tuple-element.54), channel_id=1, source_target_pairs={{0,6},{1,7},{2,4},{3,5},{4,2},{5,3},{6,0},{7,1},{8,14},{9,15},{10,... | collective-permute-start | bytes 196616 | tf_op jit(solution)/shard_map/ppermute | solution.py:341
  39.3 5.2 %collective-permute-start.18 = (bf16[128,256]{1,0:T(8,128)(2,1)S(1)}, bf16[128,256]{1,0:T(8,128)(2,1)S(1)}, u32[]{:S(2)}, u32[]{:S(2)}) collective-permute-start(bf16[128,256]{1,0:T(8,128)(2,1)S(1)} %get-tuple-element.55), channel_id=1, source_target_pairs={{0,2},{1,3},{2,0},{3,1},{4,6},{5,7},{6,4},{7,5},{8,10},{9,11},{10,... | collective-permute-start | bytes 196616 | tf_op jit(solution)/shard_map/ppermute | solution.py:341
  45.3 4.3 %collective-permute-start.19 = (f32[128,512]{1,0:T(8,128)S(1)}, f32[128,512]{1,0:T(8,128)S(1)}, u32[]{:S(2)}, u32[]{:S(2)}) collective-permute-start(f32[128,512]{1,0:T(8,128)S(1)} %get-tuple-element.60), channel_id=1, source_target_pairs={{0,8},{1,9},{2,10},{3,11},{4,12},{5,13},{6,14},{7,15},{8,0},{9,1},... | collective-permute-start | bytes 786440 | tf_op jit(solution)/shard_map/ppermute | solution.py:341
  45.4 11.2 %all-to-all-start = ((f32[32,1,128]{2,1,0:T(1,128)}), f32[32,1,128]{2,1,0:T(1,128)S(1)}, u32[]{:S(2)}, u32[]{:S(2)}) async-start(f32[32,1,128]{2,1,0:T(1,128)} %shard_map.82), calls=%async_computation | async-start | bytes 32768 | tf_op jit(solution)/shard_map/all_to_all | solution.py:370

commit v6 on v5

--- a/solution.py
+++ b/solution.py
@@ -19,6 +19,8 @@
 F32 = jnp.float32
 BF16 = jnp.bfloat16
 CORES = 2
+ORDER = ((0, 2, 1, 3), (0, 2, 1, 3))
+SUMS = ((1, 2, 0), (1, 2, 0))
 HALF = KVH // CORES
 WIDE = HALF * HD
 
@@ -186,8 +188,8 @@
     )(mine, theirs)
 
 
-def weight_kernel(nz, *refs):
-    chips = (refs[0], refs[1], refs[2], refs[3])
+def weight_kernel(nz, order, *refs):
+    chips = [refs[order.index(m)] for m in range(4)]
     f_same = (refs[4], refs[5], refs[6], refs[7])
     f_other = [refs[8].at[m] for m in range(4)]
     sends, (keep, key_mine, key_theirs, same, other) = refs[9 : 8 + nz], refs[8 + nz :]
@@ -215,7 +217,7 @@
             sends[m - 1][...] = product.astype(BF16)
 
 
-def weight(chips, f_same, f_other):
+def weight(order, chips, f_same, f_other):
     rows = chips[0].shape[0] // 3
     nz = f_same[0].shape[0]
     vmem = pl.BlockSpec(memory_space=pltpu.VMEM)
@@ -223,14 +225,14 @@
     shapes = [jax.ShapeDtypeStruct(square, BF16)] * (nz - 1)
     shapes += [jax.ShapeDtypeStruct(square, F32)] + [jax.ShapeDtypeStruct((rows, HD), BF16)] * 2
     return pl.pallas_call(
-        functools.partial(weight_kernel, nz),
+        functools.partial(weight_kernel, nz, order),
         in_specs=[vmem] * 9,
         out_specs=[vmem] * len(shapes),
         out_shape=shapes,
         scratch_shapes=[pltpu.VMEM((4 * rows, HD), BF16)] * 2,
         compiler_params=params(),
         cost_estimate=cost(2 * 8 * rows * HD * 4 * WIDE, 4 << 20),
-    )(*[chips[m] for m in (0, 1, 2, 3)], *[f_same[m] for m in (0, 1, 2, 3)], *f_other)
+    )(*[chips[m] for m in order], *[f_same[m] for m in (0, 1, 2, 3)], *f_other)
 
 
 def squares_kernel(*refs):
@@ -361,8 +363,8 @@
 
     parts, keys_mine, keys_send = [], [], []
     for h in range(HALF):
-        *sends, keep, key_mine, key_send = weight(chips[h], f_same, f_other)
-        parts += [keep] + [swap(sends[m], (m + 1) * z_mask) for m in (1, 2, 0)]
+        *sends, keep, key_mine, key_send = weight(ORDER[h], chips[h], f_same, f_other)
+        parts += [keep] + [swap(sends[m], (m + 1) * z_mask) for m in SUMS[h]]
         keys_mine.append(key_mine)
         keys_send.append(key_send)
     squares = plane_squares(parts, devices)

time: 57.7 us -> 56.8 us (0.984)
  transfers between devices with their start and end apart: 21 -> 21, of which waited for: 8 -> 8; matrix products, arithmetic and copies ran while one was open for 0% -> 0% of each run, Pallas kernels for 13% -> 14%
where the time goes in v6:
time: 56.8 us; the launch traced here: 56.6 us
  starting transfers between devices  26.2 us (46%)
  waiting for transfers between devices  17.3 us (30%)
  Pallas kernels  9.42 us (17%)
  local copies, waits for them, and re-layouts  2.81 us (5%)
  between operations  0.76 us (1%)
    ppermute x18, starting transfers between devices, swap(): return lax.ppermute(array, AXES, [(i, i ^ mask) for i in range(devices)])  19.3 us
    ppermute x18, waiting for transfers between devices, swap(): return lax.ppermute(array, AXES, [(i, i ^ mask) for i in range(devices)])  11 us
    all_to_all x1, waiting for transfers between devices, planes(): squares = lax.all_to_all(squares, AXES, 0, 0, tiled=True)  6.34 us
    pallas_call x1, Pallas kernels, attention(): pl.pallas_call(functools.partial(attention_kernel, turn), in_specs=[pl.Bl...  5.76 us
    all_to_all x1, starting transfers between devices, planes(): squares = lax.all_to_all(squares, AXES, 0, 0, tiled=True)  3.8 us
    unnamed x8, local copies, waits for them, and re-layouts  2.81 us
    ppermute x1, starting transfers between devices, planes(): v_prev = lax.ppermute(v_own, 'seq', following)  2.6 us
  transfers between devices with their start and end apart: 21, of which 8 were waited for; matrix products, arithmetic and copies ran while one was open for 0% of the time, Pallas kernels for 14%

profile of v6, /device:TPU:0, one launch (start us, length us, event | category | flops | bytes accessed | tf_op | source)
XLA Modules:
  0.0 56.6 jit_solution(4819357886211600736)
XLA Ops:
  0.6 0.5 collective-permute-start
  1.1 2.6 %collective-permute-start.1 = (bf16[128,512]{1,0:T(8,128)(2,1)}, bf16[128,512]{1,0:T(8,128)(2,1)S(1)}, u32[]{:S(2)}, u32[]{:S(2)}) collective-permute-start(bf16[128,512]{1,0:T(8,128)(2,1)} %bitcast.18), channel_id=1, source_target_pairs={{0,8},{8,16},{16,24},{24,0},{1,9},{9,17},{17,25},{25,1},{2,10},{10... | collective-permute-start | bytes 393224 | tf_op jit(solution)/shard_map/ppermute | solution.py:349
  3.7 0.0 copy-start
  3.7 1.2 %copy-done = bf16[1,128,4096]{2,1,0:T(8,128)(2,1)S(1)} copy-done((bf16[1,128,4096]{2,1,0:T(8,128)(2,1)S(1)}, bf16[1,128,4096]{2,1,0:T(8,128)(2,1)}, u32[]{:S(2)}) %copy-start) | copy-done | bytes 1048600
  5.0 0.3 shard_map.79
  5.2 1.6 %collective-permute-start.6 = (bf16[4,128,256]{2,1,0:T(8,128)(2,1)S(1)}, bf16[4,128,256]{2,1,0:T(8,128)(2,1)S(1)}, u32[]{:S(2)}, u32[]{:S(2)}) collective-permute-start(bf16[4,128,256]{2,1,0:T(8,128)(2,1)S(1)} %get-tuple-element.38), channel_id=1, source_target_pairs={{0,1},{1,0},{2,3},{3,2},{4,5},{5,4},{6,7},{7,6},{8,9},{9,8},{10,11... | collective-permute-start | bytes 786440 | tf_op jit(solution)/shard_map/ppermute | solution.py:343
  6.8 0.5 collective-permute-start.7
  7.4 1.4 %collective-permute-start.8 = (bf16[4,128,256]{2,1,0:T(8,128)(2,1)S(1)}, bf16[4,128,256]{2,1,0:T(8,128)(2,1)S(1)}, u32[]{:S(2)}, u32[]{:S(2)}) collective-permute-start(bf16[4,128,256]{2,1,0:T(8,128)(2,1)S(1)} %get-tuple-element.40), channel_id=1, source_target_pairs={{0,17},{1,16},{2,19},{3,18},{4,21},{5,20},{6,23},{7,22},{8,25},{9,... | collective-permute-start | bytes 786440 | tf_op jit(solution)/shard_map/ppermute | solution.py:343
  8.8 0.0 collective-permute-done.k_prev
  8.8 0.0 copy-start.2
  8.8 0.0 collective-permute-done.1.v_prev
  8.8 0.0 copy-start.3
  8.8 0.6 %copy-done.2 = bf16[128,512]{1,0:T(8,128)(2,1)} copy-done((bf16[128,512]{1,0:T(8,128)(2,1)}, bf16[128,512]{1,0:T(8,128)(2,1)S(1)}, u32[]{:S(2)}) %copy-start.2) | copy-done | bytes 131096
  9.4 0.0 copy-done.3
  9.5 5.8 %shard_map.77 = (bf16[2,256,128]{2,1,0:T(8,128)(2,1)}, bf16[2,256,128]{2,1,0:T(8,128)(2,1)}) custom-call(s32[1,8]{1,0:T(1,128)} %lengths.1, bf16[128,4096]{1,0:T(8,128)(2,1)} %bitcast.14, bf16[128,4096]{1,0:T(8,128)(2,1)} %bitcast.15, bf16[128,512]{1,0:T(8,128)(2,1)} %copy-done.2, bf16[128,512]{1,0:T(8,128)(2,1)} %bitcast.17, bf16[128,512]{1,0:T(8,128)(2,1)} %copy-done.3, ...), custom_call_target="tpu_custom_call" | custom-call | flops 805306368 | bytes 2097152 | tf_op jit(solution)/shard_map/pallas_call | solution.py:111
  15.3 0.1 collective-permute-start.2
  15.3 1.5 %collective-permute-done.2.theirs = bf16[2,256,128]{2,1,0:T(8,128)(2,1)S(1)} collective-permute-done((bf16[2,256,128]{2,1,0:T(8,128)(2,1)}, bf16[2,256,128]{2,1,0:T(8,128)(2,1)S(1)}, u32[]{:S(2)}, u32[]{:S(2)}) %collective-permute-start.2) | collective-permute-done | bytes 131104 | tf_op jit(solution)/shard_map/ppermute | solution.py:343
  16.9 0.0 copy-start.1
  16.9 0.9 %copy-done.1 = bf16[2,256,128]{2,1,0:T(8,128)(2,1)S(1)} copy-done((bf16[2,256,128]{2,1,0:T(8,128)(2,1)S(1)}, bf16[2,256,128]{2,1,0:T(8,128)(2,1)}, u32[]{:S(2)}) %copy-start.1) | copy-done | bytes 131096
  17.8 0.0 collective-permute-done.6.refs_5_
  17.8 0.0 collective-permute-done.7.refs_6_
  17.8 2.5 %collective-permute-done.8.refs_7_ = bf16[4,128,256]{2,1,0:T(8,128)(2,1)S(1)} collective-permute-done((bf16[4,128,256]{2,1,0:T(8,128)(2,1)S(1)}, bf16[4,128,256]{2,1,0:T(8,128)(2,1)S(1)}, u32[]{:S(2)}, u32[]{:S(2)}) %collective-permute-start.8) | collective-permute-done | bytes 262176 | tf_op jit(solution)/shard_map/ppermute | solution.py:343
  20.4 0.1 pad_maximum_fusion
  20.5 0.1 collective-permute-start.9
  20.6 1.5 %collective-permute-start.3 = (bf16[384,128]{1,0:T(8,128)(2,1)S(1)}, bf16[384,128]{1,0:T(8,128)(2,1)S(1)}, u32[]{:S(2)}, u32[]{:S(2)}) collective-permute-start(bf16[384,128]{1,0:T(8,128)(2,1)S(1)} %get-tuple-element.36.refs_0_), channel_id=1, source_target_pairs={{0,16},{1,17},{2,18},{3,19},{4,20},{5,21},{6,22},{7,23},{8,24},{9,... | collective-permute-start | bytes 294920 | tf_op jit(solution)/shard_map/ppermute | solution.py:343
  22.1 0.6 %collective-permute-start.4 = (bf16[384,128]{1,0:T(8,128)(2,1)S(1)}, bf16[384,128]{1,0:T(8,128)(2,1)S(1)}, u32[]{:S(2)}, u32[]{:S(2)}) collective-permute-start(bf16[384,128]{1,0:T(8,128)(2,1)S(1)} %get-tuple-element.36.refs_0_), channel_id=1, source_target_pairs={{0,1},{1,0},{2,3},{3,2},{4,5},{5,4},{6,7},{7,6},{8,9},{9,8},{10,11... | collective-permute-start | bytes 294920 | tf_op jit(solution)/shard_map/ppermute | solution.py:343
  22.7 1.4 %collective-permute-start.5 = (bf16[384,128]{1,0:T(8,128)(2,1)S(1)}, bf16[384,128]{1,0:T(8,128)(2,1)S(1)}, u32[]{:S(2)}, u32[]{:S(2)}) collective-permute-start(bf16[384,128]{1,0:T(8,128)(2,1)S(1)} %get-tuple-element.36.refs_0_), channel_id=1, source_target_pairs={{0,17},{1,16},{2,19},{3,18},{4,21},{5,20},{6,23},{7,22},{8,25},{9,... | collective-permute-start | bytes 294920 | tf_op jit(solution)/shard_map/ppermute | solution.py:343
  24.1 0.0 collective-permute-done.9.refs_8_
  24.1 1.4 %collective-permute-start.13 = (bf16[384,128]{1,0:T(8,128)(2,1)S(1)}, bf16[384,128]{1,0:T(8,128)(2,1)S(1)}, u32[]{:S(2)}, u32[]{:S(2)}) collective-permute-start(bf16[384,128]{1,0:T(8,128)(2,1)S(1)} %get-tuple-element.51.refs_0_), channel_id=1, source_target_pairs={{0,16},{1,17},{2,18},{3,19},{4,20},{5,21},{6,22},{7,23},{8,24},{9,... | collective-permute-start | bytes 294920 | tf_op jit(solution)/shard_map/ppermute | solution.py:343
  25.6 0.6 %collective-permute-start.14 = (bf16[384,128]{1,0:T(8,128)(2,1)S(1)}, bf16[384,128]{1,0:T(8,128)(2,1)S(1)}, u32[]{:S(2)}, u32[]{:S(2)}) collective-permute-start(bf16[384,128]{1,0:T(8,128)(2,1)S(1)} %get-tuple-element.51.refs_0_), channel_id=1, source_target_pairs={{0,1},{1,0},{2,3},{3,2},{4,5},{5,4},{6,7},{7,6},{8,9},{9,8},{10,11... | collective-permute-start | bytes 294920 | tf_op jit(solution)/shard_map/ppermute | solution.py:343
  26.2 0.0 collective-permute-done.3.refs_1_
  26.2 1.4 %collective-permute-start.15 = (bf16[384,128]{1,0:T(8,128)(2,1)S(1)}, bf16[384,128]{1,0:T(8,128)(2,1)S(1)}, u32[]{:S(2)}, u32[]{:S(2)}) collective-permute-start(bf16[384,128]{1,0:T(8,128)(2,1)S(1)} %get-tuple-element.51.refs_0_), channel_id=1, source_target_pairs={{0,17},{1,16},{2,19},{3,18},{4,21},{5,20},{6,23},{7,22},{8,25},{9,... | collective-permute-start | bytes 294920 | tf_op jit(solution)/shard_map/ppermute | solution.py:343
  27.6 0.0 collective-permute-done.4.refs_2_
  27.6 1.7 %collective-permute-done.5.refs_3_ = bf16[384,128]{1,0:T(8,128)(2,1)S(1)} collective-permute-done((bf16[384,128]{1,0:T(8,128)(2,1)S(1)}, bf16[384,128]{1,0:T(8,128)(2,1)S(1)}, u32[]{:S(2)}, u32[]{:S(2)}) %collective-permute-start.5) | collective-permute-done | bytes 98336 | tf_op jit(solution)/shard_map/ppermute | solution.py:343
  29.4 0.5 shard_map.80
  29.9 2.7 %collective-permute-start.10 = (bf16[128,256]{1,0:T(8,128)(2,1)S(1)}, bf16[128,256]{1,0:T(8,128)(2,1)S(1)}, u32[]{:S(2)}, u32[]{:S(2)}) collective-permute-start(bf16[128,256]{1,0:T(8,128)(2,1)S(1)} %get-tuple-element.48), channel_id=1, source_target_pairs={{0,4},{1,5},{2,6},{3,7},{4,0},{5,1},{6,2},{7,3},{8,12},{9,13},{10,... | collective-permute-start | bytes 196616 | tf_op jit(solution)/shard_map/ppermute | solution.py:343
  32.5 1.3 %collective-permute-start.11 = (bf16[128,256]{1,0:T(8,128)(2,1)S(1)}, bf16[128,256]{1,0:T(8,128)(2,1)S(1)}, u32[]{:S(2)}, u32[]{:S(2)}) collective-permute-start(bf16[128,256]{1,0:T(8,128)(2,1)S(1)} %get-tuple-element.49), channel_id=1, source_target_pairs={{0,6},{1,7},{2,4},{3,5},{4,2},{5,3},{6,0},{7,1},{8,14},{9,15},{10,... | collective-permute-start | bytes 196616 | tf_op jit(solution)/shard_map/ppermute | solution.py:343
  33.9 0.0 collective-permute-done.13.refs_1_
  33.9 0.2 collective-permute-start.12
  34.1 0.0 collective-permute-done.14.refs_2_
  34.1 0.0 collective-permute-done.15.refs_3_
  34.1 0.5 shard_map.81
  34.6 2.9 %collective-permute-start.16 = (bf16[128,256]{1,0:T(8,128)(2,1)S(1)}, bf16[128,256]{1,0:T(8,128)(2,1)S(1)}, u32[]{:S(2)}, u32[]{:S(2)}) collective-permute-start(bf16[128,256]{1,0:T(8,128)(2,1)S(1)} %get-tuple-element.53), channel_id=1, source_target_pairs={{0,4},{1,5},{2,6},{3,7},{4,0},{5,1},{6,2},{7,3},{8,12},{9,13},{10,... | collective-permute-start | bytes 196616 | tf_op jit(solution)/shard_map/ppermute | solution.py:343
  37.5 1.3 %collective-permute-start.17 = (bf16[128,256]{1,0:T(8,128)(2,1)S(1)}, bf16[128,256]{1,0:T(8,128)(2,1)S(1)}, u32[]{:S(2)}, u32[]{:S(2)}) collective-permute-start(bf16[128,256]{1,0:T(8,128)(2,1)S(1)} %get-tuple-element.54), channel_id=1, source_target_pairs={{0,6},{1,7},{2,4},{3,5},{4,2},{5,3},{6,0},{7,1},{8,14},{9,15},{10,... | collective-permute-start | bytes 196616 | tf_op jit(solution)/shard_map/ppermute | solution.py:343
  38.8 0.0 collective-permute-done.10.refs_1_
  38.8 0.0 collective-permute-start.18
  38.8 0.5 collective-permute-done.11.refs_2_
  39.4 0.0 collective-permute-done.12.refs_3_
  39.4 3.4 %collective-permute-done.16.refs_5_ = bf16[128,256]{1,0:T(8,128)(2,1)S(1)} collective-permute-done((bf16[128,256]{1,0:T(8,128)(2,1)S(1)}, bf16[128,256]{1,0:T(8,128)(2,1)S(1)}, u32[]{:S(2)}, u32[]{:S(2)}) %collective-permute-start.16) | collective-permute-done | bytes 65568 | tf_op jit(solution)/shard_map/ppermute | solution.py:343
  42.8 0.9 %collective-permute-done.17.refs_6_ = bf16[128,256]{1,0:T(8,128)(2,1)S(1)} collective-permute-done((bf16[128,256]{1,0:T(8,128)(2,1)S(1)}, bf16[128,256]{1,0:T(8,128)(2,1)S(1)}, u32[]{:S(2)}, u32[]{:S(2)}) %collective-permute-start.17) | collective-permute-done | bytes 65568 | tf_op jit(solution)/shard_map/ppermute | solution.py:343
  43.7 0.3 collective-permute-done.18.refs_7_
  44.0 0.7 %shard_map.82 = f32[32,1,128]{2,1,0:T(1,128)} custom-call(f32[128,256]{1,0:T(8,128)S(1)} %get-tuple-element.56.refs_0_, bf16[128,256]{1,0:T(8,128)(2,1)S(1)} %collective-permute-done.10.refs_1_, bf16[128,256]{1,0:T(8,128)(2,1)S(1)} %collective-permute-done.11.refs_2_, bf16[128,256]{1,0:T(8,128)(2,1)S(1)} %collective-permute-done.12.refs_3_, ...), custom_call_target="tpu_custom_call" | custom-call | flops 524288 | bytes 655360 | tf_op jit(solution)/shard_map/pallas_call | solution.py:253
  44.7 0.1 shard_map.83
  44.8 0.1 collective-permute-start.19
  44.9 3.8 %all-to-all-start = ((f32[32,1,128]{2,1,0:T(1,128)}), f32[32,1,128]{2,1,0:T(1,128)S(1)}, u32[]{:S(2)}, u32[]{:S(2)}) async-start(f32[32,1,128]{2,1,0:T(1,128)} %shard_map.82), calls=%async_computation | async-start | bytes 32768 | tf_op jit(solution)/shard_map/all_to_all | solution.py:372
  48.7 0.0 collective-permute-done.19.theirs
  48.7 0.7 %shard_map.84 = (f32[128,512]{1,0:T(8,128)S(1)}, bf16[1,128,512]{2,1,0:T(8,128)(2,1)}) custom-call(f32[128,256]{1,0:T(8,128)S(1)} %get-tuple-element.59.mine, f32[128,512]{1,0:T(8,128)S(1)} %collective-permute-done.19.theirs, bf16[128,128]{1,0:T(8,128)(2,1)S(1)} %get-tuple-element.61.refs_0_, bf16[128,128]{1,0:T(8,128)(2,1)S(1)} %get-tuple-element.62.refs_1_), custom_call_target="tpu_custom_call" | custom-call | bytes 786432 | tf_op jit(solution)/shard_map/pallas_call | solution.py:304
  49.4 6.3 %all-to-all-done.squares = f32[32,1,128]{2,1,0:T(1,128)S(1)} async-done(((f32[32,1,128]{2,1,0:T(1,128)}), f32[32,1,128]{2,1,0:T(1,128)S(1)}, u32[]{:S(2)}, u32[]{:S(2)}) %all-to-all-start) | async-done | bytes 16416 | tf_op jit(solution)/shard_map/all_to_all | solution.py:372
  55.8 0.8 %shard_map.85 = f32[128,512]{1,0:T(8,128)} custom-call(f32[32,1,128]{2,1,0:T(1,128)S(1)} %all-to-all-done.squares, f32[128,512]{1,0:T(8,128)S(1)} %get-tuple-element.65.rows), custom_call_target="tpu_custom_call" | custom-call | flops 65536 | bytes 524288 | tf_op jit(solution)/shard_map/pallas_call | solution.py:326
  (1 shorter events, 0.0 us)
Async XLA Ops:
  0.6 8.2 %collective-permute-start = (bf16[128,512]{1,0:T(8,128)(2,1)}, bf16[128,512]{1,0:T(8,128)(2,1)S(1)}, u32[]{:S(2)}, u32[]{:S(2)}) collective-permute-start(bf16[128,512]{1,0:T(8,128)(2,1)} %bitcast.16), channel_id=1, source_target_pairs={{0,8},{8,16},{16,24},{24,0},{1,9},{9,17},{17,25},{25,1},{2,10},{10... | collective-permute-start | bytes 393224 | tf_op jit(solution)/shard_map/ppermute | solution.py:348
  1.1 7.7 %collective-permute-start.1 = (bf16[128,512]{1,0:T(8,128)(2,1)}, bf16[128,512]{1,0:T(8,128)(2,1)S(1)}, u32[]{:S(2)}, u32[]{:S(2)}) collective-permute-start(bf16[128,512]{1,0:T(8,128)(2,1)} %bitcast.18), channel_id=1, source_target_pairs={{0,8},{8,16},{16,24},{24,0},{1,9},{9,17},{17,25},{25,1},{2,10},{10... | collective-permute-start | bytes 393224 | tf_op jit(solution)/shard_map/ppermute | solution.py:349
  3.7 1.2 %copy-start = (bf16[1,128,4096]{2,1,0:T(8,128)(2,1)S(1)}, bf16[1,128,4096]{2,1,0:T(8,128)(2,1)}, u32[]{:S(2)}) copy-start(bf16[1,128,4096]{2,1,0:T(8,128)(2,1)} %param.10) | copy-start | bytes 3145732
  5.2 12.6 %collective-permute-start.6 = (bf16[4,128,256]{2,1,0:T(8,128)(2,1)S(1)}, bf16[4,128,256]{2,1,0:T(8,128)(2,1)S(1)}, u32[]{:S(2)}, u32[]{:S(2)}) collective-permute-start(bf16[4,128,256]{2,1,0:T(8,128)(2,1)S(1)} %get-tuple-element.38), channel_id=1, source_target_pairs={{0,1},{1,0},{2,3},{3,2},{4,5},{5,4},{6,7},{7,6},{8,9},{9,8},{10,11... | collective-permute-start | bytes 786440 | tf_op jit(solution)/shard_map/ppermute | solution.py:343
  6.8 11.0 %collective-permute-start.7 = (bf16[4,128,256]{2,1,0:T(8,128)(2,1)S(1)}, bf16[4,128,256]{2,1,0:T(8,128)(2,1)S(1)}, u32[]{:S(2)}, u32[]{:S(2)}) collective-permute-start(bf16[4,128,256]{2,1,0:T(8,128)(2,1)S(1)} %get-tuple-element.39), channel_id=1, source_target_pairs={{0,16},{1,17},{2,18},{3,19},{4,20},{5,21},{6,22},{7,23},{8,24},{9,... | collective-permute-start | bytes 786440 | tf_op jit(solution)/shard_map/ppermute | solution.py:343
  7.4 13.0 %collective-permute-start.8 = (bf16[4,128,256]{2,1,0:T(8,128)(2,1)S(1)}, bf16[4,128,256]{2,1,0:T(8,128)(2,1)S(1)}, u32[]{:S(2)}, u32[]{:S(2)}) collective-permute-start(bf16[4,128,256]{2,1,0:T(8,128)(2,1)S(1)} %get-tuple-element.40), channel_id=1, source_target_pairs={{0,17},{1,16},{2,19},{3,18},{4,21},{5,20},{6,23},{7,22},{8,25},{9,... | collective-permute-start | bytes 786440 | tf_op jit(solution)/shard_map/ppermute | solution.py:343
  8.8 0.7 %copy-start.2 = (bf16[128,512]{1,0:T(8,128)(2,1)}, bf16[128,512]{1,0:T(8,128)(2,1)S(1)}, u32[]{:S(2)}) copy-start(bf16[128,512]{1,0:T(8,128)(2,1)S(1)} %collective-permute-done.k_prev) | copy-start | bytes 393220
  8.8 0.7 %copy-start.3 = (bf16[128,512]{1,0:T(8,128)(2,1)}, bf16[128,512]{1,0:T(8,128)(2,1)S(1)}, u32[]{:S(2)}) copy-start(bf16[128,512]{1,0:T(8,128)(2,1)S(1)} %collective-permute-done.1.v_prev) | copy-start | bytes 393220
  15.3 1.6 %collective-permute-start.2 = (bf16[2,256,128]{2,1,0:T(8,128)(2,1)}, bf16[2,256,128]{2,1,0:T(8,128)(2,1)S(1)}, u32[]{:S(2)}, u32[]{:S(2)}) collective-permute-start(bf16[2,256,128]{2,1,0:T(8,128)(2,1)} %get-tuple-element.35), channel_id=1, source_target_pairs={{0,8},{1,9},{2,10},{3,11},{4,12},{5,13},{6,14},{7,15},{8,0},{9,1},... | collective-permute-start | bytes 393224 | tf_op jit(solution)/shard_map/ppermute | solution.py:343
  16.9 0.9 %copy-start.1 = (bf16[2,256,128]{2,1,0:T(8,128)(2,1)S(1)}, bf16[2,256,128]{2,1,0:T(8,128)(2,1)}, u32[]{:S(2)}) copy-start(bf16[2,256,128]{2,1,0:T(8,128)(2,1)} %get-tuple-element.34.mine) | copy-start | bytes 393220
  20.5 3.6 %collective-permute-start.9 = (bf16[4,4,128,256]{3,2,1,0:T(8,128)(2,1)S(1)}, bf16[4,4,128,256]{3,2,1,0:T(8,128)(2,1)S(1)}, u32[]{:S(2)}, u32[]{:S(2)}) collective-permute-start(bf16[4,4,128,256]{3,2,1,0:T(8,128)(2,1)S(1)} %pad_maximum_fusion), channel_id=1, source_target_pairs={{0,8},{1,9},{2,10},{3,11},{4,12},{5,13},{6,14},{7,15},{8,0},{9,1},... | collective-permute-start | bytes 3145736 | tf_op jit(solution)/shard_map/ppermute | solution.py:343
  20.6 5.6 %collective-permute-start.3 = (bf16[384,128]{1,0:T(8,128)(2,1)S(1)}, bf16[384,128]{1,0:T(8,128)(2,1)S(1)}, u32[]{:S(2)}, u32[]{:S(2)}) collective-permute-start(bf16[384,128]{1,0:T(8,128)(2,1)S(1)} %get-tuple-element.36.refs_0_), channel_id=1, source_target_pairs={{0,16},{1,17},{2,18},{3,19},{4,20},{5,21},{6,22},{7,23},{8,24},{9,... | collective-permute-start | bytes 294920 | tf_op jit(solution)/shard_map/ppermute | solution.py:343
  22.1 5.6 %collective-permute-start.4 = (bf16[384,128]{1,0:T(8,128)(2,1)S(1)}, bf16[384,128]{1,0:T(8,128)(2,1)S(1)}, u32[]{:S(2)}, u32[]{:S(2)}) collective-permute-start(bf16[384,128]{1,0:T(8,128)(2,1)S(1)} %get-tuple-element.36.refs_0_), channel_id=1, source_target_pairs={{0,1},{1,0},{2,3},{3,2},{4,5},{5,4},{6,7},{7,6},{8,9},{9,8},{10,11... | collective-permute-start | bytes 294920 | tf_op jit(solution)/shard_map/ppermute | solution.py:343
  22.7 6.7 %collective-permute-start.5 = (bf16[384,128]{1,0:T(8,128)(2,1)S(1)}, bf16[384,128]{1,0:T(8,128)(2,1)S(1)}, u32[]{:S(2)}, u32[]{:S(2)}) collective-permute-start(bf16[384,128]{1,0:T(8,128)(2,1)S(1)} %get-tuple-element.36.refs_0_), channel_id=1, source_target_pairs={{0,17},{1,16},{2,19},{3,18},{4,21},{5,20},{6,23},{7,22},{8,25},{9,... | collective-permute-start | bytes 294920 | tf_op jit(solution)/shard_map/ppermute | solution.py:343
  24.1 9.7 %collective-permute-start.13 = (bf16[384,128]{1,0:T(8,128)(2,1)S(1)}, bf16[384,128]{1,0:T(8,128)(2,1)S(1)}, u32[]{:S(2)}, u32[]{:S(2)}) collective-permute-start(bf16[384,128]{1,0:T(8,128)(2,1)S(1)} %get-tuple-element.51.refs_0_), channel_id=1, source_target_pairs={{0,16},{1,17},{2,18},{3,19},{4,20},{5,21},{6,22},{7,23},{8,24},{9,... | collective-permute-start | bytes 294920 | tf_op jit(solution)/shard_map/ppermute | solution.py:343
  25.6 8.5 %collective-permute-start.14 = (bf16[384,128]{1,0:T(8,128)(2,1)S(1)}, bf16[384,128]{1,0:T(8,128)(2,1)S(1)}, u32[]{:S(2)}, u32[]{:S(2)}) collective-permute-start(bf16[384,128]{1,0:T(8,128)(2,1)S(1)} %get-tuple-element.51.refs_0_), channel_id=1, source_target_pairs={{0,1},{1,0},{2,3},{3,2},{4,5},{5,4},{6,7},{7,6},{8,9},{9,8},{10,11... | collective-permute-start | bytes 294920 | tf_op jit(solution)/shard_map/ppermute | solution.py:343
  26.2 7.9 %collective-permute-start.15 = (bf16[384,128]{1,0:T(8,128)(2,1)S(1)}, bf16[384,128]{1,0:T(8,128)(2,1)S(1)}, u32[]{:S(2)}, u32[]{:S(2)}) collective-permute-start(bf16[384,128]{1,0:T(8,128)(2,1)S(1)} %get-tuple-element.51.refs_0_), channel_id=1, source_target_pairs={{0,17},{1,16},{2,19},{3,18},{4,21},{5,20},{6,23},{7,22},{8,25},{9,... | collective-permute-start | bytes 294920 | tf_op jit(solution)/shard_map/ppermute | solution.py:343
  29.9 9.0 %collective-permute-start.10 = (bf16[128,256]{1,0:T(8,128)(2,1)S(1)}, bf16[128,256]{1,0:T(8,128)(2,1)S(1)}, u32[]{:S(2)}, u32[]{:S(2)}) collective-permute-start(bf16[128,256]{1,0:T(8,128)(2,1)S(1)} %get-tuple-element.48), channel_id=1, source_target_pairs={{0,4},{1,5},{2,6},{3,7},{4,0},{5,1},{6,2},{7,3},{8,12},{9,13},{10,... | collective-permute-start | bytes 196616 | tf_op jit(solution)/shard_map/ppermute | solution.py:343
  32.5 6.8 %collective-permute-start.11 = (bf16[128,256]{1,0:T(8,128)(2,1)S(1)}, bf16[128,256]{1,0:T(8,128)(2,1)S(1)}, u32[]{:S(2)}, u32[]{:S(2)}) collective-permute-start(bf16[128,256]{1,0:T(8,128)(2,1)S(1)} %get-tuple-element.49), channel_id=1, source_target_pairs={{0,6},{1,7},{2,4},{3,5},{4,2},{5,3},{6,0},{7,1},{8,14},{9,15},{10,... | collective-permute-start | bytes 196616 | tf_op jit(solution)/shard_map/ppermute | solution.py:343
  33.9 5.5 %collective-permute-start.12 = (bf16[128,256]{1,0:T(8,128)(2,1)S(1)}, bf16[128,256]{1,0:T(8,128)(2,1)S(1)}, u32[]{:S(2)}, u32[]{:S(2)}) collective-permute-start(bf16[128,256]{1,0:T(8,128)(2,1)S(1)} %get-tuple-element.50), channel_id=1, source_target_pairs={{0,2},{1,3},{2,0},{3,1},{4,6},{5,7},{6,4},{7,5},{8,10},{9,11},{10,... | collective-permute-start | bytes 196616 | tf_op jit(solution)/shard_map/ppermute | solution.py:343
  34.6 8.2 %collective-permute-start.16 = (bf16[128,256]{1,0:T(8,128)(2,1)S(1)}, bf16[128,256]{1,0:T(8,128)(2,1)S(1)}, u32[]{:S(2)}, u32[]{:S(2)}) collective-permute-start(bf16[128,256]{1,0:T(8,128)(2,1)S(1)} %get-tuple-element.53), channel_id=1, source_target_pairs={{0,4},{1,5},{2,6},{3,7},{4,0},{5,1},{6,2},{7,3},{8,12},{9,13},{10,... | collective-permute-start | bytes 196616 | tf_op jit(solution)/shard_map/ppermute | solution.py:343
  37.5 6.2 %collective-permute-start.17 = (bf16[128,256]{1,0:T(8,128)(2,1)S(1)}, bf16[128,256]{1,0:T(8,128)(2,1)S(1)}, u32[]{:S(2)}, u32[]{:S(2)}) collective-permute-start(bf16[128,256]{1,0:T(8,128)(2,1)S(1)} %get-tuple-element.54), channel_id=1, source_target_pairs={{0,6},{1,7},{2,4},{3,5},{4,2},{5,3},{6,0},{7,1},{8,14},{9,15},{10,... | collective-permute-start | bytes 196616 | tf_op jit(solution)/shard_map/ppermute | solution.py:343
  38.8 5.2 %collective-permute-start.18 = (bf16[128,256]{1,0:T(8,128)(2,1)S(1)}, bf16[128,256]{1,0:T(8,128)(2,1)S(1)}, u32[]{:S(2)}, u32[]{:S(2)}) collective-permute-start(bf16[128,256]{1,0:T(8,128)(2,1)S(1)} %get-tuple-element.55), channel_id=1, source_target_pairs={{0,2},{1,3},{2,0},{3,1},{4,6},{5,7},{6,4},{7,5},{8,10},{9,11},{10,... | collective-permute-start | bytes 196616 | tf_op jit(solution)/shard_map/ppermute | solution.py:343
  44.8 3.9 %collective-permute-start.19 = (f32[128,512]{1,0:T(8,128)S(1)}, f32[128,512]{1,0:T(8,128)S(1)}, u32[]{:S(2)}, u32[]{:S(2)}) collective-permute-start(f32[128,512]{1,0:T(8,128)S(1)} %get-tuple-element.60), channel_id=1, source_target_pairs={{0,8},{1,9},{2,10},{3,11},{4,12},{5,13},{6,14},{7,15},{8,0},{9,1},... | collective-permute-start | bytes 786440 | tf_op jit(solution)/shard_map/ppermute | solution.py:343
  44.9 10.9 %all-to-all-start = ((f32[32,1,128]{2,1,0:T(1,128)}), f32[32,1,128]{2,1,0:T(1,128)S(1)}, u32[]{:S(2)}, u32[]{:S(2)}) async-start(f32[32,1,128]{2,1,0:T(1,128)} %shard_map.82), calls=%async_computation | async-start | bytes 32768 | tf_op jit(solution)/shard_map/all_to_all | solution.py:372

commit v7 on v6

--- a/solution.py
+++ b/solution.py
@@ -20,7 +20,7 @@
 BF16 = jnp.bfloat16
 CORES = 2
 ORDER = ((0, 2, 1, 3), (0, 2, 1, 3))
-SUMS = ((1, 2, 0), (1, 2, 0))
+SUMS = ((2, 1, 0), (1, 2, 0))
 HALF = KVH // CORES
 WIDE = HALF * HD
 

time: 56.8 us -> 56.5 us (level)
  transfers between devices with their start and end apart: 21 -> 21, of which waited for: 8 -> 7; matrix products, arithmetic and copies ran while one was open for 0% -> 0% of each run, Pallas kernels for 14% -> 14%
where the time goes in v7:
time: 56.5 us; the launch traced here: 56.3 us
  starting transfers between devices  26 us (46%)
  waiting for transfers between devices  17.1 us (30%)
  Pallas kernels  9.42 us (17%)
  local copies, waits for them, and re-layouts  2.81 us (5%)
  between operations  0.76 us (1%)
    ppermute x18, starting transfers between devices, swap(): return lax.ppermute(array, AXES, [(i, i ^ mask) for i in range(devices)])  19.5 us
    ppermute x18, waiting for transfers between devices, swap(): return lax.ppermute(array, AXES, [(i, i ^ mask) for i in range(devices)])  10.8 us
    all_to_all x1, waiting for transfers between devices, planes(): squares = lax.all_to_all(squares, AXES, 0, 0, tiled=True)  6.34 us
    pallas_call x1, Pallas kernels, attention(): pl.pallas_call(functools.partial(attention_kernel, turn), in_specs=[pl.Bl...  5.76 us
    all_to_all x1, starting transfers between devices, planes(): squares = lax.all_to_all(squares, AXES, 0, 0, tiled=True)  3.44 us
    unnamed x8, local copies, waits for them, and re-layouts  2.81 us
    ppermute x1, starting transfers between devices, planes(): v_prev = lax.ppermute(v_own, 'seq', following)  2.6 us
  transfers between devices with their start and end apart: 21, of which 7 were waited for; matrix products, arithmetic and copies ran while one was open for 0% of the time, Pallas kernels for 14%

profile of v7, /device:TPU:0, one launch (start us, length us, event | category | flops | bytes accessed | tf_op | source)
XLA Modules:
  0.0 56.3 jit_solution(8514771693749191371)
XLA Ops:
  0.6 0.5 collective-permute-start
  1.1 2.6 %collective-permute-start.1 = (bf16[128,512]{1,0:T(8,128)(2,1)}, bf16[128,512]{1,0:T(8,128)(2,1)S(1)}, u32[]{:S(2)}, u32[]{:S(2)}) collective-permute-start(bf16[128,512]{1,0:T(8,128)(2,1)} %bitcast.18), channel_id=1, source_target_pairs={{0,8},{8,16},{16,24},{24,0},{1,9},{9,17},{17,25},{25,1},{2,10},{10... | collective-permute-start | bytes 393224 | tf_op jit(solution)/shard_map/ppermute | solution.py:349
  3.7 0.0 copy-start
  3.7 1.2 %copy-done = bf16[1,128,4096]{2,1,0:T(8,128)(2,1)S(1)} copy-done((bf16[1,128,4096]{2,1,0:T(8,128)(2,1)S(1)}, bf16[1,128,4096]{2,1,0:T(8,128)(2,1)}, u32[]{:S(2)}) %copy-start) | copy-done | bytes 1048600
  5.0 0.3 shard_map.79
  5.2 1.6 %collective-permute-start.6 = (bf16[4,128,256]{2,1,0:T(8,128)(2,1)S(1)}, bf16[4,128,256]{2,1,0:T(8,128)(2,1)S(1)}, u32[]{:S(2)}, u32[]{:S(2)}) collective-permute-start(bf16[4,128,256]{2,1,0:T(8,128)(2,1)S(1)} %get-tuple-element.38), channel_id=1, source_target_pairs={{0,1},{1,0},{2,3},{3,2},{4,5},{5,4},{6,7},{7,6},{8,9},{9,8},{10,11... | collective-permute-start | bytes 786440 | tf_op jit(solution)/shard_map/ppermute | solution.py:343
  6.8 0.5 collective-permute-start.7
  7.4 1.4 %collective-permute-start.8 = (bf16[4,128,256]{2,1,0:T(8,128)(2,1)S(1)}, bf16[4,128,256]{2,1,0:T(8,128)(2,1)S(1)}, u32[]{:S(2)}, u32[]{:S(2)}) collective-permute-start(bf16[4,128,256]{2,1,0:T(8,128)(2,1)S(1)} %get-tuple-element.40), channel_id=1, source_target_pairs={{0,17},{1,16},{2,19},{3,18},{4,21},{5,20},{6,23},{7,22},{8,25},{9,... | collective-permute-start | bytes 786440 | tf_op jit(solution)/shard_map/ppermute | solution.py:343
  8.8 0.0 collective-permute-done.k_prev
  8.8 0.0 copy-start.2
  8.8 0.0 collective-permute-done.1.v_prev
  8.8 0.0 copy-start.3
  8.8 0.6 %copy-done.2 = bf16[128,512]{1,0:T(8,128)(2,1)} copy-done((bf16[128,512]{1,0:T(8,128)(2,1)}, bf16[128,512]{1,0:T(8,128)(2,1)S(1)}, u32[]{:S(2)}) %copy-start.2) | copy-done | bytes 131096
  9.4 0.0 copy-done.3
  9.5 5.8 %shard_map.77 = (bf16[2,256,128]{2,1,0:T(8,128)(2,1)}, bf16[2,256,128]{2,1,0:T(8,128)(2,1)}) custom-call(s32[1,8]{1,0:T(1,128)} %lengths.1, bf16[128,4096]{1,0:T(8,128)(2,1)} %bitcast.14, bf16[128,4096]{1,0:T(8,128)(2,1)} %bitcast.15, bf16[128,512]{1,0:T(8,128)(2,1)} %copy-done.2, bf16[128,512]{1,0:T(8,128)(2,1)} %bitcast.17, bf16[128,512]{1,0:T(8,128)(2,1)} %copy-done.3, ...), custom_call_target="tpu_custom_call" | custom-call | flops 805306368 | bytes 2097152 | tf_op jit(solution)/shard_map/pallas_call | solution.py:111
  15.3 0.1 collective-permute-start.2
  15.3 1.5 %collective-permute-done.2.theirs = bf16[2,256,128]{2,1,0:T(8,128)(2,1)S(1)} collective-permute-done((bf16[2,256,128]{2,1,0:T(8,128)(2,1)}, bf16[2,256,128]{2,1,0:T(8,128)(2,1)S(1)}, u32[]{:S(2)}, u32[]{:S(2)}) %collective-permute-start.2) | collective-permute-done | bytes 131104 | tf_op jit(solution)/shard_map/ppermute | solution.py:343
  16.9 0.0 copy-start.1
  16.9 0.9 %copy-done.1 = bf16[2,256,128]{2,1,0:T(8,128)(2,1)S(1)} copy-done((bf16[2,256,128]{2,1,0:T(8,128)(2,1)S(1)}, bf16[2,256,128]{2,1,0:T(8,128)(2,1)}, u32[]{:S(2)}) %copy-start.1) | copy-done | bytes 131096
  17.8 0.0 collective-permute-done.6.refs_5_
  17.8 0.0 collective-permute-done.7.refs_6_
  17.8 2.5 %collective-permute-done.8.refs_7_ = bf16[4,128,256]{2,1,0:T(8,128)(2,1)S(1)} collective-permute-done((bf16[4,128,256]{2,1,0:T(8,128)(2,1)S(1)}, bf16[4,128,256]{2,1,0:T(8,128)(2,1)S(1)}, u32[]{:S(2)}, u32[]{:S(2)}) %collective-permute-start.8) | collective-permute-done | bytes 262176 | tf_op jit(solution)/shard_map/ppermute | solution.py:343
  20.4 0.1 pad_maximum_fusion
  20.5 0.1 collective-permute-start.9
  20.6 1.5 %collective-permute-start.3 = (bf16[384,128]{1,0:T(8,128)(2,1)S(1)}, bf16[384,128]{1,0:T(8,128)(2,1)S(1)}, u32[]{:S(2)}, u32[]{:S(2)}) collective-permute-start(bf16[384,128]{1,0:T(8,128)(2,1)S(1)} %get-tuple-element.36.refs_0_), channel_id=1, source_target_pairs={{0,16},{1,17},{2,18},{3,19},{4,20},{5,21},{6,22},{7,23},{8,24},{9,... | collective-permute-start | bytes 294920 | tf_op jit(solution)/shard_map/ppermute | solution.py:343
  22.1 0.6 %collective-permute-start.4 = (bf16[384,128]{1,0:T(8,128)(2,1)S(1)}, bf16[384,128]{1,0:T(8,128)(2,1)S(1)}, u32[]{:S(2)}, u32[]{:S(2)}) collective-permute-start(bf16[384,128]{1,0:T(8,128)(2,1)S(1)} %get-tuple-element.36.refs_0_), channel_id=1, source_target_pairs={{0,1},{1,0},{2,3},{3,2},{4,5},{5,4},{6,7},{7,6},{8,9},{9,8},{10,11... | collective-permute-start | bytes 294920 | tf_op jit(solution)/shard_map/ppermute | solution.py:343
  22.7 1.4 %collective-permute-start.5 = (bf16[384,128]{1,0:T(8,128)(2,1)S(1)}, bf16[384,128]{1,0:T(8,128)(2,1)S(1)}, u32[]{:S(2)}, u32[]{:S(2)}) collective-permute-start(bf16[384,128]{1,0:T(8,128)(2,1)S(1)} %get-tuple-element.36.refs_0_), channel_id=1, source_target_pairs={{0,17},{1,16},{2,19},{3,18},{4,21},{5,20},{6,23},{7,22},{8,25},{9,... | collective-permute-start | bytes 294920 | tf_op jit(solution)/shard_map/ppermute | solution.py:343
  24.1 0.0 collective-permute-done.9.refs_8_
  24.1 1.4 %collective-permute-start.13 = (bf16[384,128]{1,0:T(8,128)(2,1)S(1)}, bf16[384,128]{1,0:T(8,128)(2,1)S(1)}, u32[]{:S(2)}, u32[]{:S(2)}) collective-permute-start(bf16[384,128]{1,0:T(8,128)(2,1)S(1)} %get-tuple-element.51.refs_0_), channel_id=1, source_target_pairs={{0,16},{1,17},{2,18},{3,19},{4,20},{5,21},{6,22},{7,23},{8,24},{9,... | collective-permute-start | bytes 294920 | tf_op jit(solution)/shard_map/ppermute | solution.py:343
  25.6 0.6 %collective-permute-start.14 = (bf16[384,128]{1,0:T(8,128)(2,1)S(1)}, bf16[384,128]{1,0:T(8,128)(2,1)S(1)}, u32[]{:S(2)}, u32[]{:S(2)}) collective-permute-start(bf16[384,128]{1,0:T(8,128)(2,1)S(1)} %get-tuple-element.51.refs_0_), channel_id=1, source_target_pairs={{0,1},{1,0},{2,3},{3,2},{4,5},{5,4},{6,7},{7,6},{8,9},{9,8},{10,11... | collective-permute-start | bytes 294920 | tf_op jit(solution)/shard_map/ppermute | solution.py:343
  26.2 0.0 collective-permute-done.3.refs_1_
  26.2 1.4 %collective-permute-start.15 = (bf16[384,128]{1,0:T(8,128)(2,1)S(1)}, bf16[384,128]{1,0:T(8,128)(2,1)S(1)}, u32[]{:S(2)}, u32[]{:S(2)}) collective-permute-start(bf16[384,128]{1,0:T(8,128)(2,1)S(1)} %get-tuple-element.51.refs_0_), channel_id=1, source_target_pairs={{0,17},{1,16},{2,19},{3,18},{4,21},{5,20},{6,23},{7,22},{8,25},{9,... | collective-permute-start | bytes 294920 | tf_op jit(solution)/shard_map/ppermute | solution.py:343
  27.6 0.0 collective-permute-done.4.refs_2_
  27.6 1.7 %collective-permute-done.5.refs_3_ = bf16[384,128]{1,0:T(8,128)(2,1)S(1)} collective-permute-done((bf16[384,128]{1,0:T(8,128)(2,1)S(1)}, bf16[384,128]{1,0:T(8,128)(2,1)S(1)}, u32[]{:S(2)}, u32[]{:S(2)}) %collective-permute-start.5) | collective-permute-done | bytes 98336 | tf_op jit(solution)/shard_map/ppermute | solution.py:343
  29.4 0.5 shard_map.80
  29.9 3.7 %collective-permute-start.10 = (bf16[128,256]{1,0:T(8,128)(2,1)S(1)}, bf16[128,256]{1,0:T(8,128)(2,1)S(1)}, u32[]{:S(2)}, u32[]{:S(2)}) collective-permute-start(bf16[128,256]{1,0:T(8,128)(2,1)S(1)} %get-tuple-element.48), channel_id=1, source_target_pairs={{0,6},{1,7},{2,4},{3,5},{4,2},{5,3},{6,0},{7,1},{8,14},{9,15},{10,... | collective-permute-start | bytes 196616 | tf_op jit(solution)/shard_map/ppermute | solution.py:343
  33.5 0.0 collective-permute-start.11
  33.5 0.0 collective-permute-done.13.refs_1_
  33.5 0.8 %collective-permute-start.12 = (bf16[128,256]{1,0:T(8,128)(2,1)S(1)}, bf16[128,256]{1,0:T(8,128)(2,1)S(1)}, u32[]{:S(2)}, u32[]{:S(2)}) collective-permute-start(bf16[128,256]{1,0:T(8,128)(2,1)S(1)} %get-tuple-element.50), channel_id=1, source_target_pairs={{0,2},{1,3},{2,0},{3,1},{4,6},{5,7},{6,4},{7,5},{8,10},{9,11},{10,... | collective-permute-start | bytes 196616 | tf_op jit(solution)/shard_map/ppermute | solution.py:343
  34.3 0.0 collective-permute-done.14.refs_2_
  34.3 0.0 collective-permute-done.15.refs_3_
  34.3 0.5 shard_map.81
  34.8 2.2 %collective-permute-start.16 = (bf16[128,256]{1,0:T(8,128)(2,1)S(1)}, bf16[128,256]{1,0:T(8,128)(2,1)S(1)}, u32[]{:S(2)}, u32[]{:S(2)}) collective-permute-start(bf16[128,256]{1,0:T(8,128)(2,1)S(1)} %get-tuple-element.53), channel_id=1, source_target_pairs={{0,4},{1,5},{2,6},{3,7},{4,0},{5,1},{6,2},{7,3},{8,12},{9,13},{10,... | collective-permute-start | bytes 196616 | tf_op jit(solution)/shard_map/ppermute | solution.py:343
  37.1 1.5 %collective-permute-start.17 = (bf16[128,256]{1,0:T(8,128)(2,1)S(1)}, bf16[128,256]{1,0:T(8,128)(2,1)S(1)}, u32[]{:S(2)}, u32[]{:S(2)}) collective-permute-start(bf16[128,256]{1,0:T(8,128)(2,1)S(1)} %get-tuple-element.54), channel_id=1, source_target_pairs={{0,6},{1,7},{2,4},{3,5},{4,2},{5,3},{6,0},{7,1},{8,14},{9,15},{10,... | collective-permute-start | bytes 196616 | tf_op jit(solution)/shard_map/ppermute | solution.py:343
  38.6 0.0 collective-permute-done.10.refs_1_
  38.6 0.5 collective-permute-start.18
  39.1 2.6 %collective-permute-done.11.refs_2_ = bf16[128,256]{1,0:T(8,128)(2,1)S(1)} collective-permute-done((bf16[128,256]{1,0:T(8,128)(2,1)S(1)}, bf16[128,256]{1,0:T(8,128)(2,1)S(1)}, u32[]{:S(2)}, u32[]{:S(2)}) %collective-permute-start.11) | collective-permute-done | bytes 65568 | tf_op jit(solution)/shard_map/ppermute | solution.py:343
  41.7 0.0 collective-permute-done.12.refs_3_
  41.7 2.0 %collective-permute-done.16.refs_5_ = bf16[128,256]{1,0:T(8,128)(2,1)S(1)} collective-permute-done((bf16[128,256]{1,0:T(8,128)(2,1)S(1)}, bf16[128,256]{1,0:T(8,128)(2,1)S(1)}, u32[]{:S(2)}, u32[]{:S(2)}) %collective-permute-start.16) | collective-permute-done | bytes 65568 | tf_op jit(solution)/shard_map/ppermute | solution.py:343
  43.7 0.0 collective-permute-done.17.refs_6_
  43.7 0.4 collective-permute-done.18.refs_7_
  44.0 0.7 %shard_map.82 = f32[32,1,128]{2,1,0:T(1,128)} custom-call(f32[128,256]{1,0:T(8,128)S(1)} %get-tuple-element.56.refs_0_, bf16[128,256]{1,0:T(8,128)(2,1)S(1)} %collective-permute-done.10.refs_1_, bf16[128,256]{1,0:T(8,128)(2,1)S(1)} %collective-permute-done.11.refs_2_, bf16[128,256]{1,0:T(8,128)(2,1)S(1)} %collective-permute-done.12.refs_3_, ...), custom_call_target="tpu_custom_call" | custom-call | flops 524288 | bytes 655360 | tf_op jit(solution)/shard_map/pallas_call | solution.py:253
  44.7 0.1 shard_map.83
  44.9 0.1 collective-permute-start.19
  44.9 3.4 %all-to-all-start = ((f32[32,1,128]{2,1,0:T(1,128)}), f32[32,1,128]{2,1,0:T(1,128)S(1)}, u32[]{:S(2)}, u32[]{:S(2)}) async-start(f32[32,1,128]{2,1,0:T(1,128)} %shard_map.82), calls=%async_computation | async-start | bytes 32768 | tf_op jit(solution)/shard_map/all_to_all | solution.py:372
  48.4 0.0 collective-permute-done.19.theirs
  48.4 0.7 %shard_map.84 = (f32[128,512]{1,0:T(8,128)S(1)}, bf16[1,128,512]{2,1,0:T(8,128)(2,1)}) custom-call(f32[128,256]{1,0:T(8,128)S(1)} %get-tuple-element.59.mine, f32[128,512]{1,0:T(8,128)S(1)} %collective-permute-done.19.theirs, bf16[128,128]{1,0:T(8,128)(2,1)S(1)} %get-tuple-element.61.refs_0_, bf16[128,128]{1,0:T(8,128)(2,1)S(1)} %get-tuple-element.62.refs_1_), custom_call_target="tpu_custom_call" | custom-call | bytes 786432 | tf_op jit(solution)/shard_map/pallas_call | solution.py:304
  49.1 6.3 %all-to-all-done.squares = f32[32,1,128]{2,1,0:T(1,128)S(1)} async-done(((f32[32,1,128]{2,1,0:T(1,128)}), f32[32,1,128]{2,1,0:T(1,128)S(1)}, u32[]{:S(2)}, u32[]{:S(2)}) %all-to-all-start) | async-done | bytes 16416 | tf_op jit(solution)/shard_map/all_to_all | solution.py:372
  55.4 0.8 %shard_map.85 = f32[128,512]{1,0:T(8,128)} custom-call(f32[32,1,128]{2,1,0:T(1,128)S(1)} %all-to-all-done.squares, f32[128,512]{1,0:T(8,128)S(1)} %get-tuple-element.65.rows), custom_call_target="tpu_custom_call" | custom-call | flops 65536 | bytes 524288 | tf_op jit(solution)/shard_map/pallas_call | solution.py:326
  (1 shorter events, 0.0 us)
Async XLA Ops:
  0.6 8.2 %collective-permute-start = (bf16[128,512]{1,0:T(8,128)(2,1)}, bf16[128,512]{1,0:T(8,128)(2,1)S(1)}, u32[]{:S(2)}, u32[]{:S(2)}) collective-permute-start(bf16[128,512]{1,0:T(8,128)(2,1)} %bitcast.16), channel_id=1, source_target_pairs={{0,8},{8,16},{16,24},{24,0},{1,9},{9,17},{17,25},{25,1},{2,10},{10... | collective-permute-start | bytes 393224 | tf_op jit(solution)/shard_map/ppermute | solution.py:348
  1.1 7.7 %collective-permute-start.1 = (bf16[128,512]{1,0:T(8,128)(2,1)}, bf16[128,512]{1,0:T(8,128)(2,1)S(1)}, u32[]{:S(2)}, u32[]{:S(2)}) collective-permute-start(bf16[128,512]{1,0:T(8,128)(2,1)} %bitcast.18), channel_id=1, source_target_pairs={{0,8},{8,16},{16,24},{24,0},{1,9},{9,17},{17,25},{25,1},{2,10},{10... | collective-permute-start | bytes 393224 | tf_op jit(solution)/shard_map/ppermute | solution.py:349
  3.7 1.2 %copy-start = (bf16[1,128,4096]{2,1,0:T(8,128)(2,1)S(1)}, bf16[1,128,4096]{2,1,0:T(8,128)(2,1)}, u32[]{:S(2)}) copy-start(bf16[1,128,4096]{2,1,0:T(8,128)(2,1)} %param.10) | copy-start | bytes 3145732
  5.2 12.6 %collective-permute-start.6 = (bf16[4,128,256]{2,1,0:T(8,128)(2,1)S(1)}, bf16[4,128,256]{2,1,0:T(8,128)(2,1)S(1)}, u32[]{:S(2)}, u32[]{:S(2)}) collective-permute-start(bf16[4,128,256]{2,1,0:T(8,128)(2,1)S(1)} %get-tuple-element.38), channel_id=1, source_target_pairs={{0,1},{1,0},{2,3},{3,2},{4,5},{5,4},{6,7},{7,6},{8,9},{9,8},{10,11... | collective-permute-start | bytes 786440 | tf_op jit(solution)/shard_map/ppermute | solution.py:343
  6.8 11.0 %collective-permute-start.7 = (bf16[4,128,256]{2,1,0:T(8,128)(2,1)S(1)}, bf16[4,128,256]{2,1,0:T(8,128)(2,1)S(1)}, u32[]{:S(2)}, u32[]{:S(2)}) collective-permute-start(bf16[4,128,256]{2,1,0:T(8,128)(2,1)S(1)} %get-tuple-element.39), channel_id=1, source_target_pairs={{0,16},{1,17},{2,18},{3,19},{4,20},{5,21},{6,22},{7,23},{8,24},{9,... | collective-permute-start | bytes 786440 | tf_op jit(solution)/shard_map/ppermute | solution.py:343
  7.4 13.0 %collective-permute-start.8 = (bf16[4,128,256]{2,1,0:T(8,128)(2,1)S(1)}, bf16[4,128,256]{2,1,0:T(8,128)(2,1)S(1)}, u32[]{:S(2)}, u32[]{:S(2)}) collective-permute-start(bf16[4,128,256]{2,1,0:T(8,128)(2,1)S(1)} %get-tuple-element.40), channel_id=1, source_target_pairs={{0,17},{1,16},{2,19},{3,18},{4,21},{5,20},{6,23},{7,22},{8,25},{9,... | collective-permute-start | bytes 786440 | tf_op jit(solution)/shard_map/ppermute | solution.py:343
  8.8 0.7 %copy-start.2 = (bf16[128,512]{1,0:T(8,128)(2,1)}, bf16[128,512]{1,0:T(8,128)(2,1)S(1)}, u32[]{:S(2)}) copy-start(bf16[128,512]{1,0:T(8,128)(2,1)S(1)} %collective-permute-done.k_prev) | copy-start | bytes 393220
  8.8 0.7 %copy-start.3 = (bf16[128,512]{1,0:T(8,128)(2,1)}, bf16[128,512]{1,0:T(8,128)(2,1)S(1)}, u32[]{:S(2)}) copy-start(bf16[128,512]{1,0:T(8,128)(2,1)S(1)} %collective-permute-done.1.v_prev) | copy-start | bytes 393220
  15.3 1.6 %collective-permute-start.2 = (bf16[2,256,128]{2,1,0:T(8,128)(2,1)}, bf16[2,256,128]{2,1,0:T(8,128)(2,1)S(1)}, u32[]{:S(2)}, u32[]{:S(2)}) collective-permute-start(bf16[2,256,128]{2,1,0:T(8,128)(2,1)} %get-tuple-element.35), channel_id=1, source_target_pairs={{0,8},{1,9},{2,10},{3,11},{4,12},{5,13},{6,14},{7,15},{8,0},{9,1},... | collective-permute-start | bytes 393224 | tf_op jit(solution)/shard_map/ppermute | solution.py:343
  16.9 0.9 %copy-start.1 = (bf16[2,256,128]{2,1,0:T(8,128)(2,1)S(1)}, bf16[2,256,128]{2,1,0:T(8,128)(2,1)}, u32[]{:S(2)}) copy-start(bf16[2,256,128]{2,1,0:T(8,128)(2,1)} %get-tuple-element.34.mine) | copy-start | bytes 393220
  20.5 3.6 %collective-permute-start.9 = (bf16[4,4,128,256]{3,2,1,0:T(8,128)(2,1)S(1)}, bf16[4,4,128,256]{3,2,1,0:T(8,128)(2,1)S(1)}, u32[]{:S(2)}, u32[]{:S(2)}) collective-permute-start(bf16[4,4,128,256]{3,2,1,0:T(8,128)(2,1)S(1)} %pad_maximum_fusion), channel_id=1, source_target_pairs={{0,8},{1,9},{2,10},{3,11},{4,12},{5,13},{6,14},{7,15},{8,0},{9,1},... | collective-permute-start | bytes 3145736 | tf_op jit(solution)/shard_map/ppermute | solution.py:343
  20.6 5.6 %collective-permute-start.3 = (bf16[384,128]{1,0:T(8,128)(2,1)S(1)}, bf16[384,128]{1,0:T(8,128)(2,1)S(1)}, u32[]{:S(2)}, u32[]{:S(2)}) collective-permute-start(bf16[384,128]{1,0:T(8,128)(2,1)S(1)} %get-tuple-element.36.refs_0_), channel_id=1, source_target_pairs={{0,16},{1,17},{2,18},{3,19},{4,20},{5,21},{6,22},{7,23},{8,24},{9,... | collective-permute-start | bytes 294920 | tf_op jit(solution)/shard_map/ppermute | solution.py:343
  22.1 5.6 %collective-permute-start.4 = (bf16[384,128]{1,0:T(8,128)(2,1)S(1)}, bf16[384,128]{1,0:T(8,128)(2,1)S(1)}, u32[]{:S(2)}, u32[]{:S(2)}) collective-permute-start(bf16[384,128]{1,0:T(8,128)(2,1)S(1)} %get-tuple-element.36.refs_0_), channel_id=1, source_target_pairs={{0,1},{1,0},{2,3},{3,2},{4,5},{5,4},{6,7},{7,6},{8,9},{9,8},{10,11... | collective-permute-start | bytes 294920 | tf_op jit(solution)/shard_map/ppermute | solution.py:343
  22.7 6.7 %collective-permute-start.5 = (bf16[384,128]{1,0:T(8,128)(2,1)S(1)}, bf16[384,128]{1,0:T(8,128)(2,1)S(1)}, u32[]{:S(2)}, u32[]{:S(2)}) collective-permute-start(bf16[384,128]{1,0:T(8,128)(2,1)S(1)} %get-tuple-element.36.refs_0_), channel_id=1, source_target_pairs={{0,17},{1,16},{2,19},{3,18},{4,21},{5,20},{6,23},{7,22},{8,25},{9,... | collective-permute-start | bytes 294920 | tf_op jit(solution)/shard_map/ppermute | solution.py:343
  24.1 9.4 %collective-permute-start.13 = (bf16[384,128]{1,0:T(8,128)(2,1)S(1)}, bf16[384,128]{1,0:T(8,128)(2,1)S(1)}, u32[]{:S(2)}, u32[]{:S(2)}) collective-permute-start(bf16[384,128]{1,0:T(8,128)(2,1)S(1)} %get-tuple-element.51.refs_0_), channel_id=1, source_target_pairs={{0,16},{1,17},{2,18},{3,19},{4,20},{5,21},{6,22},{7,23},{8,24},{9,... | collective-permute-start | bytes 294920 | tf_op jit(solution)/shard_map/ppermute | solution.py:343
  25.6 8.8 %collective-permute-start.14 = (bf16[384,128]{1,0:T(8,128)(2,1)S(1)}, bf16[384,128]{1,0:T(8,128)(2,1)S(1)}, u32[]{:S(2)}, u32[]{:S(2)}) collective-permute-start(bf16[384,128]{1,0:T(8,128)(2,1)S(1)} %get-tuple-element.51.refs_0_), channel_id=1, source_target_pairs={{0,1},{1,0},{2,3},{3,2},{4,5},{5,4},{6,7},{7,6},{8,9},{9,8},{10,11... | collective-permute-start | bytes 294920 | tf_op jit(solution)/shard_map/ppermute | solution.py:343
  26.2 8.1 %collective-permute-start.15 = (bf16[384,128]{1,0:T(8,128)(2,1)S(1)}, bf16[384,128]{1,0:T(8,128)(2,1)S(1)}, u32[]{:S(2)}, u32[]{:S(2)}) collective-permute-start(bf16[384,128]{1,0:T(8,128)(2,1)S(1)} %get-tuple-element.51.refs_0_), channel_id=1, source_target_pairs={{0,17},{1,16},{2,19},{3,18},{4,21},{5,20},{6,23},{7,22},{8,25},{9,... | collective-permute-start | bytes 294920 | tf_op jit(solution)/shard_map/ppermute | solution.py:343
  29.9 8.7 %collective-permute-start.10 = (bf16[128,256]{1,0:T(8,128)(2,1)S(1)}, bf16[128,256]{1,0:T(8,128)(2,1)S(1)}, u32[]{:S(2)}, u32[]{:S(2)}) collective-permute-start(bf16[128,256]{1,0:T(8,128)(2,1)S(1)} %get-tuple-element.48), channel_id=1, source_target_pairs={{0,6},{1,7},{2,4},{3,5},{4,2},{5,3},{6,0},{7,1},{8,14},{9,15},{10,... | collective-permute-start | bytes 196616 | tf_op jit(solution)/shard_map/ppermute | solution.py:343
  33.5 8.1 %collective-permute-start.11 = (bf16[128,256]{1,0:T(8,128)(2,1)S(1)}, bf16[128,256]{1,0:T(8,128)(2,1)S(1)}, u32[]{:S(2)}, u32[]{:S(2)}) collective-permute-start(bf16[128,256]{1,0:T(8,128)(2,1)S(1)} %get-tuple-element.49), channel_id=1, source_target_pairs={{0,4},{1,5},{2,6},{3,7},{4,0},{5,1},{6,2},{7,3},{8,12},{9,13},{10,... | collective-permute-start | bytes 196616 | tf_op jit(solution)/shard_map/ppermute | solution.py:343
  33.5 8.1 %collective-permute-start.12 = (bf16[128,256]{1,0:T(8,128)(2,1)S(1)}, bf16[128,256]{1,0:T(8,128)(2,1)S(1)}, u32[]{:S(2)}, u32[]{:S(2)}) collective-permute-start(bf16[128,256]{1,0:T(8,128)(2,1)S(1)} %get-tuple-element.50), channel_id=1, source_target_pairs={{0,2},{1,3},{2,0},{3,1},{4,6},{5,7},{6,4},{7,5},{8,10},{9,11},{10,... | collective-permute-start | bytes 196616 | tf_op jit(solution)/shard_map/ppermute | solution.py:343
  34.8 8.8 %collective-permute-start.16 = (bf16[128,256]{1,0:T(8,128)(2,1)S(1)}, bf16[128,256]{1,0:T(8,128)(2,1)S(1)}, u32[]{:S(2)}, u32[]{:S(2)}) collective-permute-start(bf16[128,256]{1,0:T(8,128)(2,1)S(1)} %get-tuple-element.53), channel_id=1, source_target_pairs={{0,4},{1,5},{2,6},{3,7},{4,0},{5,1},{6,2},{7,3},{8,12},{9,13},{10,... | collective-permute-start | bytes 196616 | tf_op jit(solution)/shard_map/ppermute | solution.py:343
  37.1 6.6 %collective-permute-start.17 = (bf16[128,256]{1,0:T(8,128)(2,1)S(1)}, bf16[128,256]{1,0:T(8,128)(2,1)S(1)}, u32[]{:S(2)}, u32[]{:S(2)}) collective-permute-start(bf16[128,256]{1,0:T(8,128)(2,1)S(1)} %get-tuple-element.54), channel_id=1, source_target_pairs={{0,6},{1,7},{2,4},{3,5},{4,2},{5,3},{6,0},{7,1},{8,14},{9,15},{10,... | collective-permute-start | bytes 196616 | tf_op jit(solution)/shard_map/ppermute | solution.py:343
  38.6 5.4 %collective-permute-start.18 = (bf16[128,256]{1,0:T(8,128)(2,1)S(1)}, bf16[128,256]{1,0:T(8,128)(2,1)S(1)}, u32[]{:S(2)}, u32[]{:S(2)}) collective-permute-start(bf16[128,256]{1,0:T(8,128)(2,1)S(1)} %get-tuple-element.55), channel_id=1, source_target_pairs={{0,2},{1,3},{2,0},{3,1},{4,6},{5,7},{6,4},{7,5},{8,10},{9,11},{10,... | collective-permute-start | bytes 196616 | tf_op jit(solution)/shard_map/ppermute | solution.py:343
  44.9 3.5 %collective-permute-start.19 = (f32[128,512]{1,0:T(8,128)S(1)}, f32[128,512]{1,0:T(8,128)S(1)}, u32[]{:S(2)}, u32[]{:S(2)}) collective-permute-start(f32[128,512]{1,0:T(8,128)S(1)} %get-tuple-element.60), channel_id=1, source_target_pairs={{0,8},{1,9},{2,10},{3,11},{4,12},{5,13},{6,14},{7,15},{8,0},{9,1},... | collective-permute-start | bytes 786440 | tf_op jit(solution)/shard_map/ppermute | solution.py:343
  44.9 10.5 %all-to-all-start = ((f32[32,1,128]{2,1,0:T(1,128)}), f32[32,1,128]{2,1,0:T(1,128)S(1)}, u32[]{:S(2)}, u32[]{:S(2)}) async-start(f32[32,1,128]{2,1,0:T(1,128)} %shard_map.82), calls=%async_computation | async-start | bytes 32768 | tf_op jit(solution)/shard_map/all_to_all | solution.py:372

commit v8 on v7

--- a/solution.py
+++ b/solution.py
@@ -20,7 +20,7 @@
 BF16 = jnp.bfloat16
 CORES = 2
 ORDER = ((0, 2, 1, 3), (0, 2, 1, 3))
-SUMS = ((2, 1, 0), (1, 2, 0))
+SUMS = ((2, 1, 0), (2, 0, 1))
 HALF = KVH // CORES
 WIDE = HALF * HD
 

time: 56.5 us -> 57.2 us (1.012)
  starting transfers between devices: 26 us -> 27.2 us
    all_to_all x1, starting transfers between devices: 3.44 us -> 4.38 us  [planes(): squares = lax.all_to_all(squares, AXES, 0, 0, tiled=True)]
where the time goes in v8:
time: 57.2 us; the launch traced here: 57 us
  starting transfers between devices  27.2 us (48%)
  waiting for transfers between devices  16.7 us (29%)
  Pallas kernels  9.42 us (16%)
  local copies, waits for them, and re-layouts  2.81 us (5%)
  between operations  0.76 us (1%)
    ppermute x18, starting transfers between devices, swap(): return lax.ppermute(array, AXES, [(i, i ^ mask) for i in range(devices)])  19.7 us
    ppermute x18, waiting for transfers between devices, swap(): return lax.ppermute(array, AXES, [(i, i ^ mask) for i in range(devices)])  10.3 us
    all_to_all x1, waiting for transfers between devices, planes(): squares = lax.all_to_all(squares, AXES, 0, 0, tiled=True)  6.34 us
    pallas_call x1, Pallas kernels, attention(): pl.pallas_call(functools.partial(attention_kernel, turn), in_specs=[pl.Bl...  5.76 us
    all_to_all x1, starting transfers between devices, planes(): squares = lax.all_to_all(squares, AXES, 0, 0, tiled=True)  4.38 us
    unnamed x8, local copies, waits for them, and re-layouts  2.81 us
    ppermute x1, starting transfers between devices, planes(): v_prev = lax.ppermute(v_own, 'seq', following)  2.6 us
  transfers between devices with their start and end apart: 21, of which 7 were waited for; matrix products, arithmetic and copies ran while one was open for 0% of the time, Pallas kernels for 14%

profile of v8, /device:TPU:0, one launch (start us, length us, event | category | flops | bytes accessed | tf_op | source)
XLA Modules:
  0.0 57.0 jit_solution(15747594851185431576)
XLA Ops:
  0.6 0.5 collective-permute-start
  1.1 2.6 %collective-permute-start.1 = (bf16[128,512]{1,0:T(8,128)(2,1)}, bf16[128,512]{1,0:T(8,128)(2,1)S(1)}, u32[]{:S(2)}, u32[]{:S(2)}) collective-permute-start(bf16[128,512]{1,0:T(8,128)(2,1)} %bitcast.18), channel_id=1, source_target_pairs={{0,8},{8,16},{16,24},{24,0},{1,9},{9,17},{17,25},{25,1},{2,10},{10... | collective-permute-start | bytes 393224 | tf_op jit(solution)/shard_map/ppermute | solution.py:349
  3.7 0.0 copy-start
  3.7 1.2 %copy-done = bf16[1,128,4096]{2,1,0:T(8,128)(2,1)S(1)} copy-done((bf16[1,128,4096]{2,1,0:T(8,128)(2,1)S(1)}, bf16[1,128,4096]{2,1,0:T(8,128)(2,1)}, u32[]{:S(2)}) %copy-start) | copy-done | bytes 1048600
  5.0 0.3 shard_map.79
  5.2 1.6 %collective-permute-start.6 = (bf16[4,128,256]{2,1,0:T(8,128)(2,1)S(1)}, bf16[4,128,256]{2,1,0:T(8,128)(2,1)S(1)}, u32[]{:S(2)}, u32[]{:S(2)}) collective-permute-start(bf16[4,128,256]{2,1,0:T(8,128)(2,1)S(1)} %get-tuple-element.38), channel_id=1, source_target_pairs={{0,1},{1,0},{2,3},{3,2},{4,5},{5,4},{6,7},{7,6},{8,9},{9,8},{10,11... | collective-permute-start | bytes 786440 | tf_op jit(solution)/shard_map/ppermute | solution.py:343
  6.8 0.5 collective-permute-start.7
  7.4 1.4 %collective-permute-start.8 = (bf16[4,128,256]{2,1,0:T(8,128)(2,1)S(1)}, bf16[4,128,256]{2,1,0:T(8,128)(2,1)S(1)}, u32[]{:S(2)}, u32[]{:S(2)}) collective-permute-start(bf16[4,128,256]{2,1,0:T(8,128)(2,1)S(1)} %get-tuple-element.40), channel_id=1, source_target_pairs={{0,17},{1,16},{2,19},{3,18},{4,21},{5,20},{6,23},{7,22},{8,25},{9,... | collective-permute-start | bytes 786440 | tf_op jit(solution)/shard_map/ppermute | solution.py:343
  8.8 0.0 collective-permute-done.k_prev
  8.8 0.0 copy-start.2
  8.8 0.0 collective-permute-done.1.v_prev
  8.8 0.0 copy-start.3
  8.8 0.6 %copy-done.2 = bf16[128,512]{1,0:T(8,128)(2,1)} copy-done((bf16[128,512]{1,0:T(8,128)(2,1)}, bf16[128,512]{1,0:T(8,128)(2,1)S(1)}, u32[]{:S(2)}) %copy-start.2) | copy-done | bytes 131096
  9.4 0.0 copy-done.3
  9.5 5.8 %shard_map.77 = (bf16[2,256,128]{2,1,0:T(8,128)(2,1)}, bf16[2,256,128]{2,1,0:T(8,128)(2,1)}) custom-call(s32[1,8]{1,0:T(1,128)} %lengths.1, bf16[128,4096]{1,0:T(8,128)(2,1)} %bitcast.14, bf16[128,4096]{1,0:T(8,128)(2,1)} %bitcast.15, bf16[128,512]{1,0:T(8,128)(2,1)} %copy-done.2, bf16[128,512]{1,0:T(8,128)(2,1)} %bitcast.17, bf16[128,512]{1,0:T(8,128)(2,1)} %copy-done.3, ...), custom_call_target="tpu_custom_call" | custom-call | flops 805306368 | bytes 2097152 | tf_op jit(solution)/shard_map/pallas_call | solution.py:111
  15.3 0.1 collective-permute-start.2
  15.3 1.5 %collective-permute-done.2.theirs = bf16[2,256,128]{2,1,0:T(8,128)(2,1)S(1)} collective-permute-done((bf16[2,256,128]{2,1,0:T(8,128)(2,1)}, bf16[2,256,128]{2,1,0:T(8,128)(2,1)S(1)}, u32[]{:S(2)}, u32[]{:S(2)}) %collective-permute-start.2) | collective-permute-done | bytes 131104 | tf_op jit(solution)/shard_map/ppermute | solution.py:343
  16.9 0.0 copy-start.1
  16.9 0.9 %copy-done.1 = bf16[2,256,128]{2,1,0:T(8,128)(2,1)S(1)} copy-done((bf16[2,256,128]{2,1,0:T(8,128)(2,1)S(1)}, bf16[2,256,128]{2,1,0:T(8,128)(2,1)}, u32[]{:S(2)}) %copy-start.1) | copy-done | bytes 131096
  17.8 0.0 collective-permute-done.6.refs_5_
  17.8 0.0 collective-permute-done.7.refs_6_
  17.8 2.5 %collective-permute-done.8.refs_7_ = bf16[4,128,256]{2,1,0:T(8,128)(2,1)S(1)} collective-permute-done((bf16[4,128,256]{2,1,0:T(8,128)(2,1)S(1)}, bf16[4,128,256]{2,1,0:T(8,128)(2,1)S(1)}, u32[]{:S(2)}, u32[]{:S(2)}) %collective-permute-start.8) | collective-permute-done | bytes 262176 | tf_op jit(solution)/shard_map/ppermute | solution.py:343
  20.4 0.1 pad_maximum_fusion
  20.5 0.1 collective-permute-start.9
  20.6 1.5 %collective-permute-start.3 = (bf16[384,128]{1,0:T(8,128)(2,1)S(1)}, bf16[384,128]{1,0:T(8,128)(2,1)S(1)}, u32[]{:S(2)}, u32[]{:S(2)}) collective-permute-start(bf16[384,128]{1,0:T(8,128)(2,1)S(1)} %get-tuple-element.36.refs_0_), channel_id=1, source_target_pairs={{0,16},{1,17},{2,18},{3,19},{4,20},{5,21},{6,22},{7,23},{8,24},{9,... | collective-permute-start | bytes 294920 | tf_op jit(solution)/shard_map/ppermute | solution.py:343
  22.1 0.6 %collective-permute-start.4 = (bf16[384,128]{1,0:T(8,128)(2,1)S(1)}, bf16[384,128]{1,0:T(8,128)(2,1)S(1)}, u32[]{:S(2)}, u32[]{:S(2)}) collective-permute-start(bf16[384,128]{1,0:T(8,128)(2,1)S(1)} %get-tuple-element.36.refs_0_), channel_id=1, source_target_pairs={{0,1},{1,0},{2,3},{3,2},{4,5},{5,4},{6,7},{7,6},{8,9},{9,8},{10,11... | collective-permute-start | bytes 294920 | tf_op jit(solution)/shard_map/ppermute | solution.py:343
  22.7 1.4 %collective-permute-start.5 = (bf16[384,128]{1,0:T(8,128)(2,1)S(1)}, bf16[384,128]{1,0:T(8,128)(2,1)S(1)}, u32[]{:S(2)}, u32[]{:S(2)}) collective-permute-start(bf16[384,128]{1,0:T(8,128)(2,1)S(1)} %get-tuple-element.36.refs_0_), channel_id=1, source_target_pairs={{0,17},{1,16},{2,19},{3,18},{4,21},{5,20},{6,23},{7,22},{8,25},{9,... | collective-permute-start | bytes 294920 | tf_op jit(solution)/shard_map/ppermute | solution.py:343
  24.1 0.0 collective-permute-done.9.refs_8_
  24.1 1.4 %collective-permute-start.13 = (bf16[384,128]{1,0:T(8,128)(2,1)S(1)}, bf16[384,128]{1,0:T(8,128)(2,1)S(1)}, u32[]{:S(2)}, u32[]{:S(2)}) collective-permute-start(bf16[384,128]{1,0:T(8,128)(2,1)S(1)} %get-tuple-element.51.refs_0_), channel_id=1, source_target_pairs={{0,16},{1,17},{2,18},{3,19},{4,20},{5,21},{6,22},{7,23},{8,24},{9,... | collective-permute-start | bytes 294920 | tf_op jit(solution)/shard_map/ppermute | solution.py:343
  25.6 0.6 %collective-permute-start.14 = (bf16[384,128]{1,0:T(8,128)(2,1)S(1)}, bf16[384,128]{1,0:T(8,128)(2,1)S(1)}, u32[]{:S(2)}, u32[]{:S(2)}) collective-permute-start(bf16[384,128]{1,0:T(8,128)(2,1)S(1)} %get-tuple-element.51.refs_0_), channel_id=1, source_target_pairs={{0,1},{1,0},{2,3},{3,2},{4,5},{5,4},{6,7},{7,6},{8,9},{9,8},{10,11... | collective-permute-start | bytes 294920 | tf_op jit(solution)/shard_map/ppermute | solution.py:343
  26.2 0.0 collective-permute-done.3.refs_1_
  26.2 1.4 %collective-permute-start.15 = (bf16[384,128]{1,0:T(8,128)(2,1)S(1)}, bf16[384,128]{1,0:T(8,128)(2,1)S(1)}, u32[]{:S(2)}, u32[]{:S(2)}) collective-permute-start(bf16[384,128]{1,0:T(8,128)(2,1)S(1)} %get-tuple-element.51.refs_0_), channel_id=1, source_target_pairs={{0,17},{1,16},{2,19},{3,18},{4,21},{5,20},{6,23},{7,22},{8,25},{9,... | collective-permute-start | bytes 294920 | tf_op jit(solution)/shard_map/ppermute | solution.py:343
  27.6 0.0 collective-permute-done.4.refs_2_
  27.6 1.7 %collective-permute-done.5.refs_3_ = bf16[384,128]{1,0:T(8,128)(2,1)S(1)} collective-permute-done((bf16[384,128]{1,0:T(8,128)(2,1)S(1)}, bf16[384,128]{1,0:T(8,128)(2,1)S(1)}, u32[]{:S(2)}, u32[]{:S(2)}) %collective-permute-start.5) | collective-permute-done | bytes 98336 | tf_op jit(solution)/shard_map/ppermute | solution.py:343
  29.4 0.5 shard_map.80
  29.9 3.7 %collective-permute-start.10 = (bf16[128,256]{1,0:T(8,128)(2,1)S(1)}, bf16[128,256]{1,0:T(8,128)(2,1)S(1)}, u32[]{:S(2)}, u32[]{:S(2)}) collective-permute-start(bf16[128,256]{1,0:T(8,128)(2,1)S(1)} %get-tuple-element.48), channel_id=1, source_target_pairs={{0,6},{1,7},{2,4},{3,5},{4,2},{5,3},{6,0},{7,1},{8,14},{9,15},{10,... | collective-permute-start | bytes 196616 | tf_op jit(solution)/shard_map/ppermute | solution.py:343
  33.5 0.0 collective-permute-start.11
  33.5 0.0 collective-permute-done.13.refs_1_
  33.5 0.8 %collective-permute-start.12 = (bf16[128,256]{1,0:T(8,128)(2,1)S(1)}, bf16[128,256]{1,0:T(8,128)(2,1)S(1)}, u32[]{:S(2)}, u32[]{:S(2)}) collective-permute-start(bf16[128,256]{1,0:T(8,128)(2,1)S(1)} %get-tuple-element.50), channel_id=1, source_target_pairs={{0,2},{1,3},{2,0},{3,1},{4,6},{5,7},{6,4},{7,5},{8,10},{9,11},{10,... | collective-permute-start | bytes 196616 | tf_op jit(solution)/shard_map/ppermute | solution.py:343
  34.3 0.0 collective-permute-done.14.refs_2_
  34.3 0.0 collective-permute-done.15.refs_3_
  34.3 0.5 shard_map.81
  34.8 3.7 %collective-permute-start.16 = (bf16[128,256]{1,0:T(8,128)(2,1)S(1)}, bf16[128,256]{1,0:T(8,128)(2,1)S(1)}, u32[]{:S(2)}, u32[]{:S(2)}) collective-permute-start(bf16[128,256]{1,0:T(8,128)(2,1)S(1)} %get-tuple-element.53), channel_id=1, source_target_pairs={{0,6},{1,7},{2,4},{3,5},{4,2},{5,3},{6,0},{7,1},{8,14},{9,15},{10,... | collective-permute-start | bytes 196616 | tf_op jit(solution)/shard_map/ppermute | solution.py:343
  38.5 0.0 collective-permute-start.17
  38.5 0.0 collective-permute-done.10.refs_1_
  38.5 0.8 %collective-permute-start.18 = (bf16[128,256]{1,0:T(8,128)(2,1)S(1)}, bf16[128,256]{1,0:T(8,128)(2,1)S(1)}, u32[]{:S(2)}, u32[]{:S(2)}) collective-permute-start(bf16[128,256]{1,0:T(8,128)(2,1)S(1)} %get-tuple-element.55), channel_id=1, source_target_pairs={{0,4},{1,5},{2,6},{3,7},{4,0},{5,1},{6,2},{7,3},{8,12},{9,13},{10,... | collective-permute-start | bytes 196616 | tf_op jit(solution)/shard_map/ppermute | solution.py:343
  39.3 0.8 %collective-permute-done.11.refs_2_ = bf16[128,256]{1,0:T(8,128)(2,1)S(1)} collective-permute-done((bf16[128,256]{1,0:T(8,128)(2,1)S(1)}, bf16[128,256]{1,0:T(8,128)(2,1)S(1)}, u32[]{:S(2)}, u32[]{:S(2)}) %collective-permute-start.11) | collective-permute-done | bytes 65568 | tf_op jit(solution)/shard_map/ppermute | solution.py:343
  40.1 0.0 collective-permute-done.12.refs_3_
  40.1 1.2 %collective-permute-done.16.refs_5_ = bf16[128,256]{1,0:T(8,128)(2,1)S(1)} collective-permute-done((bf16[128,256]{1,0:T(8,128)(2,1)S(1)}, bf16[128,256]{1,0:T(8,128)(2,1)S(1)}, u32[]{:S(2)}, u32[]{:S(2)}) %collective-permute-start.16) | collective-permute-done | bytes 65568 | tf_op jit(solution)/shard_map/ppermute | solution.py:343
  41.4 2.4 %collective-permute-done.17.refs_6_ = bf16[128,256]{1,0:T(8,128)(2,1)S(1)} collective-permute-done((bf16[128,256]{1,0:T(8,128)(2,1)S(1)}, bf16[128,256]{1,0:T(8,128)(2,1)S(1)}, u32[]{:S(2)}, u32[]{:S(2)}) %collective-permute-start.17) | collective-permute-done | bytes 65568 | tf_op jit(solution)/shard_map/ppermute | solution.py:343
  43.8 0.0 collective-permute-done.18.refs_7_
  43.8 0.7 %shard_map.82 = f32[32,1,128]{2,1,0:T(1,128)} custom-call(f32[128,256]{1,0:T(8,128)S(1)} %get-tuple-element.56.refs_0_, bf16[128,256]{1,0:T(8,128)(2,1)S(1)} %collective-permute-done.10.refs_1_, bf16[128,256]{1,0:T(8,128)(2,1)S(1)} %collective-permute-done.11.refs_2_, bf16[128,256]{1,0:T(8,128)(2,1)S(1)} %collective-permute-done.12.refs_3_, ...), custom_call_target="tpu_custom_call" | custom-call | flops 524288 | bytes 655360 | tf_op jit(solution)/shard_map/pallas_call | solution.py:253
  44.5 0.1 shard_map.83
  44.6 0.1 collective-permute-start.19
  44.7 4.4 %all-to-all-start = ((f32[32,1,128]{2,1,0:T(1,128)}), f32[32,1,128]{2,1,0:T(1,128)S(1)}, u32[]{:S(2)}, u32[]{:S(2)}) async-start(f32[32,1,128]{2,1,0:T(1,128)} %shard_map.82), calls=%async_computation | async-start | bytes 32768 | tf_op jit(solution)/shard_map/all_to_all | solution.py:372
  49.1 0.0 collective-permute-done.19.theirs
  49.1 0.7 %shard_map.84 = (f32[128,512]{1,0:T(8,128)S(1)}, bf16[1,128,512]{2,1,0:T(8,128)(2,1)}) custom-call(f32[128,256]{1,0:T(8,128)S(1)} %get-tuple-element.59.mine, f32[128,512]{1,0:T(8,128)S(1)} %collective-permute-done.19.theirs, bf16[128,128]{1,0:T(8,128)(2,1)S(1)} %get-tuple-element.61.refs_0_, bf16[128,128]{1,0:T(8,128)(2,1)S(1)} %get-tuple-element.62.refs_1_), custom_call_target="tpu_custom_call" | custom-call | bytes 786432 | tf_op jit(solution)/shard_map/pallas_call | solution.py:304
  49.8 6.3 %all-to-all-done.squares = f32[32,1,128]{2,1,0:T(1,128)S(1)} async-done(((f32[32,1,128]{2,1,0:T(1,128)}), f32[32,1,128]{2,1,0:T(1,128)S(1)}, u32[]{:S(2)}, u32[]{:S(2)}) %all-to-all-start) | async-done | bytes 16416 | tf_op jit(solution)/shard_map/all_to_all | solution.py:372
  56.1 0.8 %shard_map.85 = f32[128,512]{1,0:T(8,128)} custom-call(f32[32,1,128]{2,1,0:T(1,128)S(1)} %all-to-all-done.squares, f32[128,512]{1,0:T(8,128)S(1)} %get-tuple-element.65.rows), custom_call_target="tpu_custom_call" | custom-call | flops 65536 | bytes 524288 | tf_op jit(solution)/shard_map/pallas_call | solution.py:326
  (1 shorter events, 0.0 us)
Async XLA Ops:
  0.6 8.2 %collective-permute-start = (bf16[128,512]{1,0:T(8,128)(2,1)}, bf16[128,512]{1,0:T(8,128)(2,1)S(1)}, u32[]{:S(2)}, u32[]{:S(2)}) collective-permute-start(bf16[128,512]{1,0:T(8,128)(2,1)} %bitcast.16), channel_id=1, source_target_pairs={{0,8},{8,16},{16,24},{24,0},{1,9},{9,17},{17,25},{25,1},{2,10},{10... | collective-permute-start | bytes 393224 | tf_op jit(solution)/shard_map/ppermute | solution.py:348
  1.1 7.7 %collective-permute-start.1 = (bf16[128,512]{1,0:T(8,128)(2,1)}, bf16[128,512]{1,0:T(8,128)(2,1)S(1)}, u32[]{:S(2)}, u32[]{:S(2)}) collective-permute-start(bf16[128,512]{1,0:T(8,128)(2,1)} %bitcast.18), channel_id=1, source_target_pairs={{0,8},{8,16},{16,24},{24,0},{1,9},{9,17},{17,25},{25,1},{2,10},{10... | collective-permute-start | bytes 393224 | tf_op jit(solution)/shard_map/ppermute | solution.py:349
  3.7 1.2 %copy-start = (bf16[1,128,4096]{2,1,0:T(8,128)(2,1)S(1)}, bf16[1,128,4096]{2,1,0:T(8,128)(2,1)}, u32[]{:S(2)}) copy-start(bf16[1,128,4096]{2,1,0:T(8,128)(2,1)} %param.10) | copy-start | bytes 3145732
  5.2 12.6 %collective-permute-start.6 = (bf16[4,128,256]{2,1,0:T(8,128)(2,1)S(1)}, bf16[4,128,256]{2,1,0:T(8,128)(2,1)S(1)}, u32[]{:S(2)}, u32[]{:S(2)}) collective-permute-start(bf16[4,128,256]{2,1,0:T(8,128)(2,1)S(1)} %get-tuple-element.38), channel_id=1, source_target_pairs={{0,1},{1,0},{2,3},{3,2},{4,5},{5,4},{6,7},{7,6},{8,9},{9,8},{10,11... | collective-permute-start | bytes 786440 | tf_op jit(solution)/shard_map/ppermute | solution.py:343
  6.8 11.0 %collective-permute-start.7 = (bf16[4,128,256]{2,1,0:T(8,128)(2,1)S(1)}, bf16[4,128,256]{2,1,0:T(8,128)(2,1)S(1)}, u32[]{:S(2)}, u32[]{:S(2)}) collective-permute-start(bf16[4,128,256]{2,1,0:T(8,128)(2,1)S(1)} %get-tuple-element.39), channel_id=1, source_target_pairs={{0,16},{1,17},{2,18},{3,19},{4,20},{5,21},{6,22},{7,23},{8,24},{9,... | collective-permute-start | bytes 786440 | tf_op jit(solution)/shard_map/ppermute | solution.py:343
  7.4 13.0 %collective-permute-start.8 = (bf16[4,128,256]{2,1,0:T(8,128)(2,1)S(1)}, bf16[4,128,256]{2,1,0:T(8,128)(2,1)S(1)}, u32[]{:S(2)}, u32[]{:S(2)}) collective-permute-start(bf16[4,128,256]{2,1,0:T(8,128)(2,1)S(1)} %get-tuple-element.40), channel_id=1, source_target_pairs={{0,17},{1,16},{2,19},{3,18},{4,21},{5,20},{6,23},{7,22},{8,25},{9,... | collective-permute-start | bytes 786440 | tf_op jit(solution)/shard_map/ppermute | solution.py:343
  8.8 0.7 %copy-start.2 = (bf16[128,512]{1,0:T(8,128)(2,1)}, bf16[128,512]{1,0:T(8,128)(2,1)S(1)}, u32[]{:S(2)}) copy-start(bf16[128,512]{1,0:T(8,128)(2,1)S(1)} %collective-permute-done.k_prev) | copy-start | bytes 393220
  8.8 0.7 %copy-start.3 = (bf16[128,512]{1,0:T(8,128)(2,1)}, bf16[128,512]{1,0:T(8,128)(2,1)S(1)}, u32[]{:S(2)}) copy-start(bf16[128,512]{1,0:T(8,128)(2,1)S(1)} %collective-permute-done.1.v_prev) | copy-start | bytes 393220
  15.3 1.6 %collective-permute-start.2 = (bf16[2,256,128]{2,1,0:T(8,128)(2,1)}, bf16[2,256,128]{2,1,0:T(8,128)(2,1)S(1)}, u32[]{:S(2)}, u32[]{:S(2)}) collective-permute-start(bf16[2,256,128]{2,1,0:T(8,128)(2,1)} %get-tuple-element.35), channel_id=1, source_target_pairs={{0,8},{1,9},{2,10},{3,11},{4,12},{5,13},{6,14},{7,15},{8,0},{9,1},... | collective-permute-start | bytes 393224 | tf_op jit(solution)/shard_map/ppermute | solution.py:343
  16.9 0.9 %copy-start.1 = (bf16[2,256,128]{2,1,0:T(8,128)(2,1)S(1)}, bf16[2,256,128]{2,1,0:T(8,128)(2,1)}, u32[]{:S(2)}) copy-start(bf16[2,256,128]{2,1,0:T(8,128)(2,1)} %get-tuple-element.34.mine) | copy-start | bytes 393220
  20.5 3.6 %collective-permute-start.9 = (bf16[4,4,128,256]{3,2,1,0:T(8,128)(2,1)S(1)}, bf16[4,4,128,256]{3,2,1,0:T(8,128)(2,1)S(1)}, u32[]{:S(2)}, u32[]{:S(2)}) collective-permute-start(bf16[4,4,128,256]{3,2,1,0:T(8,128)(2,1)S(1)} %pad_maximum_fusion), channel_id=1, source_target_pairs={{0,8},{1,9},{2,10},{3,11},{4,12},{5,13},{6,14},{7,15},{8,0},{9,1},... | collective-permute-start | bytes 3145736 | tf_op jit(solution)/shard_map/ppermute | solution.py:343
  20.6 5.6 %collective-permute-start.3 = (bf16[384,128]{1,0:T(8,128)(2,1)S(1)}, bf16[384,128]{1,0:T(8,128)(2,1)S(1)}, u32[]{:S(2)}, u32[]{:S(2)}) collective-permute-start(bf16[384,128]{1,0:T(8,128)(2,1)S(1)} %get-tuple-element.36.refs_0_), channel_id=1, source_target_pairs={{0,16},{1,17},{2,18},{3,19},{4,20},{5,21},{6,22},{7,23},{8,24},{9,... | collective-permute-start | bytes 294920 | tf_op jit(solution)/shard_map/ppermute | solution.py:343
  22.1 5.6 %collective-permute-start.4 = (bf16[384,128]{1,0:T(8,128)(2,1)S(1)}, bf16[384,128]{1,0:T(8,128)(2,1)S(1)}, u32[]{:S(2)}, u32[]{:S(2)}) collective-permute-start(bf16[384,128]{1,0:T(8,128)(2,1)S(1)} %get-tuple-element.36.refs_0_), channel_id=1, source_target_pairs={{0,1},{1,0},{2,3},{3,2},{4,5},{5,4},{6,7},{7,6},{8,9},{9,8},{10,11... | collective-permute-start | bytes 294920 | tf_op jit(solution)/shard_map/ppermute | solution.py:343
  22.7 6.7 %collective-permute-start.5 = (bf16[384,128]{1,0:T(8,128)(2,1)S(1)}, bf16[384,128]{1,0:T(8,128)(2,1)S(1)}, u32[]{:S(2)}, u32[]{:S(2)}) collective-permute-start(bf16[384,128]{1,0:T(8,128)(2,1)S(1)} %get-tuple-element.36.refs_0_), channel_id=1, source_target_pairs={{0,17},{1,16},{2,19},{3,18},{4,21},{5,20},{6,23},{7,22},{8,25},{9,... | collective-permute-start | bytes 294920 | tf_op jit(solution)/shard_map/ppermute | solution.py:343
  24.1 9.4 %collective-permute-start.13 = (bf16[384,128]{1,0:T(8,128)(2,1)S(1)}, bf16[384,128]{1,0:T(8,128)(2,1)S(1)}, u32[]{:S(2)}, u32[]{:S(2)}) collective-permute-start(bf16[384,128]{1,0:T(8,128)(2,1)S(1)} %get-tuple-element.51.refs_0_), channel_id=1, source_target_pairs={{0,16},{1,17},{2,18},{3,19},{4,20},{5,21},{6,22},{7,23},{8,24},{9,... | collective-permute-start | bytes 294920 | tf_op jit(solution)/shard_map/ppermute | solution.py:343
  25.6 8.8 %collective-permute-start.14 = (bf16[384,128]{1,0:T(8,128)(2,1)S(1)}, bf16[384,128]{1,0:T(8,128)(2,1)S(1)}, u32[]{:S(2)}, u32[]{:S(2)}) collective-permute-start(bf16[384,128]{1,0:T(8,128)(2,1)S(1)} %get-tuple-element.51.refs_0_), channel_id=1, source_target_pairs={{0,1},{1,0},{2,3},{3,2},{4,5},{5,4},{6,7},{7,6},{8,9},{9,8},{10,11... | collective-permute-start | bytes 294920 | tf_op jit(solution)/shard_map/ppermute | solution.py:343
  26.2 8.1 %collective-permute-start.15 = (bf16[384,128]{1,0:T(8,128)(2,1)S(1)}, bf16[384,128]{1,0:T(8,128)(2,1)S(1)}, u32[]{:S(2)}, u32[]{:S(2)}) collective-permute-start(bf16[384,128]{1,0:T(8,128)(2,1)S(1)} %get-tuple-element.51.refs_0_), channel_id=1, source_target_pairs={{0,17},{1,16},{2,19},{3,18},{4,21},{5,20},{6,23},{7,22},{8,25},{9,... | collective-permute-start | bytes 294920 | tf_op jit(solution)/shard_map/ppermute | solution.py:343
  29.9 8.6 %collective-permute-start.10 = (bf16[128,256]{1,0:T(8,128)(2,1)S(1)}, bf16[128,256]{1,0:T(8,128)(2,1)S(1)}, u32[]{:S(2)}, u32[]{:S(2)}) collective-permute-start(bf16[128,256]{1,0:T(8,128)(2,1)S(1)} %get-tuple-element.48), channel_id=1, source_target_pairs={{0,6},{1,7},{2,4},{3,5},{4,2},{5,3},{6,0},{7,1},{8,14},{9,15},{10,... | collective-permute-start | bytes 196616 | tf_op jit(solution)/shard_map/ppermute | solution.py:343
  33.5 6.6 %collective-permute-start.11 = (bf16[128,256]{1,0:T(8,128)(2,1)S(1)}, bf16[128,256]{1,0:T(8,128)(2,1)S(1)}, u32[]{:S(2)}, u32[]{:S(2)}) collective-permute-start(bf16[128,256]{1,0:T(8,128)(2,1)S(1)} %get-tuple-element.49), channel_id=1, source_target_pairs={{0,4},{1,5},{2,6},{3,7},{4,0},{5,1},{6,2},{7,3},{8,12},{9,13},{10,... | collective-permute-start | bytes 196616 | tf_op jit(solution)/shard_map/ppermute | solution.py:343
  33.5 6.6 %collective-permute-start.12 = (bf16[128,256]{1,0:T(8,128)(2,1)S(1)}, bf16[128,256]{1,0:T(8,128)(2,1)S(1)}, u32[]{:S(2)}, u32[]{:S(2)}) collective-permute-start(bf16[128,256]{1,0:T(8,128)(2,1)S(1)} %get-tuple-element.50), channel_id=1, source_target_pairs={{0,2},{1,3},{2,0},{3,1},{4,6},{5,7},{6,4},{7,5},{8,10},{9,11},{10,... | collective-permute-start | bytes 196616 | tf_op jit(solution)/shard_map/ppermute | solution.py:343
  34.8 6.5 %collective-permute-start.16 = (bf16[128,256]{1,0:T(8,128)(2,1)S(1)}, bf16[128,256]{1,0:T(8,128)(2,1)S(1)}, u32[]{:S(2)}, u32[]{:S(2)}) collective-permute-start(bf16[128,256]{1,0:T(8,128)(2,1)S(1)} %get-tuple-element.53), channel_id=1, source_target_pairs={{0,6},{1,7},{2,4},{3,5},{4,2},{5,3},{6,0},{7,1},{8,14},{9,15},{10,... | collective-permute-start | bytes 196616 | tf_op jit(solution)/shard_map/ppermute | solution.py:343
  38.5 5.3 %collective-permute-start.17 = (bf16[128,256]{1,0:T(8,128)(2,1)S(1)}, bf16[128,256]{1,0:T(8,128)(2,1)S(1)}, u32[]{:S(2)}, u32[]{:S(2)}) collective-permute-start(bf16[128,256]{1,0:T(8,128)(2,1)S(1)} %get-tuple-element.54), channel_id=1, source_target_pairs={{0,2},{1,3},{2,0},{3,1},{4,6},{5,7},{6,4},{7,5},{8,10},{9,11},{10,... | collective-permute-start | bytes 196616 | tf_op jit(solution)/shard_map/ppermute | solution.py:343
  38.5 5.3 %collective-permute-start.18 = (bf16[128,256]{1,0:T(8,128)(2,1)S(1)}, bf16[128,256]{1,0:T(8,128)(2,1)S(1)}, u32[]{:S(2)}, u32[]{:S(2)}) collective-permute-start(bf16[128,256]{1,0:T(8,128)(2,1)S(1)} %get-tuple-element.55), channel_id=1, source_target_pairs={{0,4},{1,5},{2,6},{3,7},{4,0},{5,1},{6,2},{7,3},{8,12},{9,13},{10,... | collective-permute-start | bytes 196616 | tf_op jit(solution)/shard_map/ppermute | solution.py:343
  44.6 4.5 %collective-permute-start.19 = (f32[128,512]{1,0:T(8,128)S(1)}, f32[128,512]{1,0:T(8,128)S(1)}, u32[]{:S(2)}, u32[]{:S(2)}) collective-permute-start(f32[128,512]{1,0:T(8,128)S(1)} %get-tuple-element.60), channel_id=1, source_target_pairs={{0,8},{1,9},{2,10},{3,11},{4,12},{5,13},{6,14},{7,15},{8,0},{9,1},... | collective-permute-start | bytes 786440 | tf_op jit(solution)/shard_map/ppermute | solution.py:343
  44.7 11.4 %all-to-all-start = ((f32[32,1,128]{2,1,0:T(1,128)}), f32[32,1,128]{2,1,0:T(1,128)S(1)}, u32[]{:S(2)}, u32[]{:S(2)}) async-start(f32[32,1,128]{2,1,0:T(1,128)} %shard_map.82), calls=%async_computation | async-start | bytes 32768 | tf_op jit(solution)/shard_map/all_to_all | solution.py:372
